TPU v7x, 32 devices: a whole 2x2x4 slice. The times are simulated.
32 devices in a mesh: grp: 8 (over y, x, core), in: 4 (over z).
Axes of the slice: x: 2, y: 2, z: 4, core: 2. Of those that a mesh axis runs over, the one named last changes fastest.
Arguments:
- tokens: bfloat16 [4096, 1024], P(('grp', 'in')), may hold values from -6 to 6
- segments: int32 [32, 128], P(('grp', 'in')), may hold values from 0 to 2, never falling along the last dimension, each value on 1 to 64 neighbouring positions
- cotangent: bfloat16 [4096, 1024], P(('grp', 'in')), may hold values from -6 to 6
- vectors: float32 [12288], P('in'), may hold values from -0.5 to 1.5
- vector_moment: float32 [12288], P('in'), may hold values from -4 to 4
- qkv_weight: float32 [1024, 3072], P('in', 'grp'), may hold values from -0.1875 to 0.1875
- qkv_moment: float32 [1024, 3072], P('in', 'grp'), may hold values from -3 to 3
- qkv_left: float32 [1024, 1024], P('in', 'grp'), may hold values from -0.1 to 0.8, as said below
- qkv_right: float32 [3072, 3072], P('grp', 'in'), may hold values from -0.1 to 0.8, as said below
- qkv_left_root: float32 [1024, 1024], P('in', 'grp'), may hold values from -1 to 3
- qkv_right_root: float32 [3072, 3072], P('grp', 'in'), may hold values from -1 to 3
- out_weight: float32 [1024, 1024], P('in', 'grp'), may hold values from -0.5 to 0.5
- out_moment: float32 [1024, 1024], P('in', 'grp'), may hold values from -3 to 3
- out_left: float32 [1024, 1024], P('in', 'grp'), may hold values from -0.1 to 0.8, as said below
- out_right: float32 [1024, 1024], P('grp', 'in'), may hold values from -0.1 to 0.8, as said below
- out_left_root: float32 [1024, 1024], P('in', 'grp'), may hold values from -1 to 3
- out_right_root: float32 [1024, 1024], P('grp', 'in'), may hold values from -1 to 3
- fc_weight: float32 [1024, 4096], P('in', 'grp'), may hold values from -0.1875 to 0.1875
- fc_moment: float32 [1024, 4096], P('in', 'grp'), may hold values from -3 to 3
- fc_left: float32 [1024, 1024], P('in', 'grp'), may hold values from -0.1 to 0.8, as said below
- fc_right: float32 [4096, 4096], P('grp', 'in'), may hold values from -0.1 to 0.8, as said below
- fc_left_root: float32 [1024, 1024], P('in', 'grp'), may hold values from -1 to 3
- fc_right_root: float32 [4096, 4096], P('grp', 'in'), may hold values from -1 to 3
- proj_weight: float32 [4096, 1024], P('in', 'grp'), may hold values from -0.09375 to 0.09375
- proj_moment: float32 [4096, 1024], P('in', 'grp'), may hold values from -3 to 3
- proj_left: float32 [4096, 4096], P('in', 'grp'), may hold values from -0.1 to 0.8, as said below
- proj_right: float32 [1024, 1024], P('grp', 'in'), may hold values from -0.1 to 0.8, as said below
- proj_left_root: float32 [4096, 4096], P('in', 'grp'), may hold values from -1 to 3
- proj_right_root: float32 [1024, 1024], P('grp', 'in'), may hold values from -1 to 3
Outputs:
- output: bfloat16 [4096, 1024], P(('grp', 'in'))
- input_grad: bfloat16 [4096, 1024], P(('grp', 'in'))
- qkv_grad: float32 [1024, 3072], P('in', 'grp')
- qkv_left_new: float32 [1024, 1024], P('in', 'grp')
- qkv_right_new: float32 [3072, 3072], P('grp', 'in')
- qkv_moment_new: float32 [1024, 3072], P('in', 'grp')
- qkv_weight_new: float32 [1024, 3072], P('in', 'grp')
- qkv_copy: bfloat16 [1024, 3072], P('in', 'grp')
- out_grad: float32 [1024, 1024], P('in', 'grp')
- out_left_new: float32 [1024, 1024], P('in', 'grp')
- out_right_new: float32 [1024, 1024], P('grp', 'in')
- out_moment_new: float32 [1024, 1024], P('in', 'grp')
- out_weight_new: float32 [1024, 1024], P('in', 'grp')
- out_copy: bfloat16 [1024, 1024], P('in', 'grp')
- fc_grad: float32 [1024, 4096], P('in', 'grp')
- fc_left_new: float32 [1024, 1024], P('in', 'grp')
- fc_right_new: float32 [4096, 4096], P('grp', 'in')
- fc_moment_new: float32 [1024, 4096], P('in', 'grp')
- fc_weight_new: float32 [1024, 4096], P('in', 'grp')
- fc_copy: bfloat16 [1024, 4096], P('in', 'grp')
- proj_grad: float32 [4096, 1024], P('in', 'grp')
- proj_left_new: float32 [4096, 4096], P('in', 'grp')
- proj_right_new: float32 [1024, 1024], P('grp', 'in')
- proj_moment_new: float32 [4096, 1024], P('in', 'grp')
- proj_weight_new: float32 [4096, 1024], P('in', 'grp')
- proj_copy: bfloat16 [4096, 1024], P('in', 'grp')
- vector_grad: float32 [12288], P('in')
- vector_moment_new: float32 [12288], P('in')
- vectors_new: float32 [12288], P('in')
Inputs may be any that keep to these rules, and one draw needn't show every extreme that they name: `segments`: segment numbers never fall along a sequence. `qkv_left`: Symmetric. `qkv_right`: Symmetric. `out_left`: Symmetric. `out_right`: Symmetric. `fc_left`: Symmetric. `fc_right`: Symmetric. `proj_left`: Symmetric. `proj_right`: Symmetric.
All inputs are finite; a program needn't handle non-finite values.
Results may differ from a plain program's by a relative error of at most 0.011.
The roundings to bfloat16 on the way count: a program that leaves them out, or rounds other values in their place, can miss the bound.
Values may be sent and summed in bfloat16 or wider, within the bound.
No kernel may reach another device: no remote copies, remote signals or barrier semaphores. Data moves between devices by JAX's collectives and lax.ppermute only.
A program may use at most 256 MiB of HBM per device.

v0:
```python
import math

import jax
import jax.numpy as jnp
from jax import lax
from jax.sharding import PartitionSpec as P

HEADS = 16
HEAD_DIM = 64


EPSILON = 1e-05
DECAY = 0.5
MOMENTUM = 0.5
RATE = 0.03
PRECISE = lax.Precision.HIGHEST
MASKED = -1e30


def norm_forward(values, gain, offset):
    centred = values - jnp.mean(values, axis=-1, keepdims=True)
    scaled = centred * lax.rsqrt(jnp.mean(centred * centred, axis=-1, keepdims=True) + EPSILON)
    return scaled * gain + offset


def gelu_tanh(values):
    return jax.nn.gelu(values, approximate=True)


def precise(left, right):
    return jnp.dot(left, right, precision=PRECISE, preferred_element_type=jnp.float32)


def half_dot(left, right):
    return jnp.dot(left, right, preferred_element_type=jnp.float32)


def score_block(queries, key_rows, allowed, score_scale):
    scores = (
        jnp.einsum("qhd,khd->hqk", queries, key_rows, preferred_element_type=jnp.float32)
        * score_scale
    )
    return jnp.where(allowed[None], scores, MASKED)


def on_device(
    tokens,
    segments,
    cotangent,
    vectors,
    vector_moment,
    qkv_weight,
    qkv_moment,
    qkv_left,
    qkv_right,
    qkv_left_root,
    qkv_right_root,
    out_weight,
    out_moment,
    out_left,
    out_right,
    out_left_root,
    out_right_root,
    fc_weight,
    fc_moment,
    fc_left,
    fc_right,
    fc_left_root,
    fc_right_root,
    proj_weight,
    proj_moment,
    proj_left,
    proj_right,
    proj_left_root,
    proj_right_root,
):
    copies = [
        master.astype(jnp.bfloat16) for master in (qkv_weight, out_weight, fc_weight, proj_weight)
    ]
    vector_copy = vectors.astype(jnp.bfloat16)
    qkv_rows, out_rows, fc_rows, proj_rows, vector_whole = (
        lax.all_gather(copies[0], "in", axis=0, tiled=True),
        lax.all_gather(copies[1], "in", axis=0, tiled=True),
        lax.all_gather(copies[2], "in", axis=0, tiled=True),
        lax.all_gather(copies[3], "in", axis=0, tiled=True),
        lax.all_gather(vector_copy, "in", axis=0, tiled=True),
    )
    qkv_full, out_full, fc_full, proj_full = (
        lax.all_gather(qkv_rows, "grp", axis=1, tiled=True),
        lax.all_gather(out_rows, "grp", axis=1, tiled=True),
        lax.all_gather(fc_rows, "grp", axis=1, tiled=True),
        lax.all_gather(proj_rows, "grp", axis=1, tiled=True),
    )
    model_width = tokens.shape[1]
    hidden_width = fc_full.shape[1]
    seq_length = tokens.shape[0]
    params = vector_whole.astype(jnp.float32)
    gain_one = params[0:model_width]
    shift_one = params[model_width : 2 * model_width]
    bias_query = params[2 * model_width : 3 * model_width]
    bias_value = params[3 * model_width : 4 * model_width]
    bias_out = params[4 * model_width : 5 * model_width]
    gain_two = params[5 * model_width : 6 * model_width]
    shift_two = params[6 * model_width : 7 * model_width]
    bias_fc = params[7 * model_width : 7 * model_width + hidden_width]
    bias_proj = params[7 * model_width + hidden_width :]
    inputs = tokens.astype(jnp.float32)
    normed_one = norm_forward(inputs, gain_one, shift_one).astype(jnp.bfloat16)
    qkv_bias = jnp.concatenate([bias_query, jnp.zeros_like(bias_query), bias_value])
    projected = (half_dot(normed_one, qkv_full) + qkv_bias).astype(jnp.bfloat16)
    head_parts = projected.reshape(seq_length, 3, HEADS, HEAD_DIM)
    queries = head_parts[:, 0]
    key_rows = head_parts[:, 1]
    value_rows = head_parts[:, 2]
    score_scale = HEAD_DIM ** (-0.5)
    labels = segments[0]
    position = jnp.arange(seq_length)
    allowed = (labels[:, None] == labels[None, :]) & (position[:, None] >= position[None, :])
    scores = score_block(queries, key_rows, allowed, score_scale)
    maximum = jnp.max(scores, axis=-1, keepdims=True)
    shifted = jnp.exp(scores - maximum)
    totals = jnp.sum(shifted, axis=-1, keepdims=True)
    log_totals = maximum + jnp.log(totals)
    probs_low = (shifted / totals).astype(jnp.bfloat16)
    attended = jnp.einsum("hqk,khd->qhd", probs_low, value_rows, preferred_element_type=jnp.float32)
    attended = attended.reshape(seq_length, model_width).astype(jnp.bfloat16)
    middle = inputs + (half_dot(attended, out_full) + bias_out)
    normed_two = norm_forward(middle, gain_two, shift_two).astype(jnp.bfloat16)
    pre_act = half_dot(normed_two, fc_full) + bias_fc
    activated, gelu_back = jax.vjp(gelu_tanh, pre_act)
    activated = activated.astype(jnp.bfloat16)
    output = (middle + (half_dot(activated, proj_full) + bias_proj)).astype(jnp.bfloat16)
    grad_top = cotangent.astype(jnp.float32)
    grad_proj_bias = jnp.sum(grad_top, axis=0)
    grad_act = half_dot(cotangent, proj_full.T)
    grad_pre = gelu_back(grad_act)[0].astype(jnp.bfloat16)
    grad_fc_bias = jnp.sum(grad_pre.astype(jnp.float32), axis=0)
    grad_normed_two = half_dot(grad_pre, fc_full.T)
    unused_two, norm_back_two = jax.vjp(norm_forward, middle, gain_two, shift_two)
    grad_mid_part, grad_gain_two, grad_shift_two = norm_back_two(grad_normed_two)
    grad_middle = grad_top + grad_mid_part
    grad_branch = grad_middle.astype(jnp.bfloat16)
    grad_out_bias = jnp.sum(grad_branch.astype(jnp.float32), axis=0)
    grad_attended = half_dot(grad_branch, out_full.T).astype(jnp.bfloat16)
    grad_attended = grad_attended.reshape(seq_length, HEADS, HEAD_DIM)
    again = score_block(queries, key_rows, allowed, score_scale)
    probs = jnp.exp(again - log_totals)
    grad_probs = jnp.einsum(
        "qhd,khd->hqk", grad_attended, value_rows, preferred_element_type=jnp.float32
    )
    grad_values = jnp.einsum(
        "hqk,qhd->khd", probs_low, grad_attended, preferred_element_type=jnp.float32
    )
    row_dot = jnp.sum(probs * grad_probs, axis=-1, keepdims=True)
    grad_scores = (probs * (grad_probs - row_dot)).astype(jnp.bfloat16)
    grad_queries = (
        jnp.einsum("hqk,khd->qhd", grad_scores, key_rows, preferred_element_type=jnp.float32)
        * score_scale
    )
    grad_keys = (
        jnp.einsum("hqk,qhd->khd", grad_scores, queries, preferred_element_type=jnp.float32)
        * score_scale
    )
    grad_heads = jnp.stack([grad_queries, grad_keys, grad_values], axis=1).astype(jnp.bfloat16)
    grad_heads = grad_heads.reshape(seq_length, 3 * model_width)
    head_sums = jnp.sum(grad_heads.astype(jnp.float32), axis=0)
    grad_query_bias = head_sums[0:model_width]
    grad_value_bias = head_sums[2 * model_width : 3 * model_width]
    grad_normed_one = half_dot(grad_heads, qkv_full.T)
    unused_one, norm_back_one = jax.vjp(norm_forward, inputs, gain_one, shift_one)
    grad_in_part, grad_gain_one, grad_shift_one = norm_back_one(grad_normed_one)
    input_grad = (grad_middle + grad_in_part).astype(jnp.bfloat16)
    vector_terms = jnp.concatenate(
        [
            grad_gain_one,
            grad_shift_one,
            grad_query_bias,
            grad_value_bias,
            grad_out_bias,
            grad_gain_two,
            grad_shift_two,
            grad_fc_bias,
            grad_proj_bias,
        ]
    )
    grad_qkv = half_dot(normed_one.T, grad_heads)
    grad_out_weight = half_dot(attended.T, grad_branch)
    grad_fc = half_dot(normed_two.T, grad_pre)
    grad_proj = half_dot(activated.T, cotangent)
    qkv_part, out_part, fc_part, proj_part, vector_part = (
        lax.psum_scatter(grad_qkv, "in", scatter_dimension=0, tiled=True),
        lax.psum_scatter(grad_out_weight, "in", scatter_dimension=0, tiled=True),
        lax.psum_scatter(grad_fc, "in", scatter_dimension=0, tiled=True),
        lax.psum_scatter(grad_proj, "in", scatter_dimension=0, tiled=True),
        lax.psum_scatter(vector_terms, "in", scatter_dimension=0, tiled=True),
    )
    qkv_sum, out_sum, fc_sum, proj_sum, vector_sum = lax.psum(
        (qkv_part, out_part, fc_part, proj_part, vector_part), "grp"
    )
    token_total = seq_length * lax.axis_size("grp") * lax.axis_size("in")
    factor = 1.0 / math.sqrt(token_total)
    row_grads = [qkv_sum * factor, out_sum * factor, fc_sum * factor, proj_sum * factor]
    vector_grad = vector_sum * factor
    group_index = lax.axis_index("grp")
    group_count = lax.axis_size("grp")
    owned_blocks = []
    for gradient in row_grads:
        block_cols = gradient.shape[1] // group_count
        owned_blocks.append(
            lax.dynamic_slice_in_dim(gradient, group_index * block_cols, block_cols, 1)
        )
    gathered = (
        lax.all_gather(owned_blocks[0], "in", axis=0, tiled=True),
        lax.all_gather(owned_blocks[1], "in", axis=0, tiled=True),
        lax.all_gather(owned_blocks[2], "in", axis=0, tiled=True),
        lax.all_gather(owned_blocks[3], "in", axis=0, tiled=True),
    )
    right_roots = [qkv_right_root, out_right_root, fc_right_root, proj_right_root]
    left_roots = [qkv_left_root, out_left_root, fc_left_root, proj_left_root]
    left_terms = [precise(owned_blocks[number], gathered[number].T) for number in range(4)]
    image_terms = [precise(gathered[number], right_roots[number]) for number in range(4)]
    right_terms = [precise(owned_blocks[number].T, row_grads[number]) for number in range(4)]
    group_parts = (
        lax.psum_scatter(left_terms[0], "grp", scatter_dimension=1, tiled=True),
        lax.psum_scatter(left_terms[1], "grp", scatter_dimension=1, tiled=True),
        lax.psum_scatter(left_terms[2], "grp", scatter_dimension=1, tiled=True),
        lax.psum_scatter(left_terms[3], "grp", scatter_dimension=1, tiled=True),
        lax.psum_scatter(image_terms[0], "grp", scatter_dimension=0, tiled=True),
        lax.psum_scatter(image_terms[1], "grp", scatter_dimension=0, tiled=True),
        lax.psum_scatter(image_terms[2], "grp", scatter_dimension=0, tiled=True),
        lax.psum_scatter(image_terms[3], "grp", scatter_dimension=0, tiled=True),
    )
    right_sums = (
        lax.psum_scatter(right_terms[0], "in", scatter_dimension=1, tiled=True),
        lax.psum_scatter(right_terms[1], "in", scatter_dimension=1, tiled=True),
        lax.psum_scatter(right_terms[2], "in", scatter_dimension=1, tiled=True),
        lax.psum_scatter(right_terms[3], "in", scatter_dimension=1, tiled=True),
    )
    image_full = (
        lax.all_gather(group_parts[4], "in", axis=1, tiled=True),
        lax.all_gather(group_parts[5], "in", axis=1, tiled=True),
        lax.all_gather(group_parts[6], "in", axis=1, tiled=True),
        lax.all_gather(group_parts[7], "in", axis=1, tiled=True),
    )
    precond_terms = [precise(left_roots[number], image_full[number]) for number in range(4)]
    directions = (
        lax.psum_scatter(precond_terms[0], "grp", scatter_dimension=1, tiled=True),
        lax.psum_scatter(precond_terms[1], "grp", scatter_dimension=1, tiled=True),
        lax.psum_scatter(precond_terms[2], "grp", scatter_dimension=1, tiled=True),
        lax.psum_scatter(precond_terms[3], "grp", scatter_dimension=1, tiled=True),
    )
    masters = [qkv_weight, out_weight, fc_weight, proj_weight]
    moments = [qkv_moment, out_moment, fc_moment, proj_moment]
    lefts = [qkv_left, out_left, fc_left, proj_left]
    rights = [qkv_right, out_right, fc_right, proj_right]
    updated = []
    for number in range(4):
        row_total = gathered[number].shape[0]
        col_total = row_grads[number].shape[1]
        new_left = DECAY * lefts[number] + (1.0 - DECAY) / col_total * group_parts[number]
        new_right = DECAY * rights[number] + (1.0 - DECAY) / row_total * right_sums[number]
        new_moment = MOMENTUM * moments[number] + directions[number]
        new_weight = masters[number] - RATE * new_moment
        updated.append(
            (
                owned_blocks[number],
                new_left,
                new_right,
                new_moment,
                new_weight,
                new_weight.astype(jnp.bfloat16),
            )
        )
    new_vector_moment = MOMENTUM * vector_moment + vector_grad
    new_vectors = vectors - RATE * new_vector_moment
    return (
        output,
        input_grad,
        updated[0][0],
        updated[0][1],
        updated[0][2],
        updated[0][3],
        updated[0][4],
        updated[0][5],
        updated[1][0],
        updated[1][1],
        updated[1][2],
        updated[1][3],
        updated[1][4],
        updated[1][5],
        updated[2][0],
        updated[2][1],
        updated[2][2],
        updated[2][3],
        updated[2][4],
        updated[2][5],
        updated[3][0],
        updated[3][1],
        updated[3][2],
        updated[3][3],
        updated[3][4],
        updated[3][5],
        vector_grad,
        new_vector_moment,
        new_vectors,
    )


def solution(mesh):
    placed = (
        P(("grp", "in"), None),
        P(("grp", "in"), None),
        P(("grp", "in"), None),
        P("in"),
        P("in"),
        P("in", "grp"),
        P("in", "grp"),
        P("in", "grp"),
        P("grp", "in"),
        P("in", "grp"),
        P("grp", "in"),
        P("in", "grp"),
        P("in", "grp"),
        P("in", "grp"),
        P("grp", "in"),
        P("in", "grp"),
        P("grp", "in"),
        P("in", "grp"),
        P("in", "grp"),
        P("in", "grp"),
        P("grp", "in"),
        P("in", "grp"),
        P("grp", "in"),
        P("in", "grp"),
        P("in", "grp"),
        P("in", "grp"),
        P("grp", "in"),
        P("in", "grp"),
        P("grp", "in"),
    )
    return jax.shard_map(
        on_device,
        mesh=mesh,
        in_specs=placed,
        out_specs=(
            P(("grp", "in"), None),
            P(("grp", "in"), None),
            P("in", "grp"),
            P("in", "grp"),
            P("grp", "in"),
            P("in", "grp"),
            P("in", "grp"),
            P("in", "grp"),
            P("in", "grp"),
            P("in", "grp"),
            P("grp", "in"),
            P("in", "grp"),
            P("in", "grp"),
            P("in", "grp"),
            P("in", "grp"),
            P("in", "grp"),
            P("grp", "in"),
            P("in", "grp"),
            P("in", "grp"),
            P("in", "grp"),
            P("in", "grp"),
            P("in", "grp"),
            P("grp", "in"),
            P("in", "grp"),
            P("in", "grp"),
            P("in", "grp"),
            P("in"),
            P("in"),
            P("in"),
        ),
        check_vma=False,
    )
```

profile of v0, /device:TPU:0, one launch (start us, length us, event | category | flops | bytes accessed | tf_op | source)
XLA Modules:
  0.0 2523.5 jit_solution(16134800298910434066)
XLA Ops:
  95.0 33.8 %all-gather.13.cloned.1.call-done = bf16[1024,3072]{1,0:T(8,128)(2,1)} async-done(((bf16[1024,384]{1,0:T(8,128)(2,1)}), bf16[1024,3072]{1,0:T(8,128)(2,1)}) %all-gather.13.cloned.1.call-update) | async-done | bytes 6291472 | tf_op jit(solution)/shard_map/all_gather | solution.py:89
  161.9 54.5 %all-gather.23.cloned.1.call-done = bf16[4096,1024]{1,0:T(8,128)(2,1)} async-done(((bf16[4096,128]{1,0:T(8,128)(2,1)}), bf16[4096,1024]{1,0:T(8,128)(2,1)}) %all-gather.23.cloned.1.call-update) | async-done | bytes 8388624 | tf_op jit(solution)/shard_map/all_gather | solution.py:92
  224.1 50.1 %all-gather.19.cloned.1.call-done = bf16[1024,4096]{1,0:T(8,128)(2,1)} async-done(((bf16[1024,512]{1,0:T(8,128)(2,1)}), bf16[1024,4096]{1,0:T(8,128)(2,1)}) %all-gather.19.cloned.1.call-update) | async-done | bytes 8388624 | tf_op jit(solution)/shard_map/all_gather | solution.py:91
  331.6 37.5 %reduce-scatter.31.cloned.1.call-done = f32[256,1024]{1,0:T(8,128)} async-done(((f32[1024,1024]{1,0:T(8,128)}), f32[256,1024]{1,0:T(8,128)}) %reduce-scatter.31.cloned.1.call-update) | async-done | bytes 1048592 | tf_op jit(solution)/shard_map/reduce_scatter | solution.py:192
  369.1 214.9 %reduce-scatter.21.cloned.1.call-done = f32[256,3072]{1,0:T(8,128)} async-done(((f32[1024,3072]{1,0:T(8,128)}), f32[256,3072]{1,0:T(8,128)}) %reduce-scatter.21.cloned.1.call-update) | async-done | bytes 3145744 | tf_op jit(solution)/shard_map/reduce_scatter | solution.py:191
  584.0 283.9 %reduce-scatter.41.cloned.1.call-done = f32[256,4096]{1,0:T(8,128)} async-done(((f32[1024,4096]{1,0:T(8,128)}), f32[256,4096]{1,0:T(8,128)}) %reduce-scatter.41.cloned.1.call-update) | async-done | bytes 4194320 | tf_op jit(solution)/shard_map/reduce_scatter | solution.py:193
  867.9 283.3 %reduce-scatter.51.cloned.1.call-done = f32[1024,1024]{1,0:T(8,128)} async-done(((f32[4096,1024]{1,0:T(8,128)}), f32[1024,1024]{1,0:T(8,128)}) %reduce-scatter.51.cloned.1.call-update) | async-done | bytes 4194320 | tf_op jit(solution)/shard_map/reduce_scatter | solution.py:194
  1151.2 178.6 %all-reduce.4.cloned.1.call-done = (f32[256,3072]{1,0:T(8,128)}, f32[256,1024]{1,0:T(8,128)}, f32[256,4096]{1,0:T(8,128)}, f32[1024,1024]{1,0:T(8,128)}) async-done(((f32[256,3072]{1,0:T(8,128)}, f32[256,1024]{1,0:T(8,128)}, f32[256,4096]{1,0:T(8,128)}, f32[1024,1024]{1,0:T(8,128)}), (f32[256,3072]{1,0:T(8,128)}, f32[256,1024]{1,0:T(8,128)}, f32[256,4096]{1,0:T(8,128)}, ...) | async-done | bytes 12582928 | tf_op jit(solution)/shard_map/psum | solution.py:197
  1340.2 29.9 %all-gather.25.cloned.1.call-done = f32[1024,384]{1,0:T(8,128)} async-done(((f32[256,384]{1,0:T(8,128)}), f32[1024,384]{1,0:T(8,128)}) %all-gather.25.cloned.1.call-update) | async-done | bytes 1572880 | tf_op jit(solution)/shard_map/all_gather | solution.py:213
  1378.3 38.8 %all-gather.29.cloned.1.call-done = f32[1024,512]{1,0:T(8,128)} async-done(((f32[256,512]{1,0:T(8,128)}), f32[1024,512]{1,0:T(8,128)}) %all-gather.29.cloned.1.call-update) | async-done | bytes 2097168 | tf_op jit(solution)/shard_map/all_gather | solution.py:215
  1426.9 36.9 %all-gather.33.cloned.1.call-done = f32[4096,128]{1,0:T(8,128)} async-done(((f32[1024,128]{1,0:T(8,128)}), f32[4096,128]{1,0:T(8,128)}) %all-gather.33.cloned.1.call-update) | async-done | bytes 2097168 | tf_op jit(solution)/shard_map/all_gather | solution.py:216
  1512.0 54.8 %reduce-scatter.47.cloned.1.call-done = f32[128,1024]{1,0:T(8,128)} async-done(((f32[1024,1024]{1,0:T(8,128)}), f32[128,1024]{1,0:T(8,128)}) %reduce-scatter.47.cloned.1.call-update) | async-done | bytes 524304 | tf_op jit(solution)/shard_map/reduce_scatter | solution.py:230
  1566.9 54.5 %reduce-scatter.57.cloned.1.call-done = f32[512,256]{1,0:T(8,128)} async-done(((f32[4096,256]{1,0:T(8,128)}), f32[512,256]{1,0:T(8,128)}) %reduce-scatter.57.cloned.1.call-update) | async-done | bytes 524304 | tf_op jit(solution)/shard_map/reduce_scatter | solution.py:231
  1630.9 30.5 %reduce-scatter.37.cloned.1.call-done = f32[128,256]{1,0:T(8,128)} async-done(((f32[1024,256]{1,0:T(8,128)}), f32[128,256]{1,0:T(8,128)}) %reduce-scatter.37.cloned.1.call-update) | async-done | bytes 131088 | tf_op jit(solution)/shard_map/reduce_scatter | solution.py:229
  1719.5 28.6 %all-gather.31.cloned.1.call-done = f32[128,4096]{1,0:T(8,128)} async-done(((f32[128,1024]{1,0:T(8,128)}), f32[128,4096]{1,0:T(8,128)}) %all-gather.31.cloned.1.call-update) | async-done | bytes 2097168 | tf_op jit(solution)/shard_map/all_gather | solution.py:242
  1755.2 39.3 %all-gather.35.cloned.1.call-done = f32[512,1024]{1,0:T(8,128)} async-done(((f32[512,256]{1,0:T(8,128)}), f32[512,1024]{1,0:T(8,128)}) %all-gather.35.cloned.1.call-update) | async-done | bytes 2097168 | tf_op jit(solution)/shard_map/all_gather | solution.py:243
  1919.8 38.3 %reduce-scatter.23.cloned.1.call-done = f32[256,128]{1,0:T(8,128)} async-done(((f32[256,1024]{1,0:T(8,128)}), f32[256,128]{1,0:T(8,128)}) %reduce-scatter.23.cloned.1.call-update) | async-done | bytes 131088 | tf_op jit(solution)/shard_map/reduce_scatter | solution.py:224
  1959.7 37.8 %reduce-scatter.43.cloned.1.call-done = f32[256,128]{1,0:T(8,128)} async-done(((f32[256,1024]{1,0:T(8,128)}), f32[256,128]{1,0:T(8,128)}) %reduce-scatter.43.cloned.1.call-update) | async-done | bytes 131088 | tf_op jit(solution)/shard_map/reduce_scatter | solution.py:226
  1999.1 86.1 %reduce-scatter.25.cloned.1.call-done = f32[384,768]{1,0:T(8,128)} async-done(((f32[384,3072]{1,0:T(8,128)}), f32[384,768]{1,0:T(8,128)}) %reduce-scatter.25.cloned.1.call-update) | async-done | bytes 1179664 | tf_op jit(solution)/shard_map/reduce_scatter | solution.py:234
  2087.6 48.1 %reduce-scatter.29.cloned.1.call-done = f32[256,384]{0,1:T(8,128)} async-done(((f32[256,3072]{0,1:T(8,128)}), f32[256,384]{0,1:T(8,128)}) %reduce-scatter.29.cloned.1.call-update) | async-done | bytes 393232 | tf_op jit(solution)/shard_map/reduce_scatter | solution.py:247
  2142.4 140.0 %reduce-scatter.45.cloned.1.call-done = f32[512,1024]{1,0:T(8,128)} async-done(((f32[512,4096]{1,0:T(8,128)}), f32[512,1024]{1,0:T(8,128)}) %reduce-scatter.45.cloned.1.call-update) | async-done | bytes 2097168 | tf_op jit(solution)/shard_map/reduce_scatter | solution.py:236
  2286.0 51.9 %reduce-scatter.49.cloned.1.call-done = f32[256,512]{0,1:T(8,128)} async-done(((f32[256,4096]{0,1:T(8,128)}), f32[256,512]{0,1:T(8,128)}) %reduce-scatter.49.cloned.1.call-update) | async-done | bytes 524304 | tf_op jit(solution)/shard_map/reduce_scatter | solution.py:249
  2342.2 50.8 %reduce-scatter.59.cloned.1.call-done = f32[1024,128]{0,1:T(8,128)} async-done(((f32[1024,1024]{0,1:T(8,128)}), f32[1024,128]{0,1:T(8,128)}) %reduce-scatter.59.cloned.1.call-update) | async-done | bytes 524304 | tf_op jit(solution)/shard_map/reduce_scatter | solution.py:250
  2397.0 115.4 %reduce-scatter.53.cloned.1.call-done = f32[1024,512]{1,0:T(8,128)} async-done(((f32[1024,4096]{1,0:T(8,128)}), f32[1024,512]{1,0:T(8,128)}) %reduce-scatter.53.cloned.1.call-update) | async-done | bytes 2097168 | tf_op jit(solution)/shard_map/reduce_scatter | solution.py:227
  (334 shorter events, 489.1 us)
Async XLA Ops:
  56.7 217.5 %all-gather.19.cloned.1.call-start = ((), (), s32[]{:S(2)}) async-start(), calls=%async_computation.23 | async-start | bytes 9437184 | tf_op jit(solution)/shard_map/all_gather | solution.py:91
  80.7 288.4 %reduce-scatter.31.cloned.1.call-start = ((), (), s32[]{:S(2)}) async-start(), calls=%async_computation.33 | async-start | bytes 5242880 | tf_op jit(solution)/shard_map/reduce_scatter | solution.py:192
  292.2 291.8 %reduce-scatter.21.cloned.1.call-start = ((), (), s32[]{:S(2)}) async-start(), calls=%async_computation.26 | async-start | bytes 15728640 | tf_op jit(solution)/shard_map/reduce_scatter | solution.py:191
  310.3 557.6 %reduce-scatter.41.cloned.1.call-start = ((), (), s32[]{:S(2)}) async-start(), calls=%async_computation.38 | async-start | bytes 20971520 | tf_op jit(solution)/shard_map/reduce_scatter | solution.py:193
  320.8 830.3 %reduce-scatter.51.cloned.1.call-start = ((), (), s32[]{:S(2)}) async-start(), calls=%async_computation.45 | async-start | bytes 20971520 | tf_op jit(solution)/shard_map/reduce_scatter | solution.py:194
  331.5 998.3 %all-reduce.4.cloned.1.call-start = ((), (), s32[]{:S(2)}) async-start(), calls=%async_computation.52 | async-start | bytes 25165824 | tf_op jit(solution)/shard_map/psum | solution.py:197
  1151.2 218.9 %all-gather.25.cloned.1.call-start = ((), (), s32[]{:S(2)}) async-start(), calls=%async_computation.27 | async-start | bytes 1966080 | tf_op jit(solution)/shard_map/all_gather | solution.py:213
  1426.8 194.6 %reduce-scatter.57.cloned.1.call-start = ((), (), s32[]{:S(2)}) async-start(), calls=%async_computation.49 | async-start | bytes 4718592 | tf_op jit(solution)/shard_map/reduce_scatter | solution.py:231
  1470.8 190.6 %reduce-scatter.37.cloned.1.call-start = ((), (), s32[]{:S(2)}) async-start(), calls=%async_computation.36 | async-start | bytes 1179648 | tf_op jit(solution)/shard_map/reduce_scatter | solution.py:229
  1490.2 212.2 %all-gather.27.cloned.1.call-start = ((), (), s32[]{:S(2)}) async-start(), calls=%async_computation.31 | async-start | bytes 1966080 | tf_op jit(solution)/shard_map/all_gather | solution.py:240
  1512.0 236.1 %all-gather.31.cloned.1.call-start = ((), (), s32[]{:S(2)}) async-start(), calls=%async_computation.43 | async-start | bytes 2621440 | tf_op jit(solution)/shard_map/all_gather | solution.py:242
  1566.9 227.6 %all-gather.35.cloned.1.call-start = ((), (), s32[]{:S(2)}) async-start(), calls=%async_computation.50 | async-start | bytes 2621440 | tf_op jit(solution)/shard_map/all_gather | solution.py:243
  1621.4 269.2 %reduce-scatter.35.cloned.1.call-start = ((), (), s32[]{:S(2)}) async-start(), calls=%async_computation.35 | async-start | bytes 655360 | tf_op jit(solution)/shard_map/reduce_scatter | solution.py:235
  1623.0 269.3 %reduce-scatter.55.cloned.1.call-start = ((), (), s32[]{:S(2)}) async-start(), calls=%async_computation.48 | async-start | bytes 655360 | tf_op jit(solution)/shard_map/reduce_scatter | solution.py:237
  1628.8 265.1 %reduce-scatter.33.cloned.1.call-start = ((), (), s32[]{:S(2)}) async-start(), calls=%async_computation.34 | async-start | bytes 1179648 | tf_op jit(solution)/shard_map/reduce_scatter | solution.py:225
  1630.9 287.2 %reduce-scatter.39.cloned.1.call-start = ((), (), s32[]{:S(2)}) async-start(), calls=%async_computation.37 | async-start | bytes 1179648 | tf_op jit(solution)/shard_map/reduce_scatter | solution.py:248
  1682.3 275.8 %reduce-scatter.23.cloned.1.call-start = ((), (), s32[]{:S(2)}) async-start(), calls=%async_computation.28 | async-start | bytes 1179648 | tf_op jit(solution)/shard_map/reduce_scatter | solution.py:224
  1686.9 310.6 %reduce-scatter.43.cloned.1.call-start = ((), (), s32[]{:S(2)}) async-start(), calls=%async_computation.40 | async-start | bytes 1179648 | tf_op jit(solution)/shard_map/reduce_scatter | solution.py:226
  1690.0 395.2 %reduce-scatter.25.cloned.1.call-start = ((), (), s32[]{:S(2)}) async-start(), calls=%async_computation.29 | async-start | bytes 5898240 | tf_op jit(solution)/shard_map/reduce_scatter | solution.py:234
  1698.5 437.2 %reduce-scatter.29.cloned.1.call-start = ((), (), s32[]{:S(2)}) async-start(), calls=%async_computation.32 | async-start | bytes 3538944 | tf_op jit(solution)/shard_map/reduce_scatter | solution.py:247
  1708.2 574.3 %reduce-scatter.45.cloned.1.call-start = ((), (), s32[]{:S(2)}) async-start(), calls=%async_computation.41 | async-start | bytes 10485760 | tf_op jit(solution)/shard_map/reduce_scatter | solution.py:236
  1719.0 618.9 %reduce-scatter.49.cloned.1.call-start = ((), (), s32[]{:S(2)}) async-start(), calls=%async_computation.44 | async-start | bytes 4718592 | tf_op jit(solution)/shard_map/reduce_scatter | solution.py:249
  1755.1 637.9 %reduce-scatter.59.cloned.1.call-start = ((), (), s32[]{:S(2)}) async-start(), calls=%async_computation.51 | async-start | bytes 4718592 | tf_op jit(solution)/shard_map/reduce_scatter | solution.py:250
  1810.5 701.9 %reduce-scatter.53.cloned.1.call-start = ((), (), s32[]{:S(2)}) async-start(), calls=%async_computation.47 | async-start | bytes 18874368 | tf_op jit(solution)/shard_map/reduce_scatter | solution.py:227
  (77 other events, 4966.0 us)
Sparse Core Ops, SparseCore 0:
  10.2 40.1 all-gather.20
  82.5 46.1 all-gather.12
  160.4 55.9 all-gather.22
  218.1 55.9 all-gather.18
  292.3 76.7 reduce-scatter.30
  371.6 212.3 reduce-scatter.20
  586.5 281.3 reduce-scatter.40
  870.1 281.0 reduce-scatter.50
  1155.6 174.1 all-reduce.3
  1332.9 37.1 all-gather.24
  1372.2 44.7 all-gather.28
  1419.1 44.6 all-gather.32
  1467.0 44.9 reduce-scatter.26
  1515.5 51.2 reduce-scatter.46
  1570.1 51.3 reduce-scatter.56
  1663.1 39.2 all-gather.26
  1703.9 44.1 all-gather.30
  1749.8 44.6 all-gather.34
  1999.9 85.2 reduce-scatter.24
  2089.0 46.7 reduce-scatter.28
  2137.9 144.4 reduce-scatter.44
  2285.8 52.0 reduce-scatter.48
  2341.6 51.3 reduce-scatter.58
  2396.4 115.9 reduce-scatter.52
  (9 shorter events, 274.5 us)
where the time goes:
time: 2530 us; the launch traced here: 2520 us
  waiting for transfers between devices  2110 us (83%)
  matrix products  186 us (7%)
  blocking collectives  133 us (5%)
  other arithmetic  40.8 us (2%)
  local copies, waits for them, and re-layouts  32.9 us (1%)
    reduce_scatter x1, waiting for transfers between devices, on_device(): lax.psum_scatter(grad_fc, 'in', scatter_dimension=0, tiled=True)  284 us
    reduce_scatter x1, waiting for transfers between devices, on_device(): lax.psum_scatter(grad_proj, 'in', scatter_dimension=0, tiled=True)  283 us
    reduce_scatter x1, waiting for transfers between devices, on_device(): lax.psum_scatter(grad_qkv, 'in', scatter_dimension=0, tiled=True)  215 us
    psum x1, waiting for transfers between devices, on_device(): lax.psum((qkv_part, out_part, fc_part, proj_part, vector_part), 'grp')  179 us
    reduce_scatter x1, waiting for transfers between devices, on_device(): lax.psum_scatter(right_terms[2], 'in', scatter_dimension=1, tiled=True)  140 us
    reduce_scatter x1, waiting for transfers between devices, on_device(): lax.psum_scatter(left_terms[3], 'grp', scatter_dimension=1, tiled=True)  115 us
    dot_general x16, matrix products, precise(): jnp.dot(left, right, precision=PRECISE, preferred_element_type=jnp.float32)  109 us
    reduce_scatter x1, waiting for transfers between devices, on_device(): lax.psum_scatter(right_terms[0], 'in', scatter_dimension=1, tiled=True)  86.1 us
  transfers between devices with their start and end apart: 33, of which 29 were waited for; matrix products, arithmetic and copies ran while one was open for 9% of the time, Pallas kernels for 0%

commit v1 on v0

v1 whole, which is shorter than its diff:
```python
import math

import jax
import jax.numpy as jnp
import numpy as np
from jax import lax
from jax.experimental import pallas as pl
from jax.experimental.pallas import tpu as pltpu
from jax.sharding import Mesh
from jax.sharding import PartitionSpec as P

HEADS = 16
HEAD_DIM = 64
EPSILON = 1e-05
DECAY = 0.5
MOMENTUM = 0.5
RATE = 0.03
MASKED = -1e30
ROOT_TWO_PI = math.sqrt(2.0 / math.pi)
BF16 = jnp.bfloat16
F32 = jnp.float32
PLANE = ("y", "x")
CHIPS = ("y", "x", "in")
ALL = ("y", "x", "c", "in")


def dot(left, right):
    return jnp.dot(left, right, preferred_element_type=F32)


def dot_tn(left, right):
    return lax.dot_general(left, right, (((0,), (0,)), ((), ())), preferred_element_type=F32)


def dot_nt(left, right):
    return lax.dot_general(left, right, (((1,), (1,)), ((), ())), preferred_element_type=F32)


def lane_half(shape, half):
    return (lax.broadcasted_iota(jnp.int32, shape, 1) // HEAD_DIM) == half


def softmax_rows(scores):
    shifted = jnp.exp(scores - jnp.max(scores, axis=-1, keepdims=True))
    return shifted / jnp.sum(shifted, axis=-1, keepdims=True)


def attention_forward(qkv, bias):
    sequences, length, _ = bias.shape
    width = qkv.shape[1] // 3
    pair = 2 * HEAD_DIM
    scale = HEAD_DIM ** (-0.5)

    def body(qkv_ref, bias_ref, out_ref):
        for seq in range(sequences):
            rows = slice(seq * length, (seq + 1) * length)
            mask = bias_ref[seq]
            for col in range(0, width, pair):
                queries = qkv_ref[rows, col : col + pair]
                key_rows = qkv_ref[rows, width + col : width + col + pair]
                value_rows = qkv_ref[rows, 2 * width + col : 2 * width + col + pair]
                parts = []
                for half in range(2):
                    own = jnp.where(lane_half(queries.shape, half), queries, jnp.zeros_like(queries))
                    probs = softmax_rows(dot_nt(own, key_rows) * scale + mask)
                    parts.append(dot(probs.astype(BF16), value_rows))
                picked = jnp.where(lane_half(parts[0].shape, 0), parts[0], parts[1])
                out_ref[rows, col : col + pair] = picked.astype(BF16)

    return pl.pallas_call(
        body,
        out_shape=jax.ShapeDtypeStruct((qkv.shape[0], width), BF16),
        in_specs=[pl.BlockSpec(memory_space=pltpu.VMEM)] * 2,
        out_specs=pl.BlockSpec(memory_space=pltpu.VMEM),
        name="attention_forward",
    )(qkv, bias)


def attention_backward(qkv, bias, grad):
    sequences, length, _ = bias.shape
    width = qkv.shape[1] // 3
    pair = 2 * HEAD_DIM
    scale = HEAD_DIM ** (-0.5)

    def body(qkv_ref, bias_ref, grad_ref, out_ref):
        for seq in range(sequences):
            rows = slice(seq * length, (seq + 1) * length)
            mask = bias_ref[seq]
            for col in range(0, width, pair):
                queries = qkv_ref[rows, col : col + pair]
                key_rows = qkv_ref[rows, width + col : width + col + pair]
                value_rows = qkv_ref[rows, 2 * width + col : 2 * width + col + pair]
                grads = grad_ref[rows, col : col + pair]
                found = []
                for half in range(2):
                    lanes = lane_half(queries.shape, half)
                    own = jnp.where(lanes, queries, jnp.zeros_like(queries))
                    probs = softmax_rows(dot_nt(own, key_rows) * scale + mask)
                    own_grad = jnp.where(lanes, grads, jnp.zeros_like(grads))
                    grad_probs = dot_nt(own_grad, value_rows)
                    row_dot = jnp.sum(probs * grad_probs, axis=-1, keepdims=True)
                    grad_scores = (probs * (grad_probs - row_dot)).astype(BF16)
                    found.append(
                        (
                            dot(grad_scores, key_rows) * scale,
                            dot_tn(grad_scores, queries) * scale,
                            dot_tn(probs.astype(BF16), grads),
                        )
                    )
                low_lanes = lane_half((length, pair), 0)
                for third in range(3):
                    picked = jnp.where(low_lanes, found[0][third], found[1][third])
                    start = third * width + col
                    out_ref[rows, start : start + pair] = picked.astype(BF16)

    return pl.pallas_call(
        body,
        out_shape=jax.ShapeDtypeStruct(qkv.shape, BF16),
        in_specs=[pl.BlockSpec(memory_space=pltpu.VMEM)] * 3,
        out_specs=pl.BlockSpec(memory_space=pltpu.VMEM),
        name="attention_backward",
    )(qkv, bias, grad)


def assemble(pieces, places, axis):
    count, shape = len(pieces), pieces[0].shape
    size = shape[axis]

    def body(place_ref, *refs):
        for k in range(count):
            span = pl.ds(pl.multiple_of(place_ref[k] * size, size), size)
            if axis == 0:
                refs[count][span, :] = refs[k][...]
            else:
                refs[count][:, span] = refs[k][...]

    in_vmem = pl.BlockSpec(memory_space=pltpu.VMEM)
    whole = tuple(extent * (count if n == axis else 1) for n, extent in enumerate(shape))
    return pl.pallas_call(
        body,
        out_shape=jax.ShapeDtypeStruct(whole, pieces[0].dtype),
        in_specs=[pl.BlockSpec(memory_space=pltpu.SMEM)] + [in_vmem] * count,
        out_specs=in_vmem,
        name="assemble",
    )(jnp.stack(places).astype(jnp.int32), *pieces)


def whole(array):
    return pl.BlockSpec(array.shape, lambda step: (0,) * len(array.shape))


def column_kernel(own, blocks, which, right_root, numbers):
    width, cols = own.shape
    count, _, rows, share = blocks.shape
    chunks = width // rows

    def body(number_ref, own_ref, block_ref, right_ref, mine_ref, theirs_ref, left_ref):
        core, depth = number_ref[0], number_ref[1]
        near = own_ref[pl.ds(pl.multiple_of(depth * rows, rows), rows), :]

        @pl.loop(0, chunks)
        def _(d):
            chunk = number_ref[2 + d]
            for g in range(count // chunks):
                left_ref[:, g * share : (g + 1) * share] = block_ref[g * chunks + chunk, 0]
            image = dot(left_ref[...], own_ref[...]).astype(BF16)
            span = pl.ds(pl.multiple_of(d * rows, rows), rows)
            for pick, target in ((core, mine_ref), (1 - core, theirs_ref)):
                right = right_ref[:, pl.ds(pl.multiple_of(pick * cols, cols), cols)].astype(BF16)
                start = pl.multiple_of(chunk * rows + pick * share, share)
                target[span, :cols] = dot(image, right).astype(target.dtype)
                left = dot_nt(near, own_ref[pl.ds(start, share), :])
                target[span, cols:] = left.astype(target.dtype)

    shape = (width, cols + share)
    return pl.pallas_call(
        body,
        grid=(1,),
        out_shape=(jax.ShapeDtypeStruct(shape, F32), jax.ShapeDtypeStruct(shape, BF16)),
        in_specs=[
            pl.BlockSpec(memory_space=pltpu.SMEM),
            whole(own),
            pl.BlockSpec((count, 1, rows, share), lambda step: (0, which, 0, 0)),
            whole(right_root),
        ],
        out_specs=(pl.BlockSpec(shape, lambda step: (0, 0)),) * 2,
        scratch_shapes=[pltpu.VMEM((rows, width), BF16)],
        compiler_params=pltpu.CompilerParams(vmem_limit_bytes=40 << 20),
        name="column_terms",
    )(numbers, own, blocks, right_root)


def row_kernel(own, blocks, which, left_root, numbers):
    count, width = own.shape
    devices, _, rows, share = blocks.shape
    chunks = width // rows
    tall = left_root.shape[0]
    piece = tall + 2 * share

    def body(number_ref, own_ref, block_ref, left_ref, mine_ref, theirs_ref, right_ref):
        core, depth = number_ref[0], number_ref[1]
        targets = ((core, mine_ref), (1 - core, theirs_ref))
        near = own_ref[:, pl.ds(pl.multiple_of(depth * rows, rows), rows)]
        for d in range(chunks):
            chunk = number_ref[2 + d]
            for k, (pick, target) in enumerate(targets):
                part = pl.ds(pl.multiple_of(pick * share, share), share)
                lanes = slice((k * chunks + d) * share, (k * chunks + d + 1) * share)
                for g in range(devices // chunks):
                    right_ref[g * share : (g + 1) * share, lanes] = block_ref[
                        g * chunks + chunk, 0, part, :
                    ]
                start = pl.multiple_of(chunk * rows + pick * share, share)
                right = dot_tn(own_ref[:, pl.ds(start, share)], near).astype(target.dtype)
                low = d * piece + tall
                target[low : low + share, :] = right[:, :share]
                target[low + share : low + 2 * share, :] = right[:, share:]
        image = dot(own_ref[...], right_ref[...]).astype(BF16)
        for first in range(0, tall, rows):
            ahead = dot(left_ref[first : first + rows, :].astype(BF16), image)
            for k, (_, target) in enumerate(targets):
                for d in range(chunks):
                    lanes = slice((k * chunks + d) * share, (k * chunks + d + 1) * share)
                    low = d * piece + first
                    target[low : low + rows, :] = ahead[:, lanes].astype(target.dtype)

    shape = (chunks * piece, share)
    return pl.pallas_call(
        body,
        grid=(1,),
        out_shape=(jax.ShapeDtypeStruct(shape, F32), jax.ShapeDtypeStruct(shape, BF16)),
        in_specs=[
            pl.BlockSpec(memory_space=pltpu.SMEM),
            whole(own),
            pl.BlockSpec((devices, 1, rows, share), lambda step: (0, which, 0, 0)),
            whole(left_root),
        ],
        out_specs=(pl.BlockSpec(shape, lambda step: (0, 0)),) * 2,
        scratch_shapes=[pltpu.VMEM((width, width), BF16)],
        compiler_params=pltpu.CompilerParams(vmem_limit_bytes=40 << 20),
        name="row_terms",
    )(numbers, own, blocks, left_root)


class Place:
    def __init__(self):
        self.rows = lax.axis_size("y")
        self.plane = self.rows * lax.axis_size("x")
        self.depth = lax.axis_size("in")
        self.q = lax.axis_index("y") * lax.axis_size("x") + lax.axis_index("x")
        self.c = lax.axis_index("c")
        self.z = lax.axis_index("in")
        self.last = {}

    def send(self, value, axes, pairs, lane=None):
        if lane in self.last:
            value, _ = lax.optimization_barrier((value, self.last[lane]))
        value = lax.ppermute(value, axes, pairs)
        if lane is not None:
            self.last[lane] = value
        return value

    def swap_core(self, value):
        return self.send(value, "c", [(0, 1), (1, 0)])

    def swap_plane(self, value, distance):
        pairs = [(k, k ^ distance) for k in range(self.plane)]
        return self.send(value, PLANE, pairs, distance)

    def ring(self, value):
        return self.send(value, "in", [(k, (k + 1) % self.depth) for k in range(self.depth)], "z")

    def on_chips(self, value, target, lane):
        pairs = []
        for q in range(self.plane):
            for z in range(self.depth):
                found = target(q, z)
                if found is not None:
                    pairs.append((q * self.depth + z, found[0] * self.depth + found[1]))
        return self.send(value, CHIPS, pairs, lane)

    def by_core(self, own, other):
        return jnp.where(self.c == 0, own, other), jnp.where(self.c == 0, other, own)

    def mine(self, pair):
        return jnp.where(self.c == 0, pair[0], pair[1])

    def theirs(self, pair):
        return jnp.where(self.c == 0, pair[1], pair[0])

    def shuffle(self, values, index):
        values = list(values)
        bit = 1
        while bit < len(values):
            on = (index // bit) % 2 == 1
            values = [jnp.where(on, values[k ^ bit], values[k]) for k in range(len(values))]
            bit *= 2
        return values

    def ring_pieces(self, value):
        pieces = [value]
        for _ in range(self.depth - 1):
            pieces.append(self.ring(pieces[-1]))
        return pieces

    def gather_depth(self, value, axis=0):
        places = [(self.z - k) % self.depth for k in range(self.depth)]
        return assemble(self.ring_pieces(value), places, axis)

    def transpose_chips(self, value):
        return self.on_chips(value, lambda q, z: (z, q), "z")

    def spread_plane(self, value):
        q, z = self.q, self.z
        if self.plane != 4:
            total = jnp.where(q == z, value, jnp.zeros_like(value))
            for d in range(1, self.plane):
                total = total + self.on_chips(
                    value, lambda a, b, d=d: (a ^ d, b) if a == b else None, d
                )
            return total
        half = value.shape[0] // 2
        low, high = value[:half], value[half:]
        low_x = self.on_chips(low, lambda a, b: (a ^ 1, b) if a == b else None, 1)
        high_y = self.on_chips(high, lambda a, b: (a ^ 2, b) if a == b else None, 2)
        high_x = self.on_chips(
            jnp.where(q == z, high, high_y), lambda a, b: (a ^ 1, b) if a ^ b in (0, 2) else None, 1
        )
        low_y = self.on_chips(
            jnp.where(q == z, low, low_x), lambda a, b: (a ^ 2, b) if a ^ b in (0, 1) else None, 2
        )
        apart = q ^ z
        low = jnp.where(apart == 0, low, jnp.where(apart == 1, low_x, low_y))
        high = jnp.where(apart == 0, high, jnp.where(apart == 2, high_y, high_x))
        return jnp.concatenate([low, high])

    def gather_tokens(self, value):
        mine = jnp.concatenate(self.gather_plane(value))
        return jnp.concatenate([mine, self.swap_core(mine)])

    def reduce_tokens(self, mine, theirs):
        total = mine + self.swap_core(theirs.astype(BF16)).astype(F32)
        return self.reduce_plane(jnp.split(total, self.plane))

    def gather_plane(self, value):
        if self.plane != 4:
            return [value] + [self.swap_plane(value, d) for d in range(1, self.plane)]
        half = value.shape[0] // 2
        by_x = self.swap_plane(value, 1)
        by_y = self.swap_plane(value, 2)
        first = self.swap_plane(by_y[:half], 1)
        second = self.swap_plane(by_x[half:], 2)
        return [value, by_x, by_y, jnp.concatenate([first, second])]

    def reduce_plane(self, values):
        if self.plane != 4:
            total = values[0]
            for d in range(1, self.plane):
                total = total + self.swap_plane(values[d].astype(BF16), d).astype(F32)
            return total
        half = values[0].shape[0] // 2
        far = values[3].astype(BF16)
        first = self.swap_plane(far[:half], 1)
        second = self.swap_plane(far[half:], 2)
        to_y = jnp.concatenate([values[2][:half] + first.astype(F32), values[2][half:]]).astype(BF16)
        to_x = jnp.concatenate([values[1][:half], values[1][half:] + second.astype(F32)]).astype(BF16)
        by_x = self.swap_plane(to_x, 1)
        by_y = self.swap_plane(to_y, 2)
        return values[0] + by_x.astype(F32) + by_y.astype(F32)

    def reduce_depth(self, value, sent=BF16, axis=0):
        size = value.shape[axis] // self.depth
        total = None
        for step in range(self.depth):
            place = (self.z - 1 - step) % self.depth
            chunk = lax.dynamic_slice_in_dim(value, place * size, size, axis)
            total = chunk if total is None else total.astype(F32) + chunk
            if step < self.depth - 1:
                total = self.ring(total.astype(sent))
        return total


def norm_parts(values):
    centred = values - jnp.mean(values, axis=-1, keepdims=True)
    spread = lax.rsqrt(jnp.mean(centred * centred, axis=-1, keepdims=True) + EPSILON)
    return centred * spread, spread


def norm_backward(grad, scaled, spread, gain):
    inner = grad * gain
    mean_one = jnp.mean(inner, axis=-1, keepdims=True)
    mean_two = jnp.mean(inner * scaled, axis=-1, keepdims=True)
    return spread * (inner - mean_one - scaled * mean_two)


def gelu(values):
    return 0.5 * values * (1.0 + jnp.tanh(ROOT_TWO_PI * (values + 0.044715 * values**3)))


def gelu_slope(values):
    squared = values * values
    bent = jnp.tanh(ROOT_TWO_PI * (values + 0.044715 * squared * values))
    return 0.5 * (1.0 + bent) + 0.5 * values * (1.0 - bent * bent) * (
        ROOT_TWO_PI * (1.0 + 3.0 * 0.044715 * squared)
    )


def on_device(
    tokens,
    segments,
    cotangent,
    vectors,
    vector_moment,
    qkv_weight,
    qkv_moment,
    qkv_left,
    qkv_right,
    qkv_left_root,
    qkv_right_root,
    out_weight,
    out_moment,
    out_left,
    out_right,
    out_left_root,
    out_right_root,
    fc_weight,
    fc_moment,
    fc_left,
    fc_right,
    fc_left_root,
    fc_right_root,
    proj_weight,
    proj_moment,
    proj_left,
    proj_right,
    proj_left_root,
    proj_right_root,
):
    here = Place()
    plane, depth = here.plane, here.depth
    length, width = tokens.shape
    z, q, c = here.z, here.q, here.c

    def pair_columns(share):
        return jnp.concatenate(here.by_core(share, here.swap_core(share)), axis=1)

    def by_parity(pair):
        rows, cols = pair.shape
        split = pair.reshape(rows, cols // (2 * HEAD_DIM), 2, HEAD_DIM)
        return here.mine((split[:, :, 0], split[:, :, 1])).reshape(rows, cols // 2)

    qkv_share = by_parity(pair_columns(qkv_weight.astype(BF16)))
    fc_share = fc_weight.astype(BF16)
    proj_split = proj_weight.astype(BF16).reshape(2, -1, proj_weight.shape[1])
    proj_share = jnp.concatenate(
        here.by_core(here.mine(proj_split), here.swap_core(here.theirs(proj_split))), axis=1
    )
    out_split = out_weight.astype(BF16).reshape(-1, 2, HEAD_DIM, out_weight.shape[1])
    out_split = (
        out_split[:, 0].reshape(-1, out_weight.shape[1]),
        out_split[:, 1].reshape(-1, out_weight.shape[1]),
    )
    out_share = jnp.concatenate(
        here.by_core(here.mine(out_split), here.swap_core(here.theirs(out_split))), axis=1
    )

    plane_cotangent = here.gather_tokens(cotangent)
    qkv_parts = here.gather_plane(here.gather_depth(qkv_share))
    vector_whole = jnp.roll(
        jnp.concatenate(here.ring_pieces(vectors.astype(BF16))[::-1]), (z + 1) * vectors.shape[0]
    )
    out_parts = here.gather_plane(here.gather_depth(out_share))
    out_full = jnp.concatenate(here.shuffle(out_parts, q), axis=1)
    fc_full = here.gather_depth(fc_share)
    proj_full = here.gather_depth(here.transpose_chips(proj_share), axis=1)

    share_rows, share_cols = qkv_left_root.shape
    right_root = proj_right_root.astype(BF16)
    root_blocks = lax.all_gather(
        jnp.stack(
            [root.astype(BF16) for root in (qkv_left_root, out_left_root, fc_left_root)]
            + [jnp.concatenate([right_root[:, :share_cols], right_root[:, share_cols:]])]
        ),
        ALL,
    )
    numbers = jnp.stack([c, z] + [q ^ d for d in range(plane)]).astype(jnp.int32)

    params = vector_whole.astype(F32)
    unit = fc_weight.shape[1]
    hidden = unit * 2 * plane
    gain_one, shift_one, bias_query, bias_value, bias_out, gain_two, shift_two = (
        params[k * width : (k + 1) * width] for k in range(7)
    )
    bias_fc = lax.dynamic_slice_in_dim(params, 7 * width + (2 * q + c) * unit, unit)
    bias_proj = params[7 * width + hidden :]

    pair_tokens = jnp.concatenate([tokens, here.swap_core(tokens)])
    labels = jnp.concatenate([segments, here.swap_core(segments)])
    position = jnp.arange(length)
    allowed = (labels[:, :, None] == labels[:, None, :]) & (position[:, None] >= position[None, :])
    mask = jnp.where(allowed, 0.0, MASKED).astype(F32)

    inputs = pair_tokens.astype(F32)
    scaled_one, spread_one = norm_parts(inputs)
    normed_one = (scaled_one * gain_one + shift_one).astype(BF16)
    qkv_bias = jnp.concatenate([bias_query, jnp.zeros_like(bias_query), bias_value])
    qkv_bias = qkv_bias.reshape(-1, 2, HEAD_DIM)
    qkv_bias = here.mine((qkv_bias[:, 0], qkv_bias[:, 1])).reshape(-1)
    projected = jnp.concatenate(
        here.shuffle([dot(normed_one, part) for part in qkv_parts], q), axis=1
    )
    projected = (projected + qkv_bias).astype(BF16)
    attended = attention_forward(projected, mask)
    branch = dot(attended[:length], out_full) + here.swap_core(dot(attended[length:], out_full))
    middle = inputs[:length] + (branch + bias_out)
    scaled_two, spread_two = norm_parts(middle)
    normed_two = here.gather_tokens((scaled_two * gain_two + shift_two).astype(BF16))
    pre_act = dot(normed_two, fc_full) + bias_fc
    activated = gelu(pre_act).astype(BF16)

    token_total = length * 2 * plane * depth
    factor = 1.0 / math.sqrt(token_total)
    half = plane * length
    proj_sum = here.reduce_depth(dot_tn(activated, plane_cotangent), axis=1)
    grad_pre = (dot_nt(plane_cotangent, proj_full) * gelu_slope(pre_act)).astype(BF16)
    grad_normed_two = here.reduce_tokens(
        dot_nt(grad_pre[:half], fc_full), dot_nt(grad_pre[half:], fc_full)
    )
    fc_grad = here.reduce_depth(dot_tn(normed_two, grad_pre)) * factor
    output = here.reduce_tokens(
        dot(activated[:half], proj_full), dot(activated[half:], proj_full)
    )
    output = (middle + (output + bias_proj)).astype(BF16)

    proj_scaled = (proj_sum * factor).astype(BF16)
    proj_rows = here.transpose_chips(proj_scaled)
    proj_own = here.gather_depth(proj_scaled, axis=1)
    fc_own = here.gather_depth(fc_grad.astype(BF16))
    far_rows = jnp.concatenate(here.shuffle(here.gather_plane(proj_rows), q), axis=1)
    far_rows = jnp.concatenate(here.by_core(far_rows, here.swap_core(far_rows)))

    grad_top = cotangent.astype(F32)
    grad_middle = grad_top + norm_backward(grad_normed_two, scaled_two, spread_two, gain_two)
    own_branch = grad_middle.astype(BF16)
    grad_branch = jnp.concatenate([own_branch, here.swap_core(own_branch)])
    grad_attended = dot_nt(grad_branch, out_full).astype(BF16)
    grad_heads = attention_backward(projected, mask, grad_attended)
    head_blocks = here.shuffle(jnp.split(grad_heads, plane, axis=1), q)
    branch_blocks = here.shuffle(jnp.split(grad_branch, plane, axis=1), q)

    rows_own, qkv_cols = qkv_weight.shape
    out_cols = out_weight.shape[1]

    def out_term(block):
        term = dot_tn(attended, block).reshape(depth, -1, 2 * out_cols)
        term = jnp.concatenate([term[:, :, :out_cols], term[:, :, out_cols:]], axis=1)
        return term.reshape(width, out_cols)

    first_sum = here.reduce_depth(
        here.reduce_plane(
            [
                jnp.concatenate([dot_tn(normed_one, head), out_term(branch)], axis=1)
                for head, branch in zip(head_blocks, branch_blocks)
            ]
        )
    )
    first_sum = first_sum * factor

    other_one = sum(dot_nt(block[length:], part) for block, part in zip(head_blocks, qkv_parts))
    grad_normed_one = sum(dot_nt(block[:length], part) for block, part in zip(head_blocks, qkv_parts))
    grad_normed_one = grad_normed_one + here.swap_core(other_one)
    own_scaled = scaled_one[:length]
    grad_in = norm_backward(grad_normed_one, own_scaled, spread_one[:length], gain_one)
    input_grad = (grad_middle + grad_in).astype(BF16)

    proj_halves = jnp.split(proj_rows, 2, axis=1)
    proj_grad = jnp.concatenate(
        here.by_core(here.mine(proj_halves), here.swap_core(here.theirs(proj_halves)))
    ).astype(F32)

    qkv_parity = first_sum[:, :qkv_cols].reshape(rows_own, -1, 1, HEAD_DIM)
    qkv_pair = jnp.concatenate(here.by_core(qkv_parity, here.swap_core(qkv_parity)), axis=2)
    qkv_pair = qkv_pair.reshape(rows_own, 2 * qkv_cols)
    qkv_grad = here.mine((qkv_pair[:, :qkv_cols], qkv_pair[:, qkv_cols:]))
    out_halves = jnp.split(first_sum[:, qkv_cols:], 2)
    out_pair = here.by_core(here.mine(out_halves), here.swap_core(here.theirs(out_halves)))
    out_grad = jnp.stack(
        [part.reshape(-1, HEAD_DIM, out_cols) for part in out_pair], axis=1
    ).reshape(out_weight.shape)

    def sum_over_group(mine, theirs):
        total = mine + here.swap_core(theirs).astype(F32)
        return here.reduce_plane(jnp.split(total, plane))

    aligned = share_cols % 128 == 0

    def column_terms(own, which, right_root):
        if aligned:
            return column_kernel(own, root_blocks, which, right_root, numbers)
        blocks = root_blocks.reshape(2 * plane, depth, 4, share_rows, share_cols)[:, :, which]
        left_root = blocks.transpose(1, 2, 0, 3).reshape(depth, share_rows, width)
        left_root = jnp.concatenate(here.shuffle(list(left_root), q))
        image = dot(left_root, own).astype(BF16)
        right_halves = jnp.split(right_root.astype(BF16), 2, axis=1)
        left = dot_nt(lax.dynamic_slice_in_dim(own, z * rows_own, rows_own), own)
        left = here.shuffle(jnp.split(left, plane, axis=1), q)
        left = jnp.split(jnp.concatenate(left), 2, axis=1)
        mine, theirs = (
            jnp.concatenate([dot(image, pick(right_halves)), pick(left)], axis=1)
            for pick in (here.mine, here.theirs)
        )
        return mine, theirs.astype(BF16)

    def row_terms(own, which, left_root):
        if aligned:
            return row_kernel(own, root_blocks, which, left_root, numbers)
        blocks = root_blocks.reshape(2 * plane, depth, 4, 2, share_rows // 2, share_cols)[:, :, which]
        chunk = width // depth
        right = dot_tn(own, lax.dynamic_slice_in_dim(own, z * chunk, chunk, 1))
        right = here.shuffle(jnp.split(right, plane), q)
        left_root = left_root.astype(BF16)
        found = []
        for pick in (here.mine, here.theirs):
            root = pick((blocks[:, :, 0], blocks[:, :, 1]))
            root = [root[:, r].reshape(width, share_cols) for r in range(depth)]
            root = jnp.concatenate(here.shuffle(root, q), axis=1)
            ahead = jnp.split(dot(left_root, dot(own, root).astype(BF16)), plane, axis=1)
            stats = [
                jnp.concatenate(jnp.split(pick(jnp.split(pair, 2)), 2, axis=1)) for pair in right
            ]
            found.append(
                jnp.concatenate([jnp.concatenate(parts) for parts in zip(ahead, stats)])
            )
        return found[0], found[1].astype(BF16)

    def far_columns(own):
        far = here.spread_plane(own)
        return here.by_core(far, here.swap_core(far))

    proj_total = sum_over_group(*row_terms(proj_own, 3, proj_left_root))
    proj_direction = proj_total[: proj_weight.shape[0]]
    proj_right_sum = jnp.concatenate(jnp.split(proj_total[proj_weight.shape[0] :], 2), axis=1)
    proj_left_sum = dot_nt(far_rows, proj_own)

    unit_cols = fc_weight.shape[1]
    fc_total = sum_over_group(*column_terms(fc_own, 2, fc_right_root))
    fc_direction = here.transpose_chips(fc_total[:, :unit_cols].astype(BF16)).astype(F32)
    fc_left_sum = fc_total[:, unit_cols:]

    first_own = here.gather_depth(jnp.concatenate([qkv_grad, out_grad], axis=1).astype(BF16))
    qkv_own, out_own = first_own[:, :qkv_cols], first_own[:, qkv_cols:]
    qkv_total = sum_over_group(*column_terms(qkv_own, 0, qkv_right_root))
    qkv_direction = here.transpose_chips(qkv_total[:, :qkv_cols].astype(BF16)).astype(F32)
    qkv_left_sum = qkv_total[:, qkv_cols:]
    out_total = sum_over_group(*column_terms(out_own, 1, out_right_root))
    out_direction = here.transpose_chips(out_total[:, :out_cols].astype(BF16)).astype(F32)
    out_left_sum = out_total[:, out_cols:]

    fc_right_sum = dot_tn(fc_own, jnp.concatenate(far_columns(fc_own), axis=1))
    first_far = far_columns(first_own)
    qkv_right_sum = dot_tn(
        qkv_own, jnp.concatenate([part[:, :qkv_cols] for part in first_far], axis=1)
    )
    out_right_sum = dot_tn(
        out_own, jnp.concatenate([part[:, qkv_cols:] for part in first_far], axis=1)
    )

    def interleave(value, block):
        value = value.reshape(-1, 1, block)
        zeros = jnp.zeros_like(value)
        return jnp.concatenate(here.by_core(value, zeros), axis=1).reshape(-1)

    head_sums = interleave(jnp.sum(grad_heads.astype(F32), axis=0), HEAD_DIM)
    fc_bias_terms = lax.dynamic_update_slice_in_dim(
        jnp.zeros((hidden,), F32), jnp.sum(grad_pre.astype(F32), axis=0), (2 * q + c) * unit, 0
    )
    vector_terms = jnp.concatenate(
        [
            jnp.sum(grad_normed_one * own_scaled, axis=0),
            jnp.sum(grad_normed_one, axis=0),
            head_sums[:width],
            head_sums[2 * width :],
            jnp.sum(own_branch.astype(F32), axis=0),
            jnp.sum(grad_normed_two * scaled_two, axis=0),
            jnp.sum(grad_normed_two, axis=0),
            fc_bias_terms,
            jnp.sum(grad_top, axis=0),
        ]
    )
    vector_sum = here.swap_core(vector_terms) + vector_terms
    vector_sum = here.reduce_depth(vector_sum.reshape(-1, 128), F32)
    distance = 1
    while distance < plane:
        vector_sum = vector_sum + here.swap_plane(vector_sum, distance)
        distance *= 2
    vector_grad = vector_sum.reshape(-1) * factor

    results = []
    for grad, weight, moment, left, right, found, row_total, col_total in (
        (
            qkv_grad,
            qkv_weight,
            qkv_moment,
            qkv_left,
            qkv_right,
            (qkv_left_sum, qkv_right_sum, qkv_direction),
            width,
            3 * width,
        ),
        (
            out_grad,
            out_weight,
            out_moment,
            out_left,
            out_right,
            (out_left_sum, out_right_sum, out_direction),
            width,
            width,
        ),
        (
            fc_grad,
            fc_weight,
            fc_moment,
            fc_left,
            fc_right,
            (fc_left_sum, fc_right_sum, fc_direction),
            width,
            hidden,
        ),
        (
            proj_grad,
            proj_weight,
            proj_moment,
            proj_left,
            proj_right,
            (proj_left_sum, proj_right_sum, proj_direction),
            hidden,
            width,
        ),
    ):
        left_sum, right_sum, direction = found
        new_moment = MOMENTUM * moment + direction
        new_weight = weight - RATE * new_moment
        results += [
            grad,
            DECAY * left + (1.0 - DECAY) / col_total * left_sum,
            DECAY * right + (1.0 - DECAY) / row_total * right_sum,
            new_moment,
            new_weight,
            new_weight.astype(BF16),
        ]
    new_vector_moment = MOMENTUM * vector_moment + vector_grad
    new_vectors = vectors - RATE * new_vector_moment
    return (output, input_grad, *results, vector_grad, new_vector_moment, new_vectors)


def solution(mesh):
    groups, depth = mesh.shape["grp"], mesh.shape["in"]
    fine = Mesh(mesh.devices.reshape(groups // 4, 2, 2, depth), ALL)
    grp = ("y", "x", "c")
    tokens, cols, rows, flat = P(ALL, None), P("in", grp), P(grp, "in"), P("in")
    matrix_in = (cols, cols, cols, rows, cols, rows)
    matrix_out = (cols, cols, rows, cols, cols, cols)
    return jax.shard_map(
        on_device,
        mesh=fine,
        in_specs=(tokens, tokens, tokens, flat, flat) + matrix_in * 4,
        out_specs=(tokens, tokens) + matrix_out * 4 + (flat, flat, flat),
        check_vma=False,
    )
```

time: 2530 us -> 683 us (0.27)
  waiting for transfers between devices: 2110 us -> 296 us
  starting transfers between devices: 2.93 us -> 170 us
  matrix products: 186 us -> 45 us
  blocking collectives: 133 us -> 0 us
  Pallas kernels: 0 us -> 49.8 us
    reduce_scatter x20 -> x0, waiting for transfers between devices: 1570 us -> none  [the longest x1 284 us: on_device(): lax.psum_scatter(grad_fc, 'in', scatter_dimension=0, tiled=True)]
    all_gather x12 -> x1, waiting for transfers between devices: 360 us -> 0.01 us  [on_device(): lax.all_gather(jnp.stack([root.astype(BF16) for root in (qkv_left_root, o...]
    ppermute x0 -> x122, waiting for transfers between devices: none -> 296 us  [send(): value = lax.ppermute(value, axes, pairs)]
    psum x1 -> x0, waiting for transfers between devices: 179 us -> none  [on_device(): lax.psum((qkv_part, out_part, fc_part, proj_part, vector_part), 'grp')]
    ppermute x0 -> x122, starting transfers between devices: none -> 169 us  [send(): value = lax.ppermute(value, axes, pairs)]
    dot_general x34 -> x35, matrix products: 186 us -> 45 us  [the longest x13 20.4 us: dot_nt(): lax.dot_general(left, right, (((1,), (1,)), ((), ())), preferred_element_...]
    all_gather x5 -> x0, blocking collectives: 92.8 us -> none  [the longest x1 28.4 us: on_device(): lax.all_gather(copies[0], 'in', axis=0, tiled=True)]
    pallas_call x0 -> x13, Pallas kernels: none -> 49.8 us  [the longest x7 15.5 us: assemble(): pl.pallas_call(body, out_shape=jax.ShapeDtypeStruct(whole, pieces[0].dtyp...]
  transfers between devices with their start and end apart: 33 -> 123, of which waited for: 29 -> 61; matrix products, arithmetic and copies ran while one was open for 9% -> 19% of each run, Pallas kernels for 0% -> 7%
where the time goes in v1:
time: 683 us; the launch traced here: 674 us
  waiting for transfers between devices  296 us (43%)
  starting transfers between devices  170 us (25%)
  other arithmetic  52 us (8%)
  Pallas kernels  49.8 us (7%)
  matrix products  45 us (7%)
  local copies, waits for them, and re-layouts  44.7 us (7%)
  between operations  17.4 us (3%)
    ppermute x122, waiting for transfers between devices, send(): value = lax.ppermute(value, axes, pairs)  296 us
    ppermute x122, starting transfers between devices, send(): value = lax.ppermute(value, axes, pairs)  169 us
    unnamed x357, local copies, waits for them, and re-layouts  22 us
    dot_general x13, matrix products, dot_nt(): lax.dot_general(left, right, (((1,), (1,)), ((), ())), preferred_element_...  20.4 us
    pallas_call x7, Pallas kernels, assemble(): pl.pallas_call(body, out_shape=jax.ShapeDtypeStruct(whole, pieces[0].dtyp...  15.5 us
    dot_general x13, matrix products, dot_tn(): lax.dot_general(left, right, (((0,), (0,)), ((), ())), preferred_element_...  14.2 us
  transfers between devices with their start and end apart: 123, of which 61 were waited for; matrix products, arithmetic and copies ran while one was open for 19% of the time, Pallas kernels for 7%

profile of v1, /device:TPU:0, one launch (start us, length us, event | category | flops | bytes accessed | tf_op | source)
XLA Modules:
  0.0 673.9 jit_solution(5180493466081951483)
XLA Ops:
  30.2 7.6 %collective-permute-done.3.refs_2_ = bf16[256,384]{1,0:T(8,128)(2,1)S(1)} collective-permute-done((bf16[256,384]{1,0:T(8,128)(2,1)S(1)}, bf16[256,384]{1,0:T(8,128)(2,1)S(1)}, u32[]{:S(2)}, u32[]{:S(2)}) %collective-permute-start.3) | collective-permute-done | bytes 196640 | tf_op jit(solution)/shard_map/ppermute | solution.py:258
  38.0 8.8 %collective-permute-done.4.refs_3_ = bf16[256,384]{1,0:T(8,128)(2,1)S(1)} collective-permute-done((bf16[256,384]{1,0:T(8,128)(2,1)S(1)}, bf16[256,384]{1,0:T(8,128)(2,1)S(1)}, u32[]{:S(2)}, u32[]{:S(2)}) %collective-permute-start.4) | collective-permute-done | bytes 196640 | tf_op jit(solution)/shard_map/ppermute | solution.py:258
  77.4 6.9 %collective-permute-done.20.refs_3_ = bf16[128,256]{1,0:T(8,128)(2,1)} collective-permute-done((bf16[128,256]{1,0:T(8,128)(2,1)}, bf16[128,256]{1,0:T(8,128)(2,1)}, u32[]{:S(2)}, u32[]{:S(2)}) %collective-permute-start.20) | collective-permute-done | bytes 65568 | tf_op jit(solution)/shard_map/ppermute | solution.py:258
  88.1 7.6 %collective-permute-done.15 = bf16[512,384]{1,0:T(8,128)(2,1)S(1)} collective-permute-done((bf16[512,384]{1,0:T(8,128)(2,1)S(1)}, bf16[512,384]{1,0:T(8,128)(2,1)S(1)}, u32[]{:S(2)}, u32[]{:S(2)}) %collective-permute-start.15) | collective-permute-done | bytes 393248 | tf_op jit(solution)/shard_map/ppermute | solution.py:258
  108.0 7.1 %attention_forward.1 = bf16[256,512]{1,0:T(8,128)(2,1)} custom-call(bf16[256,1536]{1,0:T(8,128)(2,1)} %fusion.28.qkv_ref, f32[2,128,128]{2,1,0:T(8,128)} %and_select_fusion.bias_ref), custom_call_target="tpu_custom_call" | custom-call | tf_op jit(solution)/shard_map/attention_forward/pallas_call | solution.py:70
  123.4 8.9 %collective-permute-done.32.refs_2_ = bf16[256,512]{1,0:T(8,128)(2,1)S(1)} collective-permute-done((bf16[256,512]{1,0:T(8,128)(2,1)}, bf16[256,512]{1,0:T(8,128)(2,1)S(1)}, u32[]{:S(2)}, u32[]{:S(2)}) %collective-permute-start.32) | collective-permute-done | bytes 262176 | tf_op jit(solution)/shard_map/ppermute | solution.py:258
  156.2 10.9 %collective-permute-start.36 = (bf16[512,256]{1,0:T(8,128)(2,1)S(1)}, bf16[512,256]{1,0:T(8,128)(2,1)S(1)}, u32[]{:S(2)}, u32[]{:S(2)}) collective-permute-start(bf16[512,256]{1,0:T(8,128)(2,1)S(1)} %collective-permute-done.35.refs_0_), channel_id=1, source_target_pairs={{0,1},{1,2},{2,3},{3,0},{4,5},{5,6},{6,7},{7,4},{8,9},{9,10},{10,1... | collective-permute-start | bytes 786440 | tf_op jit(solution)/shard_map/ppermute | solution.py:258
  167.1 9.7 %collective-permute-done.36.refs_1_ = bf16[512,256]{1,0:T(8,128)(2,1)S(1)} collective-permute-done((bf16[512,256]{1,0:T(8,128)(2,1)S(1)}, bf16[512,256]{1,0:T(8,128)(2,1)S(1)}, u32[]{:S(2)}, u32[]{:S(2)}) %collective-permute-start.36) | collective-permute-done | bytes 262176 | tf_op jit(solution)/shard_map/ppermute | solution.py:258
  179.3 8.9 %collective-permute-done.37.refs_2_ = bf16[512,256]{1,0:T(8,128)(2,1)} collective-permute-done((bf16[512,256]{1,0:T(8,128)(2,1)S(1)}, bf16[512,256]{1,0:T(8,128)(2,1)}, u32[]{:S(2)}, u32[]{:S(2)}) %collective-permute-start.37) | collective-permute-done | bytes 262176 | tf_op jit(solution)/shard_map/ppermute | solution.py:258
  192.8 9.7 %collective-permute-done.38.refs_3_ = bf16[512,256]{1,0:T(8,128)(2,1)} collective-permute-done((bf16[512,256]{1,0:T(8,128)(2,1)}, bf16[512,256]{1,0:T(8,128)(2,1)}, u32[]{:S(2)}, u32[]{:S(2)}) %collective-permute-start.38) | collective-permute-done | bytes 262176 | tf_op jit(solution)/shard_map/ppermute | solution.py:258
  220.3 7.8 %collective-permute-done.52 = bf16[512,256]{1,0:T(8,128)(2,1)S(1)} collective-permute-done((bf16[512,256]{1,0:T(8,128)(2,1)S(1)}, bf16[512,256]{1,0:T(8,128)(2,1)S(1)}, u32[]{:S(2)}, u32[]{:S(2)}) %collective-permute-start.52) | collective-permute-done | bytes 262176 | tf_op jit(solution)/shard_map/ppermute | solution.py:258
  231.5 10.7 %collective-permute-done.53 = bf16[512,256]{1,0:T(8,128)(2,1)S(1)} collective-permute-done((bf16[512,256]{1,0:T(8,128)(2,1)S(1)}, bf16[512,256]{1,0:T(8,128)(2,1)S(1)}, u32[]{:S(2)}, u32[]{:S(2)}) %collective-permute-start.53) | collective-permute-done | bytes 262176 | tf_op jit(solution)/shard_map/ppermute | solution.py:258
  259.3 6.3 collective-permute-start.42
  311.1 9.5 %attention_backward.1 = bf16[256,1536]{1,0:T(8,128)(2,1)} custom-call(bf16[256,1536]{1,0:T(8,128)(2,1)} %fusion.28.qkv_ref, f32[2,128,128]{2,1,0:T(8,128)} %and_select_fusion.bias_ref, bf16[256,512]{1,0:T(8,128)(2,1)} %convolution_convert_fusion.4.grad_ref), custom_call_target="tpu_custom_call" | custom-call | tf_op jit(solution)/shard_map/attention_backward/pallas_call | solution.py:116
  352.5 10.4 %collective-permute-done.70.refs_1_ = bf16[256,512]{1,0:T(8,128)(2,1)S(1)} collective-permute-done((bf16[256,512]{1,0:T(8,128)(2,1)S(1)}, bf16[256,512]{1,0:T(8,128)(2,1)S(1)}, u32[]{:S(2)}, u32[]{:S(2)}) %collective-permute-start.70) | collective-permute-done | bytes 262176 | tf_op jit(solution)/shard_map/ppermute | solution.py:258
  363.3 9.8 %collective-permute-done.71.refs_2_ = bf16[256,512]{1,0:T(8,128)(2,1)S(1)} collective-permute-done((bf16[256,512]{1,0:T(8,128)(2,1)S(1)}, bf16[256,512]{1,0:T(8,128)(2,1)S(1)}, u32[]{:S(2)}, u32[]{:S(2)}) %collective-permute-start.71) | collective-permute-done | bytes 262176 | tf_op jit(solution)/shard_map/ppermute | solution.py:258
  373.9 8.6 %collective-permute-done.72.refs_3_ = bf16[256,512]{1,0:T(8,128)(2,1)S(1)} collective-permute-done((bf16[256,512]{1,0:T(8,128)(2,1)S(1)}, bf16[256,512]{1,0:T(8,128)(2,1)S(1)}, u32[]{:S(2)}, u32[]{:S(2)}) %collective-permute-start.72) | collective-permute-done | bytes 262176 | tf_op jit(solution)/shard_map/ppermute | solution.py:258
  383.3 7.8 %collective-permute-done.73 = bf16[256,512]{1,0:T(8,128)(2,1)S(1)} collective-permute-done((bf16[256,512]{1,0:T(8,128)(2,1)S(1)}, bf16[256,512]{1,0:T(8,128)(2,1)S(1)}, u32[]{:S(2)}, u32[]{:S(2)}) %collective-permute-start.73) | collective-permute-done | bytes 262176 | tf_op jit(solution)/shard_map/ppermute | solution.py:258
  392.5 7.0 %collective-permute-done.74 = bf16[256,512]{1,0:T(8,128)(2,1)S(1)} collective-permute-done((bf16[256,512]{1,0:T(8,128)(2,1)S(1)}, bf16[256,512]{1,0:T(8,128)(2,1)S(1)}, u32[]{:S(2)}, u32[]{:S(2)}) %collective-permute-start.74) | collective-permute-done | bytes 262176 | tf_op jit(solution)/shard_map/ppermute | solution.py:258
  442.7 6.3 collective-permute-done.82
  469.3 20.5 %collective-permute-start.89 = (bf16[256,512]{1,0:T(8,128)(2,1)S(1)}, bf16[256,512]{1,0:T(8,128)(2,1)}, u32[]{:S(2)}, u32[]{:S(2)}) collective-permute-start(bf16[256,512]{1,0:T(8,128)(2,1)S(1)} %pad_maximum_fusion.27.refs_0_), channel_id=1, source_target_pairs={{0,1},{1,2},{2,3},{3,0},{4,5},{5,6},{6,7},{7,4},{8,9},{9,10},{10,1... | collective-permute-start | bytes 786440 | tf_op jit(solution)/shard_map/ppermute | solution.py:258
  561.2 7.1 %collective-permute-done.103 = bf16[512,512]{1,0:T(8,128)(2,1)S(1)} collective-permute-done((bf16[512,512]{1,0:T(8,128)(2,1)S(1)}, bf16[512,512]{1,0:T(8,128)(2,1)S(1)}, u32[]{:S(2)}, u32[]{:S(2)}) %collective-permute-start.103) | collective-permute-done | bytes 524320 | tf_op jit(solution)/shard_map/ppermute | solution.py:258
  605.6 8.4 %collective-permute-done.105 = bf16[512,512]{1,0:T(8,128)(2,1)S(1)} collective-permute-done((bf16[512,512]{1,0:T(8,128)(2,1)S(1)}, bf16[512,512]{1,0:T(8,128)(2,1)S(1)}, u32[]{:S(2)}, u32[]{:S(2)}) %collective-permute-start.105) | collective-permute-done | bytes 524320 | tf_op jit(solution)/shard_map/ppermute | solution.py:258
  618.8 15.4 %collective-permute-start.117 = (f32[24,128]{1,0:T(8,128)S(1)}, f32[24,128]{1,0:T(8,128)S(1)}, u32[]{:S(2)}, u32[]{:S(2)}) collective-permute-start(f32[24,128]{1,0:T(8,128)S(1)} %constant_dynamic-slice_fusion), channel_id=1, source_target_pairs={{0,1},{1,2},{2,3},{3,0},{4,5},{5,6},{6,7},{7,4},{8,9},{9,10},{10,1... | collective-permute-start | bytes 36872 | tf_op jit(solution)/shard_map/ppermute | solution.py:258
  (831 shorter events, 434.9 us)
Async XLA Ops:
  7.3 395.3 %all-gather.3.cloned.1.call-start = ((), (), s32[]{:S(2)}) async-start(), calls=%async_computation | async-start | bytes 8650752 | tf_op jit(solution)/shard_map/all_gather | solution.py:479
  7.3 39.6 %collective-permute-start.8 = (bf16[128,1024]{1,0:T(8,128)(2,1)}, bf16[128,1024]{1,0:T(8,128)(2,1)S(1)}, u32[]{:S(2)}, u32[]{:S(2)}) collective-permute-start(bf16[128,1024]{1,0:T(8,128)(2,1)} %param.31), channel_id=1, source_target_pairs={{0,8},{8,0},{16,24},{24,16},{1,9},{9,1},{17,25},{25,17},{2,10},{10... | collective-permute-start | bytes 786440 | tf_op jit(solution)/shard_map/ppermute | solution.py:258
  10.3 36.6 %collective-permute-start.9 = (bf16[128,1024]{1,0:T(8,128)(2,1)}, bf16[128,1024]{1,0:T(8,128)(2,1)S(1)}, u32[]{:S(2)}, u32[]{:S(2)}) collective-permute-start(bf16[128,1024]{1,0:T(8,128)(2,1)} %param.31), channel_id=1, source_target_pairs={{0,16},{8,24},{16,0},{24,8},{1,17},{9,25},{17,1},{25,9},{2,18},{10... | collective-permute-start | bytes 786440 | tf_op jit(solution)/shard_map/ppermute | solution.py:258
  12.9 24.9 %collective-permute-start = (bf16[128,1024]{1,0:T(8,128)(2,1)}, bf16[128,1024]{1,0:T(8,128)(2,1)S(1)}, u32[]{:S(2)}, u32[]{:S(2)}) collective-permute-start(bf16[128,1024]{1,0:T(8,128)(2,1)} %param.29), channel_id=1, source_target_pairs={{0,4},{4,0},{1,5},{5,1},{2,6},{6,2},{3,7},{7,3},{8,12},{12,8},{9,1... | collective-permute-start | bytes 786440 | tf_op jit(solution)/shard_map/ppermute | solution.py:258
  37.7 80.9 %collective-permute-start.34 = (bf16[512,128]{1,0:T(8,128)(2,1)}, bf16[512,128]{1,0:T(8,128)(2,1)}, u32[]{:S(2)}, u32[]{:S(2)}) collective-permute-start(bf16[512,128]{1,0:T(8,128)(2,1)} %broadcast_select_fusion.57), channel_id=1, source_target_pairs={{0,4},{4,0},{1,5},{5,1},{2,6},{6,2},{3,7},{7,3},{8,12},{12,8},{9,1... | collective-permute-start | bytes 393224 | tf_op jit(solution)/shard_map/ppermute | solution.py:258
  60.8 25.2 %collective-permute-start.11 = (bf16[1024,384]{1,0:T(8,128)(2,1)}, bf16[1024,384]{1,0:T(8,128)(2,1)S(1)}, u32[]{:S(2)}, u32[]{:S(2)}) collective-permute-start(bf16[1024,384]{1,0:T(8,128)(2,1)} %assemble.7), channel_id=1, source_target_pairs={{0,16},{8,24},{16,0},{24,8},{1,17},{9,25},{17,1},{25,9},{2,18},{10... | collective-permute-start | bytes 2359304 | tf_op jit(solution)/shard_map/ppermute | solution.py:258
  61.4 24.6 %collective-permute-start.13 = (bf16[1024,384]{1,0:T(8,128)(2,1)}, bf16[1024,384]{1,0:T(8,128)(2,1)S(1)}, u32[]{:S(2)}, u32[]{:S(2)}) collective-permute-start(bf16[1024,384]{1,0:T(8,128)(2,1)} %assemble.7), channel_id=1, source_target_pairs={{0,8},{8,0},{16,24},{24,16},{1,9},{9,1},{17,25},{25,17},{2,10},{10... | collective-permute-start | bytes 2359304 | tf_op jit(solution)/shard_map/ppermute | solution.py:258
  84.3 37.6 %collective-permute-start.31 = (bf16[256,512]{1,0:T(8,128)(2,1)}, bf16[256,512]{1,0:T(8,128)(2,1)}, u32[]{:S(2)}, u32[]{:S(2)}) collective-permute-start(bf16[256,512]{1,0:T(8,128)(2,1)} %convert_element_type.297.refs_0_), channel_id=1, source_target_pairs={{0,1},{1,2},{2,3},{3,0},{4,5},{5,6},{6,7},{7,4},{8,9},{9,10},{10,1... | collective-permute-start | bytes 786440 | tf_op jit(solution)/shard_map/ppermute | solution.py:258
  138.6 50.9 %collective-permute-start.40 = (bf16[512,1024]{1,0:T(8,128)(2,1)}, bf16[512,1024]{1,0:T(8,128)(2,1)S(1)}, u32[]{:S(2)}, u32[]{:S(2)}) collective-permute-start(bf16[512,1024]{1,0:T(8,128)(2,1)} %get-tuple-element.386), channel_id=1, source_target_pairs={{0,4},{4,0},{1,5},{5,1},{2,6},{6,2},{3,7},{7,3},{8,12},{12,8},{9,1... | collective-permute-start | bytes 3145736 | tf_op jit(solution)/shard_map/ppermute | solution.py:258
  154.1 50.7 %collective-permute-start.30 = (bf16[512,1024]{1,0:T(8,128)(2,1)}, bf16[512,1024]{1,0:T(8,128)(2,1)}, u32[]{:S(2)}, u32[]{:S(2)}) collective-permute-start(bf16[512,1024]{1,0:T(8,128)(2,1)} %get-tuple-element.390), channel_id=1, source_target_pairs={{0,4},{4,0},{1,5},{5,1},{2,6},{6,2},{3,7},{7,3},{8,12},{12,8},{9,1... | collective-permute-start | bytes 3145736 | tf_op jit(solution)/shard_map/ppermute | solution.py:258
  156.2 20.7 %collective-permute-start.36 = (bf16[512,256]{1,0:T(8,128)(2,1)S(1)}, bf16[512,256]{1,0:T(8,128)(2,1)S(1)}, u32[]{:S(2)}, u32[]{:S(2)}) collective-permute-start(bf16[512,256]{1,0:T(8,128)(2,1)S(1)} %collective-permute-done.35.refs_0_), channel_id=1, source_target_pairs={{0,1},{1,2},{2,3},{3,0},{4,5},{5,6},{6,7},{7,4},{8,9},{9,10},{10,1... | collective-permute-start | bytes 786440 | tf_op jit(solution)/shard_map/ppermute | solution.py:258
  220.3 36.7 %collective-permute-start.41 = (bf16[512,1024]{1,0:T(8,128)(2,1)}, bf16[512,1024]{1,0:T(8,128)(2,1)}, u32[]{:S(2)}, u32[]{:S(2)}) collective-permute-start(bf16[512,1024]{1,0:T(8,128)(2,1)} %convolution_convert_fusion), channel_id=1, source_target_pairs={{0,4},{4,0},{1,5},{5,1},{2,6},{6,2},{3,7},{7,3},{8,12},{12,8},{9,1... | collective-permute-start | bytes 3145736 | tf_op jit(solution)/shard_map/ppermute | solution.py:258
  231.5 34.0 %collective-permute-start.39 = (bf16[512,1024]{1,0:T(8,128)(2,1)}, bf16[512,1024]{1,0:T(8,128)(2,1)}, u32[]{:S(2)}, u32[]{:S(2)}) collective-permute-start(bf16[512,1024]{1,0:T(8,128)(2,1)} %convolution_convert_fusion.1), channel_id=1, source_target_pairs={{0,4},{4,0},{1,5},{5,1},{2,6},{6,2},{3,7},{7,3},{8,12},{12,8},{9,1... | collective-permute-start | bytes 3145736 | tf_op jit(solution)/shard_map/ppermute | solution.py:258
  299.7 24.9 %collective-permute-start.60 = (bf16[512,256]{1,0:T(8,128)(2,1)S(1)}, bf16[512,256]{1,0:T(8,128)(2,1)S(1)}, u32[]{:S(2)}, u32[]{:S(2)}) collective-permute-start(bf16[512,256]{1,0:T(8,128)(2,1)S(1)} %collective-permute-done.58), channel_id=1, source_target_pairs={{0,16},{8,24},{16,0},{24,8},{1,17},{9,25},{17,1},{25,9},{2,18},{10... | collective-permute-start | bytes 786440 | tf_op jit(solution)/shard_map/ppermute | solution.py:258
  304.7 19.9 %collective-permute-start.59 = (bf16[512,256]{1,0:T(8,128)(2,1)S(1)}, bf16[512,256]{1,0:T(8,128)(2,1)S(1)}, u32[]{:S(2)}, u32[]{:S(2)}) collective-permute-start(bf16[512,256]{1,0:T(8,128)(2,1)S(1)} %collective-permute-done.58), channel_id=1, source_target_pairs={{0,8},{8,0},{16,24},{24,16},{1,9},{9,1},{17,25},{25,17},{2,10},{10... | collective-permute-start | bytes 786440 | tf_op jit(solution)/shard_map/ppermute | solution.py:258
  308.7 23.4 %collective-permute-start.67 = (bf16[512,256]{1,0:T(8,128)(2,1)S(1)}, bf16[512,256]{1,0:T(8,128)(2,1)}, u32[]{:S(2)}, u32[]{:S(2)}) collective-permute-start(bf16[512,256]{1,0:T(8,128)(2,1)S(1)} %multiply_convert_fusion.refs_0_), channel_id=1, source_target_pairs={{0,1},{1,2},{2,3},{3,0},{4,5},{5,6},{6,7},{7,4},{8,9},{9,10},{10,1... | collective-permute-start | bytes 786440 | tf_op jit(solution)/shard_map/ppermute | solution.py:258
  347.8 25.3 %collective-permute-start.66 = (bf16[1024,512]{1,0:T(8,128)(2,1)S(1)}, bf16[1024,512]{1,0:T(8,128)(2,1)S(1)}, u32[]{:S(2)}, u32[]{:S(2)}) collective-permute-start(bf16[1024,512]{1,0:T(8,128)(2,1)S(1)} %pad_maximum_fusion.4), channel_id=1, source_target_pairs={{0,16},{8,24},{16,0},{24,8},{1,17},{9,25},{17,1},{25,9},{2,18},{10... | collective-permute-start | bytes 3145736 | tf_op jit(solution)/shard_map/ppermute | solution.py:258
  348.6 24.5 %collective-permute-start.65 = (bf16[1024,512]{1,0:T(8,128)(2,1)S(1)}, bf16[1024,512]{1,0:T(8,128)(2,1)S(1)}, u32[]{:S(2)}, u32[]{:S(2)}) collective-permute-start(bf16[1024,512]{1,0:T(8,128)(2,1)S(1)} %pad_maximum_fusion.3), channel_id=1, source_target_pairs={{0,8},{8,0},{16,24},{24,16},{1,9},{9,1},{17,25},{25,17},{2,10},{10... | collective-permute-start | bytes 3145736 | tf_op jit(solution)/shard_map/ppermute | solution.py:258
  400.1 126.7 %collective-permute-start.51 = (f32[128,1024]{1,0:T(8,128)}, f32[128,1024]{1,0:T(8,128)}, u32[]{:S(2)}, u32[]{:S(2)}) collective-permute-start(f32[128,1024]{1,0:T(8,128)} %fusion.41), channel_id=1, source_target_pairs={{0,4},{4,0},{1,5},{5,1},{2,6},{6,2},{3,7},{7,3},{8,12},{12,8},{9,1... | collective-permute-start | bytes 1572872 | tf_op jit(solution)/shard_map/ppermute | solution.py:258
  410.9 19.1 %collective-permute-start.79 = (bf16[5120,128]{1,0:T(8,128)(2,1)}, bf16[5120,128]{1,0:T(8,128)(2,1)}, u32[]{:S(2)}, u32[]{:S(2)}) collective-permute-start(bf16[5120,128]{1,0:T(8,128)(2,1)} %get-tuple-element.197), channel_id=1, source_target_pairs={{0,4},{4,0},{1,5},{5,1},{2,6},{6,2},{3,7},{7,3},{8,12},{12,8},{9,1... | collective-permute-start | bytes 3932168 | tf_op jit(solution)/shard_map/ppermute | solution.py:258
  422.8 28.3 %collective-permute-start.76 = (f32[256,6,1,64]{0,3,2,1:T(8,128)}, f32[256,6,1,64]{0,3,2,1:T(8,128)S(1)}, u32[]{:S(2)}, u32[]{:S(2)}) collective-permute-start(f32[256,6,1,64]{0,3,2,1:T(8,128)} %bitcast.122), channel_id=1, source_target_pairs={{0,4},{4,0},{1,5},{5,1},{2,6},{6,2},{3,7},{7,3},{8,12},{12,8},{9,1... | collective-permute-start | bytes 1179656 | tf_op jit(solution)/shard_map/ppermute | solution.py:258
  469.3 26.9 %collective-permute-start.89 = (bf16[256,512]{1,0:T(8,128)(2,1)S(1)}, bf16[256,512]{1,0:T(8,128)(2,1)}, u32[]{:S(2)}, u32[]{:S(2)}) collective-permute-start(bf16[256,512]{1,0:T(8,128)(2,1)S(1)} %pad_maximum_fusion.27.refs_0_), channel_id=1, source_target_pairs={{0,1},{1,2},{2,3},{3,0},{4,5},{5,6},{6,7},{7,4},{8,9},{9,10},{10,1... | collective-permute-start | bytes 786440 | tf_op jit(solution)/shard_map/ppermute | solution.py:258
  510.6 59.4 %collective-permute-start.115 = (bf16[512,1024]{1,0:T(8,128)(2,1)}, bf16[512,1024]{1,0:T(8,128)(2,1)}, u32[]{:S(2)}, u32[]{:S(2)}) collective-permute-start(bf16[512,1024]{1,0:T(8,128)(2,1)} %pad_maximum_fusion.7), channel_id=1, source_target_pairs={{0,4},{4,0},{1,5},{5,1},{2,6},{6,2},{3,7},{7,3},{8,12},{12,8},{9,1... | collective-permute-start | bytes 3145736 | tf_op jit(solution)/shard_map/ppermute | solution.py:258
  614.1 20.0 %collective-permute-start.107 = (bf16[512,512]{1,0:T(8,128)(2,1)S(1)}, bf16[512,512]{1,0:T(8,128)(2,1)S(1)}, u32[]{:S(2)}, u32[]{:S(2)}) collective-permute-start(bf16[512,512]{1,0:T(8,128)(2,1)S(1)} %get-tuple-element.227), channel_id=1, source_target_pairs={{0,16},{9,25},{18,2},{27,11},{4,20},{13,29},{22,6},{31,15}} | collective-permute-start | bytes 1572872 | tf_op jit(solution)/shard_map/ppermute | solution.py:258
  (265 other events, 2926.8 us)
Sparse Core Ops, SparseCore 0:
  156.3 95.9 all-gather.2

commit v2 on v1

v2 whole, which is shorter than its diff:
```python
import math

import jax
import jax.numpy as jnp
import numpy as np
from jax import lax
from jax.experimental import pallas as pl
from jax.experimental.pallas import tpu as pltpu
from jax.sharding import Mesh
from jax.sharding import PartitionSpec as P

HEADS = 16
HEAD_DIM = 64
EPSILON = 1e-05
DECAY = 0.5
MOMENTUM = 0.5
RATE = 0.03
MASKED = -1e30
ROOT_TWO_PI = math.sqrt(2.0 / math.pi)
BF16 = jnp.bfloat16
F32 = jnp.float32
PLANE = ("y", "x")
CHIPS = ("y", "x", "in")
ALL = ("y", "x", "c", "in")


def dot(left, right):
    return jnp.dot(left, right, preferred_element_type=F32)


def dot_tn(left, right):
    return lax.dot_general(left, right, (((0,), (0,)), ((), ())), preferred_element_type=F32)


def dot_nt(left, right):
    return lax.dot_general(left, right, (((1,), (1,)), ((), ())), preferred_element_type=F32)


def lane_half(shape, half):
    return (lax.broadcasted_iota(jnp.int32, shape, 1) // HEAD_DIM) == half


def softmax_rows(scores):
    shifted = jnp.exp(scores - jnp.max(scores, axis=-1, keepdims=True))
    return shifted / jnp.sum(shifted, axis=-1, keepdims=True)


def attention_forward(qkv, bias):
    sequences, length, _ = bias.shape
    width = qkv.shape[1] // 3
    pair = 2 * HEAD_DIM
    scale = HEAD_DIM ** (-0.5)

    def body(qkv_ref, bias_ref, out_ref):
        for seq in range(sequences):
            rows = slice(seq * length, (seq + 1) * length)
            mask = bias_ref[seq]
            for col in range(0, width, pair):
                queries = qkv_ref[rows, col : col + pair]
                key_rows = qkv_ref[rows, width + col : width + col + pair]
                value_rows = qkv_ref[rows, 2 * width + col : 2 * width + col + pair]
                parts = []
                for half in range(2):
                    own = jnp.where(lane_half(queries.shape, half), queries, jnp.zeros_like(queries))
                    probs = softmax_rows(dot_nt(own, key_rows) * scale + mask)
                    parts.append(dot(probs.astype(BF16), value_rows))
                picked = jnp.where(lane_half(parts[0].shape, 0), parts[0], parts[1])
                out_ref[rows, col : col + pair] = picked.astype(BF16)

    return pl.pallas_call(
        body,
        out_shape=jax.ShapeDtypeStruct((qkv.shape[0], width), BF16),
        in_specs=[pl.BlockSpec(memory_space=pltpu.VMEM)] * 2,
        out_specs=pl.BlockSpec(memory_space=pltpu.VMEM),
        name="attention_forward",
    )(qkv, bias)


def attention_backward(qkv, bias, grad):
    sequences, length, _ = bias.shape
    width = qkv.shape[1] // 3
    pair = 2 * HEAD_DIM
    scale = HEAD_DIM ** (-0.5)

    def body(qkv_ref, bias_ref, grad_ref, out_ref):
        for seq in range(sequences):
            rows = slice(seq * length, (seq + 1) * length)
            mask = bias_ref[seq]
            for col in range(0, width, pair):
                queries = qkv_ref[rows, col : col + pair]
                key_rows = qkv_ref[rows, width + col : width + col + pair]
                value_rows = qkv_ref[rows, 2 * width + col : 2 * width + col + pair]
                grads = grad_ref[rows, col : col + pair]
                found = []
                for half in range(2):
                    lanes = lane_half(queries.shape, half)
                    own = jnp.where(lanes, queries, jnp.zeros_like(queries))
                    probs = softmax_rows(dot_nt(own, key_rows) * scale + mask)
                    own_grad = jnp.where(lanes, grads, jnp.zeros_like(grads))
                    grad_probs = dot_nt(own_grad, value_rows)
                    row_dot = jnp.sum(probs * grad_probs, axis=-1, keepdims=True)
                    grad_scores = (probs * (grad_probs - row_dot)).astype(BF16)
                    found.append(
                        (
                            dot(grad_scores, key_rows) * scale,
                            dot_tn(grad_scores, queries) * scale,
                            dot_tn(probs.astype(BF16), grads),
                        )
                    )
                low_lanes = lane_half((length, pair), 0)
                for third in range(3):
                    picked = jnp.where(low_lanes, found[0][third], found[1][third])
                    start = third * width + col
                    out_ref[rows, start : start + pair] = picked.astype(BF16)

    return pl.pallas_call(
        body,
        out_shape=jax.ShapeDtypeStruct(qkv.shape, BF16),
        in_specs=[pl.BlockSpec(memory_space=pltpu.VMEM)] * 3,
        out_specs=pl.BlockSpec(memory_space=pltpu.VMEM),
        name="attention_backward",
    )(qkv, bias, grad)


def whole(array):
    return pl.BlockSpec(array.shape, lambda step: (0,) * len(array.shape))


def join(pieces):
    rows, cols = pieces[0].shape

    def body(*refs):
        for k in range(len(pieces)):
            refs[-1][k * rows : (k + 1) * rows, :] = refs[k][...]

    in_vmem = pl.BlockSpec(memory_space=pltpu.VMEM)
    return pl.pallas_call(
        body,
        out_shape=jax.ShapeDtypeStruct((len(pieces) * rows, cols), pieces[0].dtype),
        in_specs=[in_vmem] * len(pieces),
        out_specs=in_vmem,
        name="join",
    )(*pieces)


def first_kernel(normed, heads, attended, branch, numbers, distances, dtype):
    width, chips = normed.shape[1], numbers.shape[0] - 2
    cols, pair = heads.shape[1] // chips, branch.shape[1] // chips
    rows, share = width // chips, pair // 2
    tall = attended.shape[1] // chips

    def body(number_ref, normed_ref, heads_ref, attended_ref, branch_ref, *targets):
        for d, target in zip(distances, targets):
            chip = number_ref[2 + d]
            head = heads_ref[:, pl.ds(pl.multiple_of(chip * cols, cols), cols)]
            target[:, :cols] = dot_tn(normed_ref[...], head).astype(dtype)
            term = branch_ref[:, pl.ds(pl.multiple_of(chip * pair, pair), pair)]
            term = dot_tn(attended_ref[...], term).astype(dtype)
            for k in range(chips):
                for half in range(2):
                    start = k * rows + half * tall
                    target[start : start + tall, cols:] = term[
                        k * tall : (k + 1) * tall, half * share : (half + 1) * share
                    ]

    in_vmem = pl.BlockSpec(memory_space=pltpu.VMEM)
    return pl.pallas_call(
        body,
        out_shape=[jax.ShapeDtypeStruct((width, cols + share), dtype)] * len(distances),
        in_specs=[pl.BlockSpec(memory_space=pltpu.SMEM)] + [in_vmem] * 4,
        out_specs=[in_vmem] * len(distances),
        name="first_terms",
    )(numbers, normed, heads, attended, branch)


def column_kernel(own, blocks, parts, numbers):
    width = own.shape[0]
    count, _, rows, share = blocks.shape
    chunks = width // rows
    sizes = [root.shape[0] for _, root in parts]
    total = sum(sizes)
    used = len(parts)

    def body(number_ref, own_ref, *refs):
        block_refs, right_refs = refs[:used], refs[used : 2 * used]
        mine_ref, theirs_ref, left_ref = refs[2 * used :]
        core, depth = number_ref[0], number_ref[1]
        near = pl.ds(pl.multiple_of(depth * rows, rows), rows)

        @pl.loop(0, chunks)
        def _(d):
            chunk = number_ref[2 + d]
            span = pl.ds(pl.multiple_of(d * rows, rows), rows)
            first = 0
            for k, cols in enumerate(sizes):
                lanes = slice(first, first + cols)
                for g in range(count // chunks):
                    left_ref[:, g * share : (g + 1) * share] = block_refs[k][g * chunks + chunk, 0]
                image = dot(left_ref[...], own_ref[:, lanes]).astype(BF16)
                for pick, target in ((core, mine_ref), (1 - core, theirs_ref)):
                    right = right_refs[k][:, pl.ds(pl.multiple_of(pick * cols, cols), cols)]
                    target[span, lanes] = dot(image, right.astype(BF16)).astype(target.dtype)
                    start = pl.multiple_of(chunk * rows + pick * share, share)
                    left = dot_nt(own_ref[near, lanes], own_ref[pl.ds(start, share), lanes])
                    low = total + k * share
                    target[span, low : low + share] = left.astype(target.dtype)
                first += cols

    shape = (width, total + used * share)
    return pl.pallas_call(
        body,
        grid=(1,),
        out_shape=(jax.ShapeDtypeStruct(shape, F32), jax.ShapeDtypeStruct(shape, BF16)),
        in_specs=[pl.BlockSpec(memory_space=pltpu.SMEM), whole(own)]
        + [
            pl.BlockSpec((count, 1, rows, share), lambda step, which=which: (0, which, 0, 0))
            for which, _ in parts
        ]
        + [whole(root) for _, root in parts],
        out_specs=(pl.BlockSpec(shape, lambda step: (0, 0)),) * 2,
        scratch_shapes=[pltpu.VMEM((rows, width), BF16)],
        compiler_params=pltpu.CompilerParams(vmem_limit_bytes=40 << 20),
        name="column_terms",
    )(numbers, own, *[blocks] * used, *[root for _, root in parts])


def row_kernel(own, blocks, which, left_root, numbers):
    width, count = own.shape
    devices, _, rows, share = blocks.shape
    chunks = width // rows
    tall = left_root.shape[0]
    piece = tall + 2 * share

    def body(number_ref, own_ref, block_ref, left_ref, mine_ref, theirs_ref, right_ref):
        core, depth = number_ref[0], number_ref[1]
        targets = ((core, mine_ref), (1 - core, theirs_ref))
        near = own_ref[pl.ds(pl.multiple_of(depth * rows, rows), rows), :]
        for d in range(chunks):
            chunk = number_ref[2 + d]
            for k, (pick, target) in enumerate(targets):
                part = pl.ds(pl.multiple_of(pick * share, share), share)
                lanes = slice((k * chunks + d) * share, (k * chunks + d + 1) * share)
                for g in range(devices // chunks):
                    right_ref[g * share : (g + 1) * share, lanes] = block_ref[
                        g * chunks + chunk, 0, part, :
                    ]
                start = pl.multiple_of(chunk * rows + pick * share, share)
                right = dot_nt(own_ref[pl.ds(start, share), :], near).astype(target.dtype)
                low = d * piece + tall
                target[low : low + share, :] = right[:, :share]
                target[low + share : low + 2 * share, :] = right[:, share:]
        for first in range(0, tall, rows):
            image = dot_nt(left_ref[first : first + rows, :].astype(BF16), own_ref[...])
            ahead = dot(image.astype(BF16), right_ref[...])
            for k, (_, target) in enumerate(targets):
                for d in range(chunks):
                    lanes = slice((k * chunks + d) * share, (k * chunks + d + 1) * share)
                    low = d * piece + first
                    target[low : low + rows, :] = ahead[:, lanes].astype(target.dtype)

    shape = (chunks * piece, share)
    return pl.pallas_call(
        body,
        grid=(1,),
        out_shape=(jax.ShapeDtypeStruct(shape, F32), jax.ShapeDtypeStruct(shape, BF16)),
        in_specs=[
            pl.BlockSpec(memory_space=pltpu.SMEM),
            whole(own),
            pl.BlockSpec((devices, 1, rows, share), lambda step: (0, which, 0, 0)),
            whole(left_root),
        ],
        out_specs=(pl.BlockSpec(shape, lambda step: (0, 0)),) * 2,
        scratch_shapes=[pltpu.VMEM((width, width), BF16)],
        compiler_params=pltpu.CompilerParams(vmem_limit_bytes=40 << 20),
        name="row_terms",
    )(numbers, own, blocks, left_root)


class Place:
    def __init__(self):
        self.rows = lax.axis_size("y")
        self.plane = self.rows * lax.axis_size("x")
        self.depth = lax.axis_size("in")
        self.q = lax.axis_index("y") * lax.axis_size("x") + lax.axis_index("x")
        self.c = lax.axis_index("c")
        self.z = lax.axis_index("in")
        self.last = {}

    def send(self, values, axes, pairs, lane=None):
        if lane in self.last:
            values, _ = lax.optimization_barrier((values, self.last[lane]))
        values = [lax.ppermute(value, axes, pair) for value, pair in zip(values, pairs)]
        if lane is not None:
            self.last[lane] = values
        return values

    def after(self, value, *earlier):
        return lax.optimization_barrier((value, *earlier))[0]

    def all_after(self, values, *earlier):
        return lax.optimization_barrier((tuple(values), *earlier))[0]

    def swap_core(self, value):
        return self.send([value], "c", [[(0, 1), (1, 0)]])[0]

    def swap_plane(self, values, distances, lane="plane"):
        pairs = [[(k, k ^ d) for k in range(self.plane)] for d in distances]
        return self.send(values, PLANE, pairs, lane)

    def on_depth(self, value):
        if "depth" in self.last:
            value, _ = lax.optimization_barrier((value, self.last["depth"]))
        value = lax.all_to_all(value, "in", 0, 0, tiled=True)
        self.last["depth"] = value
        return value

    def on_chips(self, values, targets, lane):
        pairs = []
        for target in targets:
            found = [
                (q, z, target(q, z))
                for q in range(self.plane)
                for z in range(self.depth)
                if target(q, z) is not None
            ]
            pairs.append([(q * self.depth + z, t[0] * self.depth + t[1]) for q, z, t in found])
        return self.send(values, CHIPS, pairs, lane)

    def by_core(self, own, other):
        return jnp.where(self.c == 0, own, other), jnp.where(self.c == 0, other, own)

    def mine(self, pair):
        return jnp.where(self.c == 0, pair[0], pair[1])

    def theirs(self, pair):
        return jnp.where(self.c == 0, pair[1], pair[0])

    def shuffle(self, values, index):
        values = list(values)
        bit = 1
        while bit < len(values):
            on = (index // bit) % 2 == 1
            values = [jnp.where(on, values[k ^ bit], values[k]) for k in range(len(values))]
            bit *= 2
        return values

    def gather_depth(self, value):
        return self.on_depth(jnp.broadcast_to(value[None], (self.depth,) + value.shape))

    def transpose_chips(self, value, lane):
        return self.on_chips([value], [lambda q, z: (z, q)], lane)[0]

    def spread_plane(self, value):
        q, z = self.q, self.z
        if self.plane != 4:
            total = jnp.where(q == z, value, jnp.zeros_like(value))
            targets = [
                lambda a, b, d=d: (a ^ d, b) if a == b else None for d in range(1, self.plane)
            ]
            for part in self.on_chips([value] * len(targets), targets, "plane"):
                total = total + part
            return total
        half = value.shape[0] // 2
        low, high = value[:half], value[half:]
        low_x, high_y = self.on_chips(
            [low, high],
            [
                lambda a, b: (a ^ 1, b) if a == b else None,
                lambda a, b: (a ^ 2, b) if a == b else None,
            ],
            "plane",
        )
        high_x, low_y = self.on_chips(
            [jnp.where(q == z, high, high_y), jnp.where(q == z, low, low_x)],
            [
                lambda a, b: (a ^ 1, b) if a ^ b in (0, 2) else None,
                lambda a, b: (a ^ 2, b) if a ^ b in (0, 1) else None,
            ],
            "plane",
        )
        apart = q ^ z
        low = jnp.where(apart == 0, low, jnp.where(apart == 1, low_x, low_y))
        high = jnp.where(apart == 0, high, jnp.where(apart == 2, high_y, high_x))
        return jnp.concatenate([low, high])

    def gather_tokens(self, value):
        mine = self.gather_plane(value)
        return join(mine + [self.swap_core(part) for part in mine])

    def reduce_tokens(self, mine, theirs):
        total = mine + self.swap_core(theirs.astype(BF16)).astype(F32)
        return self.reduce_plane(jnp.split(total, self.plane))

    def by_two_steps(self, shape):
        return self.plane == 4 and math.prod(shape) > 200_000

    def gather_plane(self, value):
        if not self.by_two_steps(value.shape):
            others = range(1, self.plane)
            return [value] + self.swap_plane([value] * len(others), others)
        half = value.shape[0] // 2
        by_x, by_y = self.swap_plane([value, value], (1, 2))
        first, second = self.swap_plane([by_y[:half], by_x[half:]], (1, 2))
        return [value, by_x, by_y, jnp.concatenate([first, second])]

    def reduce_plane(self, values):
        total = values[0]
        others = [value.astype(BF16) for value in values[1:]]
        for part in self.swap_plane(others, range(1, self.plane)):
            total = total + part.astype(F32)
        return total

    def reduce_plane_late(self, far, rest):
        if self.plane != 4:
            return self.reduce_plane([*rest(), far])
        half = far.shape[0] // 2
        first, second = self.swap_plane([far[:half], far[half:]], (1, 2))
        own, to_x, to_y = rest()
        to_y = jnp.concatenate([to_y[:half] + first.astype(F32), to_y[half:]])
        to_x = jnp.concatenate([to_x[:half], to_x[half:] + second.astype(F32)])
        by_x, by_y = self.swap_plane([to_x.astype(BF16), to_y.astype(BF16)], (1, 2))
        return own + by_x.astype(F32) + by_y.astype(F32)


def norm_parts(values):
    centred = values - jnp.mean(values, axis=-1, keepdims=True)
    spread = lax.rsqrt(jnp.mean(centred * centred, axis=-1, keepdims=True) + EPSILON)
    return centred * spread, spread


def norm_backward(grad, scaled, spread, gain):
    inner = grad * gain
    mean_one = jnp.mean(inner, axis=-1, keepdims=True)
    mean_two = jnp.mean(inner * scaled, axis=-1, keepdims=True)
    return spread * (inner - mean_one - scaled * mean_two)


def gelu(values):
    return 0.5 * values * (1.0 + jnp.tanh(ROOT_TWO_PI * (values + 0.044715 * values**3)))


def gelu_slope(values):
    squared = values * values
    bent = jnp.tanh(ROOT_TWO_PI * (values + 0.044715 * squared * values))
    return 0.5 * (1.0 + bent) + 0.5 * values * (1.0 - bent * bent) * (
        ROOT_TWO_PI * (1.0 + 3.0 * 0.044715 * squared)
    )


def on_device(
    tokens,
    segments,
    cotangent,
    vectors,
    vector_moment,
    qkv_weight,
    qkv_moment,
    qkv_left,
    qkv_right,
    qkv_left_root,
    qkv_right_root,
    out_weight,
    out_moment,
    out_left,
    out_right,
    out_left_root,
    out_right_root,
    fc_weight,
    fc_moment,
    fc_left,
    fc_right,
    fc_left_root,
    fc_right_root,
    proj_weight,
    proj_moment,
    proj_left,
    proj_right,
    proj_left_root,
    proj_right_root,
):
    here = Place()
    plane, depth = here.plane, here.depth
    length, width = tokens.shape
    z, q, c = here.z, here.q, here.c
    block = 2 * HEAD_DIM if qkv_weight.shape[1] % (2 * HEAD_DIM) == 0 else HEAD_DIM

    def far_columns(own):
        far = here.spread_plane(own)
        return here.by_core(far, here.swap_core(far))

    def pair_columns(share):
        return jnp.concatenate(here.by_core(share, here.swap_core(share)), axis=1)

    def by_parity(pair):
        parts = jnp.split(pair, pair.shape[1] // block, axis=1)
        return jnp.concatenate([here.mine(parts[k : k + 2]) for k in range(0, len(parts), 2)], axis=1)

    qkv_share = by_parity(pair_columns(qkv_weight.astype(BF16)))
    fc_share = fc_weight.astype(BF16)
    proj_split = proj_weight.astype(BF16).reshape(2, -1, proj_weight.shape[1])
    proj_share = jnp.concatenate(
        here.by_core(here.mine(proj_split), here.swap_core(here.theirs(proj_split))), axis=1
    )
    out_split = out_weight.astype(BF16).reshape(-1, 2, block, out_weight.shape[1])
    out_split = (
        out_split[:, 0].reshape(-1, out_weight.shape[1]),
        out_split[:, 1].reshape(-1, out_weight.shape[1]),
    )
    out_share = jnp.concatenate(
        here.by_core(here.mine(out_split), here.swap_core(here.theirs(out_split))), axis=1
    )

    proj_turned = here.transpose_chips(proj_share.T, "plane")
    plane_cotangent = here.gather_tokens(cotangent)
    qkv_parts = here.gather_plane(here.gather_depth(qkv_share).reshape(width, -1))
    small_share = jnp.concatenate(
        [out_share, vectors.astype(BF16).reshape(-1, out_share.shape[1])]
    )
    small_whole = here.gather_depth(small_share)
    vector_whole = small_whole[:, out_share.shape[0] :].reshape(-1)
    out_rows = small_whole[:, : out_share.shape[0]].reshape(-1, out_share.shape[1])
    out_full = jnp.concatenate(here.shuffle(here.gather_plane(out_rows), q), axis=1)
    fc_full = here.gather_depth(fc_share).reshape(width, -1)
    proj_full = here.gather_depth(proj_turned).reshape(width, -1)

    numbers = jnp.stack([c, z] + [q ^ d for d in range(plane)]).astype(jnp.int32)

    params = vector_whole.astype(F32)
    unit = fc_weight.shape[1]
    hidden = unit * 2 * plane
    gain_one, shift_one, bias_query, bias_value, bias_out, gain_two, shift_two = (
        params[k * width : (k + 1) * width] for k in range(7)
    )
    bias_fc = lax.dynamic_slice_in_dim(params, 7 * width + (2 * q + c) * unit, unit)
    bias_proj = params[7 * width + hidden :]

    pair_tokens = jnp.concatenate([tokens, here.swap_core(tokens)])
    labels = jnp.concatenate([segments, here.swap_core(segments)])
    position = jnp.arange(length)
    allowed = (labels[:, :, None] == labels[:, None, :]) & (position[:, None] >= position[None, :])
    mask = jnp.where(allowed, 0.0, MASKED).astype(F32)

    inputs = pair_tokens.astype(F32)
    scaled_one, spread_one = norm_parts(inputs)
    normed_one = (scaled_one * gain_one + shift_one).astype(BF16)
    qkv_bias = jnp.concatenate([bias_query, jnp.zeros_like(bias_query), bias_value])
    qkv_bias = qkv_bias.reshape(-1, 2, block)
    qkv_bias = here.mine((qkv_bias[:, 0], qkv_bias[:, 1])).reshape(-1)
    projected = jnp.concatenate(
        here.shuffle([dot(normed_one, part) for part in qkv_parts], q), axis=1
    )
    projected = (projected + qkv_bias).astype(BF16)
    share_rows, share_cols = qkv_left_root.shape
    right_root = proj_right_root.astype(BF16)
    root_blocks = lax.all_gather(
        here.after(
            jnp.stack(
                [root.astype(BF16) for root in (qkv_left_root, out_left_root, fc_left_root)]
                + [jnp.concatenate([right_root[:, :share_cols], right_root[:, share_cols:]])]
            ),
            projected,
        ),
        ALL,
    )
    attended = attention_forward(projected, mask)
    attended = here.after(attended, plane_cotangent, fc_full)
    branch = dot(attended[:length], out_full) + here.swap_core(dot(attended[length:], out_full))
    middle = inputs[:length] + (branch + bias_out)
    scaled_two, spread_two = norm_parts(middle)
    normed_two = here.gather_tokens((scaled_two * gain_two + shift_two).astype(BF16))
    normed_two = here.after(normed_two, proj_full)
    pre_act = dot(normed_two, fc_full) + bias_fc
    activated = gelu(pre_act).astype(BF16)

    token_total = length * 2 * plane * depth
    factor = 1.0 / math.sqrt(token_total)
    half = plane * length
    proj_terms = dot_tn(plane_cotangent, activated)
    proj_parts = here.on_depth(proj_terms.reshape(depth, -1, unit).astype(BF16))
    late_cotangent = here.after(plane_cotangent, proj_terms)
    grad_pre = (dot(late_cotangent, proj_full) * gelu_slope(pre_act)).astype(BF16)
    two_mine, two_theirs = dot_nt(grad_pre[:half], fc_full), dot_nt(grad_pre[half:], fc_full)
    grad_normed_two = here.reduce_tokens(two_mine, two_theirs)
    fc_terms = dot_tn(here.after(normed_two, two_mine, two_theirs), grad_pre)

    grad_top = cotangent.astype(F32)
    grad_middle = grad_top + norm_backward(grad_normed_two, scaled_two, spread_two, gain_two)
    own_branch = grad_middle.astype(BF16)
    grad_branch = jnp.concatenate([own_branch, here.swap_core(own_branch)])

    def total(parts):
        return jnp.sum(parts.astype(F32), axis=0) * factor

    proj_sum = total(here.after(proj_parts, own_branch))
    fc_grad = total(
        here.on_depth(here.after(fc_terms.reshape(depth, -1, unit).astype(BF16), own_branch))
    )

    fc_own = here.gather_depth(fc_grad.astype(BF16)).reshape(width, -1)

    grad_attended = dot_nt(grad_branch, out_full).astype(BF16)
    grad_heads = attention_backward(projected, mask, grad_attended)

    rows_own, qkv_cols = qkv_weight.shape
    out_cols = out_weight.shape[1]
    aligned = out_cols % 128 == 0
    head_blocks = here.shuffle(jnp.split(grad_heads, plane, axis=1), q)

    def first_terms(distances, dtype):
        if aligned:
            return first_kernel(
                normed_one, grad_heads, attended, grad_branch, numbers, distances, dtype
            )
        found = []
        for d in distances:
            block = lax.dynamic_slice_in_dim(grad_branch, (q ^ d) * 2 * out_cols, 2 * out_cols, 1)
            term = dot_tn(attended, block).reshape(depth, -1, 2 * out_cols)
            term = jnp.concatenate([term[:, :, :out_cols], term[:, :, out_cols:]], axis=1)
            term = term.reshape(width, out_cols)
            head = dot_tn(normed_one, head_blocks[d])
            found.append(jnp.concatenate([head, term], axis=1).astype(dtype))
        return found

    def second_terms():
        own, *rest = first_terms(tuple(range(plane - 1)), F32)
        return own, *here.all_after(rest, fc_grad)

    first_parts_ready = here.reduce_plane_late(
        first_terms((plane - 1,), BF16)[0], second_terms
    ).astype(BF16)
    first_parts = here.on_depth(first_parts_ready.reshape(depth, -1, qkv_cols + out_cols))

    other_one = sum(dot_nt(part[length:], rows) for part, rows in zip(head_blocks, qkv_parts))
    grad_normed_one = sum(dot_nt(part[:length], rows) for part, rows in zip(head_blocks, qkv_parts))
    grad_normed_one = grad_normed_one + here.swap_core(other_one)
    own_scaled = scaled_one[:length]
    grad_in = norm_backward(grad_normed_one, own_scaled, spread_one[:length], gain_one)
    input_grad = (grad_middle + grad_in).astype(BF16)

    def sum_over_group(mine, theirs):
        return here.reduce_plane(jnp.split(mine + here.swap_core(theirs).astype(F32), plane))

    def column_terms(own, parts):
        if aligned:
            return column_kernel(own, root_blocks, parts, numbers)
        first, found = 0, []
        for which, right_root in parts:
            cols = right_root.shape[0]
            piece = own[:, first : first + cols]
            first += cols
            blocks = root_blocks.reshape(2 * plane, depth, 4, share_rows, share_cols)[:, :, which]
            left_root = blocks.transpose(1, 2, 0, 3).reshape(depth, share_rows, width)
            left_root = jnp.concatenate(here.shuffle(list(left_root), q))
            image = dot(left_root, piece).astype(BF16)
            right_halves = jnp.split(right_root.astype(BF16), 2, axis=1)
            left = dot_nt(lax.dynamic_slice_in_dim(piece, z * rows_own, rows_own), piece)
            left = here.shuffle(jnp.split(left, plane, axis=1), q)
            left = jnp.split(jnp.concatenate(left), 2, axis=1)
            found.append(
                [(dot(image, pick(right_halves)), pick(left)) for pick in (here.mine, here.theirs)]
            )
        mine, theirs = (
            jnp.concatenate([one[k][0] for one in found] + [one[k][1] for one in found], axis=1)
            for k in range(2)
        )
        return mine, theirs.astype(BF16)

    def row_terms(own, which, left_root):
        if aligned:
            return row_kernel(own, root_blocks, which, left_root, numbers)
        blocks = root_blocks.reshape(2 * plane, depth, 4, 2, share_rows // 2, share_cols)[:, :, which]
        chunk = width // depth
        right = dot_nt(own, lax.dynamic_slice_in_dim(own, z * chunk, chunk))
        right = here.shuffle(jnp.split(right, plane), q)
        image = dot_nt(left_root.astype(BF16), own).astype(BF16)
        found = []
        for pick in (here.mine, here.theirs):
            root = pick((blocks[:, :, 0], blocks[:, :, 1]))
            root = [root[:, r].reshape(width, share_cols) for r in range(depth)]
            root = jnp.concatenate(here.shuffle(root, q), axis=1)
            ahead = jnp.split(dot(image, root), plane, axis=1)
            stats = [
                jnp.concatenate(jnp.split(pick(jnp.split(pair, 2)), 2, axis=1)) for pair in right
            ]
            found.append(
                jnp.concatenate([jnp.concatenate(parts) for parts in zip(ahead, stats)])
            )
        return found[0], found[1].astype(BF16)

    fc_mine, fc_theirs = column_terms(fc_own, [(2, fc_right_root)])
    fc_other = here.swap_core(fc_theirs)
    fc_total = here.reduce_plane(jnp.split(fc_mine + fc_other.astype(F32), plane))
    first_sum = total(here.after(first_parts, fc_total))

    qkv_parity = first_sum[:, :qkv_cols]
    qkv_other = here.swap_core(qkv_parity)
    qkv_pair = []
    for k in range(0, qkv_cols, block):
        qkv_pair += here.by_core(qkv_parity[:, k : k + block], qkv_other[:, k : k + block])
    half_count = len(qkv_pair) // 2
    qkv_grad = jnp.concatenate(
        [here.mine((qkv_pair[k], qkv_pair[k + half_count])) for k in range(half_count)], axis=1
    )
    out_halves = jnp.split(first_sum[:, qkv_cols:], 2)
    out_pair = here.by_core(here.mine(out_halves), here.swap_core(here.theirs(out_halves)))
    out_grad = jnp.stack(
        [part.reshape(-1, block, out_cols) for part in out_pair], axis=1
    ).reshape(out_weight.shape)
    first_low = jnp.concatenate([qkv_grad, out_grad], axis=1).astype(BF16)
    first_own = here.gather_depth(first_low).reshape(width, -1)

    fc_far = far_columns(here.after(fc_own, first_low))

    late_activated = here.after(activated, first_low)
    output = here.reduce_tokens(
        dot_nt(late_activated[:half], proj_full), dot_nt(late_activated[half:], proj_full)
    )
    output = (middle + (output + bias_proj)).astype(BF16)

    first_total = sum_over_group(
        *column_terms(here.after(first_own, fc_far[0], output), [(0, qkv_right_root), (1, out_right_root)])
    )

    proj_own = here.gather_depth(proj_sum.astype(BF16)).reshape(width, -1)
    unit_cols = fc_weight.shape[1]
    first_far = far_columns(first_own)
    proj_total = sum_over_group(*row_terms(proj_own, 3, proj_left_root))
    proj_far = far_columns(proj_own)
    own_cols = proj_weight.shape[1]
    proj_grad = jnp.concatenate(
        [
            lax.dynamic_slice_in_dim(part, (2 * q + c) * own_cols, own_cols).T
            for part in proj_far
        ]
    ).astype(F32)
    proj_left_sum = dot_tn(jnp.concatenate(proj_far, axis=1), proj_own)

    def interleave(value):
        value = value.reshape(-1, 1, block)
        zeros = jnp.zeros_like(value)
        return jnp.concatenate(here.by_core(value, zeros), axis=1).reshape(-1)

    head_sums = interleave(jnp.sum(grad_heads.astype(F32), axis=0))
    fc_bias_terms = lax.dynamic_update_slice_in_dim(
        jnp.zeros((hidden,), F32), jnp.sum(grad_pre.astype(F32), axis=0), (2 * q + c) * unit, 0
    )
    vector_terms = jnp.concatenate(
        [
            jnp.sum(grad_normed_one * own_scaled, axis=0),
            jnp.sum(grad_normed_one, axis=0),
            head_sums[:width],
            head_sums[2 * width :],
            jnp.sum(own_branch.astype(F32), axis=0),
            jnp.sum(grad_normed_two * scaled_two, axis=0),
            jnp.sum(grad_normed_two, axis=0),
            fc_bias_terms,
            jnp.sum(grad_top, axis=0),
        ]
    )
    vector_sum = here.swap_core(vector_terms) + vector_terms
    vector_sum = jnp.sum(here.on_depth(vector_sum.reshape(depth, -1, 128)), axis=0)
    distance = 1
    while distance < plane:
        vector_sum = vector_sum + here.swap_plane([vector_sum], [distance], None)[0]
        distance *= 2
    vector_grad = vector_sum.reshape(-1) * factor

    cut = qkv_cols + out_cols
    first_direction = here.transpose_chips(first_total[:, :cut].astype(BF16), "turn").astype(F32)
    fc_direction = here.transpose_chips(fc_total[:, :unit_cols].astype(BF16), "turn").astype(F32)
    qkv_direction, out_direction = first_direction[:, :qkv_cols], first_direction[:, qkv_cols:]
    qkv_left_sum = first_total[:, cut : cut + out_cols]
    out_left_sum = first_total[:, cut + out_cols :]
    fc_left_sum = fc_total[:, unit_cols:]
    proj_direction = proj_total[: proj_weight.shape[0]]
    proj_right_sum = jnp.concatenate(jnp.split(proj_total[proj_weight.shape[0] :], 2), axis=1)

    fc_right_sum = dot_tn(fc_own, jnp.concatenate(fc_far, axis=1))
    qkv_right_sum = dot_tn(
        first_own[:, :qkv_cols], jnp.concatenate([part[:, :qkv_cols] for part in first_far], axis=1)
    )
    out_right_sum = dot_tn(
        first_own[:, qkv_cols:], jnp.concatenate([part[:, qkv_cols:] for part in first_far], axis=1)
    )

    results = []
    for grad, weight, moment, left, right, found, row_total, col_total in (
        (
            qkv_grad,
            qkv_weight,
            qkv_moment,
            qkv_left,
            qkv_right,
            (qkv_left_sum, qkv_right_sum, qkv_direction),
            width,
            3 * width,
        ),
        (
            out_grad,
            out_weight,
            out_moment,
            out_left,
            out_right,
            (out_left_sum, out_right_sum, out_direction),
            width,
            width,
        ),
        (
            fc_grad,
            fc_weight,
            fc_moment,
            fc_left,
            fc_right,
            (fc_left_sum, fc_right_sum, fc_direction),
            width,
            hidden,
        ),
        (
            proj_grad,
            proj_weight,
            proj_moment,
            proj_left,
            proj_right,
            (proj_left_sum, proj_right_sum, proj_direction),
            hidden,
            width,
        ),
    ):
        left_sum, right_sum, direction = found
        new_moment = MOMENTUM * moment + direction
        new_weight = weight - RATE * new_moment
        results += [
            grad,
            DECAY * left + (1.0 - DECAY) / col_total * left_sum,
            DECAY * right + (1.0 - DECAY) / row_total * right_sum,
            new_moment,
            new_weight,
            new_weight.astype(BF16),
        ]
    new_vector_moment = MOMENTUM * vector_moment + vector_grad
    new_vectors = vectors - RATE * new_vector_moment
    return (output, input_grad, *results, vector_grad, new_vector_moment, new_vectors)


def solution(mesh):
    groups, depth = mesh.shape["grp"], mesh.shape["in"]
    fine = Mesh(mesh.devices.reshape(groups // 4, 2, 2, depth), ALL)
    grp = ("y", "x", "c")
    tokens, cols, rows, flat = P(ALL, None), P("in", grp), P(grp, "in"), P("in")
    matrix_in = (cols, cols, cols, rows, cols, rows)
    matrix_out = (cols, cols, rows, cols, cols, cols)
    return jax.shard_map(
        on_device,
        mesh=fine,
        in_specs=(tokens, tokens, tokens, flat, flat) + matrix_in * 4,
        out_specs=(tokens, tokens) + matrix_out * 4 + (flat, flat, flat),
        check_vma=False,
    )
```

time: 683 us -> 574 us (0.84)
  waiting for transfers between devices: 296 us -> 224 us
  starting transfers between devices: 170 us -> 131 us
  local copies, waits for them, and re-layouts: 44.7 us -> 30.5 us
  other arithmetic: 52 us -> 63.6 us
    ppermute x122 -> x76, waiting for transfers between devices: 296 us -> 148 us  [send(): lax.ppermute(value, axes, pair)]
    ppermute x122 -> x76, starting transfers between devices: 169 us -> 85.8 us  [send(): lax.ppermute(value, axes, pair)]
    all_to_all x0 -> x11, waiting for transfers between devices: none -> 75.1 us  [on_depth(): value = lax.all_to_all(value, 'in', 0, 0, tiled=True)]
    all_to_all x0 -> x11, starting transfers between devices: none -> 45.1 us  [on_depth(): value = lax.all_to_all(value, 'in', 0, 0, tiled=True)]
    unnamed x357 -> x236, local copies, waits for them, and re-layouts: 22 us -> 10.8 us
    another operation x18 -> x9, other arithmetic: 4.79 us -> 13.7 us
    broadcast_in_dim x0 -> x7, local copies, waits for them, and re-layouts: none -> 7.1 us  [gather_depth(): jnp.broadcast_to(value[None], (self.depth,) + value.shape)]
    pallas_call x3 -> x2, Pallas kernels: 12 us -> 15 us  [column_kernel(): pl.pallas_call(body, grid=(1,), out_shape=(jax.ShapeDtypeStruct(shape, F3...]
  transfers between devices with their start and end apart: 123 -> 88, of which waited for: 61 -> 50; matrix products, arithmetic and copies ran while one was open for 19% -> 22% of each run, Pallas kernels for 7% -> 9%
where the time goes in v2:
time: 574 us; the launch traced here: 564 us
  waiting for transfers between devices  224 us (39%)
  starting transfers between devices  131 us (23%)
  other arithmetic  63.6 us (11%)
  Pallas kernels  52.5 us (9%)
  matrix products  46.5 us (8%)
  local copies, waits for them, and re-layouts  30.5 us (5%)
  between operations  16.1 us (3%)
    ppermute x76, waiting for transfers between devices, send(): lax.ppermute(value, axes, pair)  148 us
    ppermute x76, starting transfers between devices, send(): lax.ppermute(value, axes, pair)  85.8 us
    all_to_all x11, waiting for transfers between devices, on_depth(): value = lax.all_to_all(value, 'in', 0, 0, tiled=True)  75.1 us
    all_to_all x11, starting transfers between devices, on_depth(): value = lax.all_to_all(value, 'in', 0, 0, tiled=True)  45.1 us
    dot_general x13, matrix products, dot_nt(): lax.dot_general(left, right, (((1,), (1,)), ((), ())), preferred_element_...  20.7 us
    pallas_call x2, Pallas kernels, column_kernel(): pl.pallas_call(body, grid=(1,), out_shape=(jax.ShapeDtypeStruct(shape, F3...  15 us
    another operation x7, other arithmetic  13.7 us
    dot_general x8, matrix products, dot(): return jnp.dot(left, right, preferred_element_type=F32)  13.3 us
  transfers between devices with their start and end apart: 88, of which 50 were waited for; matrix products, arithmetic and copies ran while one was open for 22% of the time, Pallas kernels for 9%

profile of v2, /device:TPU:0, one launch (start us, length us, event | category | flops | bytes accessed | tf_op | source)
XLA Modules:
  0.0 563.7 jit_solution(12296754971833866579)
XLA Ops:
  12.8 6.4 %all-to-all-start = ((bf16[4,256,384]{2,1,0:T(8,128)(2,1)}), bf16[4,256,384]{2,1,0:T(8,128)(2,1)S(1)}, u32[]{:S(2)}, u32[]{:S(2)}) async-start(bf16[4,256,384]{2,1,0:T(8,128)(2,1)} %broadcast_in_dim.29), calls=%async_computation | async-start | bytes 1572864 | tf_op jit(solution)/shard_map/all_to_all | solution.py:313
  21.1 25.2 %all-to-all-done = bf16[4,256,384]{2,1,0:T(8,128)(2,1)S(1)} async-done(((bf16[4,256,384]{2,1,0:T(8,128)(2,1)}), bf16[4,256,384]{2,1,0:T(8,128)(2,1)S(1)}, u32[]{:S(2)}, u32[]{:S(2)}) %all-to-all-start) | async-done | bytes 786464 | tf_op jit(solution)/shard_map/all_to_all | solution.py:313
  70.8 11.6 %collective-permute-done.8 = bf16[1024,384]{1,0:T(8,128)(2,1)S(1)} collective-permute-done((bf16[1024,384]{1,0:T(8,128)(2,1)S(1)}, bf16[1024,384]{1,0:T(8,128)(2,1)S(1)}, u32[]{:S(2)}, u32[]{:S(2)}) %collective-permute-start.8) | collective-permute-done | bytes 786464 | tf_op jit(solution)/shard_map/ppermute | solution.py:292
  109.5 7.1 %attention_forward.1.attended_ref = bf16[256,512]{1,0:T(8,128)(2,1)} custom-call(bf16[256,1536]{1,0:T(8,128)(2,1)} %fusion.27.qkv_ref, f32[2,128,128]{2,1,0:T(8,128)} %and_select_fusion.bias_ref), custom_call_target="tpu_custom_call" | custom-call | tf_op jit(solution)/shard_map/attention_forward/pallas_call | solution.py:70
  120.6 5.9 %all-to-all-done.2 = bf16[4,256,512]{2,1,0:T(8,128)(2,1)S(1)} async-done(((bf16[4,256,512]{2,1,0:T(8,128)(2,1)}), bf16[4,256,512]{2,1,0:T(8,128)(2,1)S(1)}, u32[]{:S(2)}, u32[]{:S(2)}) %all-to-all-start.2) | async-done | bytes 1048608 | tf_op jit(solution)/shard_map/all_to_all | solution.py:313
  141.5 5.9 %collective-permute-done.21.refs_1_ = bf16[128,1024]{1,0:T(8,128)(2,1)} collective-permute-done((bf16[128,1024]{1,0:T(8,128)(2,1)}, bf16[128,1024]{1,0:T(8,128)(2,1)}, u32[]{:S(2)}, u32[]{:S(2)}) %collective-permute-start.21) | collective-permute-done | bytes 262176 | tf_op jit(solution)/shard_map/ppermute | solution.py:292
  147.5 6.4 %collective-permute-done.22.refs_2_ = bf16[128,1024]{1,0:T(8,128)(2,1)} collective-permute-done((bf16[128,1024]{1,0:T(8,128)(2,1)}, bf16[128,1024]{1,0:T(8,128)(2,1)}, u32[]{:S(2)}, u32[]{:S(2)}) %collective-permute-start.22) | collective-permute-done | bytes 262176 | tf_op jit(solution)/shard_map/ppermute | solution.py:292
  159.2 21.1 %all-to-all-done.3 = bf16[4,256,512]{2,1,0:T(8,128)(2,1)S(1)} async-done(((bf16[4,256,512]{2,1,0:T(8,128)(2,1)}), bf16[4,256,512]{2,1,0:T(8,128)(2,1)S(1)}, u32[]{:S(2)}, u32[]{:S(2)}) %all-to-all-start.3) | async-done | bytes 1048608 | tf_op jit(solution)/shard_map/all_to_all | solution.py:313
  215.2 6.4 %all-to-all-done.4 = bf16[4,256,512]{2,1,0:T(8,128)(2,1)S(1)} async-done(((bf16[4,256,512]{2,1,0:T(8,128)(2,1)}), bf16[4,256,512]{2,1,0:T(8,128)(2,1)S(1)}, u32[]{:S(2)}, u32[]{:S(2)}) %all-to-all-start.4) | async-done | bytes 1048608 | tf_op jit(solution)/shard_map/all_to_all | solution.py:313
  229.9 9.5 %attention_backward.1.heads_ref = bf16[256,1536]{1,0:T(8,128)(2,1)} custom-call(bf16[256,1536]{1,0:T(8,128)(2,1)} %fusion.27.qkv_ref, f32[2,128,128]{2,1,0:T(8,128)} %and_select_fusion.bias_ref, bf16[256,512]{1,0:T(8,128)(2,1)} %convolution_convert_fusion.2.grad_ref), custom_call_target="tpu_custom_call" | custom-call | tf_op jit(solution)/shard_map/attention_backward/pallas_call | solution.py:116
  274.8 7.7 %all-to-all-done.6 = bf16[4,256,512]{2,1,0:T(8,128)(2,1)S(1)} async-done(((bf16[4,256,512]{2,1,0:T(8,128)(2,1)}), bf16[4,256,512]{2,1,0:T(8,128)(2,1)S(1)}, u32[]{:S(2)}, u32[]{:S(2)}) %all-to-all-start.6) | async-done | bytes 1048608 | tf_op jit(solution)/shard_map/all_to_all | solution.py:313
  284.1 6.6 %column_terms.2 = (f32[1024,640]{1,0:T(8,128)S(1)}, bf16[1024,640]{1,0:T(8,128)(2,1)}) custom-call(s32[6]{0:T(128)S(1)} %copy-done.8, bf16[1024,512]{1,0:T(8,128)(2,1)S(1)} %bitcast.96, bf16[32,4,256,128]{3,2,1,0:T(8,128)(2,1)} %bitcast.106, f32[512,1024]{1,0:T(8,128)S(1)} %copy-done.4), custom_call_target="tpu_custom_call" | custom-call | tf_op jit(solution)/shard_map/column_terms/pallas_call | solution.py:210
  299.9 5.3 all-to-all-start.7
  340.0 7.7 %collective-permute-done.44 = bf16[512,512]{1,0:T(8,128)(2,1)S(1)} collective-permute-done((bf16[512,512]{1,0:T(8,128)(2,1)S(1)}, bf16[512,512]{1,0:T(8,128)(2,1)S(1)}, u32[]{:S(2)}, u32[]{:S(2)}) %collective-permute-start.44) | collective-permute-done | bytes 524320 | tf_op jit(solution)/shard_map/ppermute | solution.py:292
  398.2 8.4 %column_terms.3 = (f32[1024,768]{1,0:T(8,128)S(1)}, bf16[1024,768]{1,0:T(8,128)(2,1)}) custom-call(s32[6]{0:T(128)S(1)} %copy-done.8, bf16[1024,512]{1,0:T(8,128)(2,1)S(1)} %bitcast.101, bf16[32,4,256,128]{3,2,1,0:T(8,128)(2,1)} %bitcast.107, bf16[32,4,256,128]{3,2,1,0:T(8,128)(2,1)} %bitcast.108, f32[384,768]{1,0:T(8,128)S(1)} %copy-done.6, ...), custom_call_target="tpu_custom_call" | custom-call | tf_op jit(solution)/shard_map/column_terms/pallas_call | solution.py:210
  413.6 5.9 %all-to-all-done.9 = bf16[4,256,512]{2,1,0:T(8,128)(2,1)S(1)} async-done(((bf16[4,256,512]{2,1,0:T(8,128)(2,1)}), bf16[4,256,512]{2,1,0:T(8,128)(2,1)S(1)}, u32[]{:S(2)}, u32[]{:S(2)}) %all-to-all-start.9) | async-done | bytes 1048608 | tf_op jit(solution)/shard_map/all_to_all | solution.py:313
  434.7 6.8 %row_terms.1 = (f32[5120,128]{1,0:T(8,128)S(1)}, bf16[5120,128]{1,0:T(8,128)(2,1)}) custom-call(s32[6]{0:T(128)S(1)} %copy-done.8, bf16[1024,512]{1,0:T(8,128)(2,1)S(1)} %bitcast.104, bf16[32,4,256,128]{3,2,1,0:T(8,128)(2,1)} %bitcast.109, f32[1024,512]{1,0:T(8,128)S(1)} %copy-done.5), custom_call_target="tpu_custom_call" | custom-call | tf_op jit(solution)/shard_map/row_terms/pallas_call | solution.py:262
  452.0 5.9 %collective-permute-start.57 = (bf16[512,512]{1,0:T(8,128)(2,1)S(1)}, bf16[512,512]{1,0:T(8,128)(2,1)S(1)}, u32[]{:S(2)}, u32[]{:S(2)}) collective-permute-start(bf16[512,512]{1,0:T(8,128)(2,1)S(1)} %bitcast.118), channel_id=1, source_target_pairs={{0,8},{9,1},{18,26},{27,19},{4,12},{13,5},{22,30},{31,23}} | collective-permute-start | bytes 1572872 | tf_op jit(solution)/shard_map/ppermute | solution.py:292
  464.4 18.0 %collective-permute-done.57 = bf16[512,512]{1,0:T(8,128)(2,1)S(1)} collective-permute-done((bf16[512,512]{1,0:T(8,128)(2,1)S(1)}, bf16[512,512]{1,0:T(8,128)(2,1)S(1)}, u32[]{:S(2)}, u32[]{:S(2)}) %collective-permute-start.57) | collective-permute-done | bytes 524320 | tf_op jit(solution)/shard_map/ppermute | solution.py:292
  484.5 8.9 %collective-permute-start.60 = (bf16[512,512]{1,0:T(8,128)(2,1)S(1)}, bf16[512,512]{1,0:T(8,128)(2,1)S(1)}, u32[]{:S(2)}, u32[]{:S(2)}) collective-permute-start(bf16[512,512]{1,0:T(8,128)(2,1)S(1)} %broadcast_select_fusion.9), channel_id=1, source_target_pairs={{0,8},{2,10},{9,1},{11,3},{16,24},{18,26},{25,17},{27,19},{4,12},{... | collective-permute-start | bytes 1572872 | tf_op jit(solution)/shard_map/ppermute | solution.py:292
  495.5 8.3 %collective-permute-done.60 = bf16[512,512]{1,0:T(8,128)(2,1)S(1)} collective-permute-done((bf16[512,512]{1,0:T(8,128)(2,1)S(1)}, bf16[512,512]{1,0:T(8,128)(2,1)S(1)}, u32[]{:S(2)}, u32[]{:S(2)}) %collective-permute-start.60) | collective-permute-done | bytes 524320 | tf_op jit(solution)/shard_map/ppermute | solution.py:292
  508.2 6.7 %collective-permute-done.65 = bf16[1280,128]{1,0:T(8,128)(2,1)S(1)} collective-permute-done((bf16[1280,128]{1,0:T(8,128)(2,1)S(1)}, bf16[1280,128]{1,0:T(8,128)(2,1)S(1)}, u32[]{:S(2)}, u32[]{:S(2)}) %collective-permute-start.65) | collective-permute-done | bytes 327712 | tf_op jit(solution)/shard_map/ppermute | solution.py:292
  514.9 5.9 %collective-permute-done.66 = bf16[1280,128]{1,0:T(8,128)(2,1)S(1)} collective-permute-done((bf16[1280,128]{1,0:T(8,128)(2,1)S(1)}, bf16[1280,128]{1,0:T(8,128)(2,1)S(1)}, u32[]{:S(2)}, u32[]{:S(2)}) %collective-permute-start.66) | collective-permute-done | bytes 327712 | tf_op jit(solution)/shard_map/ppermute | solution.py:292
  524.5 7.0 %collective-permute-done.68 = bf16[512,512]{1,0:T(8,128)(2,1)S(1)} collective-permute-done((bf16[512,512]{1,0:T(8,128)(2,1)S(1)}, bf16[512,512]{1,0:T(8,128)(2,1)S(1)}, u32[]{:S(2)}, u32[]{:S(2)}) %collective-permute-start.68) | collective-permute-done | bytes 524320 | tf_op jit(solution)/shard_map/ppermute | solution.py:292
  (577 shorter events, 333.3 us)
Async XLA Ops:
  12.8 33.5 %all-to-all-start = ((bf16[4,256,384]{2,1,0:T(8,128)(2,1)}), bf16[4,256,384]{2,1,0:T(8,128)(2,1)S(1)}, u32[]{:S(2)}, u32[]{:S(2)}) async-start(bf16[4,256,384]{2,1,0:T(8,128)(2,1)} %broadcast_in_dim.29), calls=%async_computation | async-start | bytes 1572864 | tf_op jit(solution)/shard_map/all_to_all | solution.py:313
  20.2 30.3 %collective-permute-start.4 = (bf16[256,512]{0,1:T(8,128)(2,1)S(1)}, bf16[256,512]{0,1:T(8,128)(2,1)S(1)}, u32[]{:S(2)}, u32[]{:S(2)}) collective-permute-start(bf16[256,512]{0,1:T(8,128)(2,1)S(1)} %maximum_bitcast_fusion), channel_id=1, source_target_pairs={{0,0},{1,8},{2,16},{3,24},{8,1},{9,9},{10,17},{11,25},{16,2},{17,1... | collective-permute-start | bytes 786440 | tf_op jit(solution)/shard_map/ppermute | solution.py:292
  47.1 21.3 %all-to-all-start.1 = ((bf16[4,140,256]{2,1,0:T(8,128)(2,1)}), bf16[4,140,256]{2,1,0:T(8,128)(2,1)S(1)}, u32[]{:S(2)}, u32[]{:S(2)}) async-start(bf16[4,140,256]{2,1,0:T(8,128)(2,1)} %broadcast_in_dim.28), calls=%async_computation.1 | async-start | bytes 589824 | tf_op jit(solution)/shard_map/all_to_all | solution.py:313
  50.5 232.0 %all-gather.3.cloned.1.call-start = ((), (), s32[]{:S(2)}) async-start(), calls=%async_computation.11 | async-start | bytes 8650752 | tf_op jit(solution)/shard_map/all_gather | solution.py:555
  94.9 31.6 %all-to-all-start.2 = ((bf16[4,256,512]{2,1,0:T(8,128)(2,1)}), bf16[4,256,512]{2,1,0:T(8,128)(2,1)S(1)}, u32[]{:S(2)}, u32[]{:S(2)}) async-start(bf16[4,256,512]{2,1,0:T(8,128)(2,1)} %broadcast_in_dim.33), calls=%async_computation.2 | async-start | bytes 2097152 | tf_op jit(solution)/shard_map/all_to_all | solution.py:313
  131.4 48.9 %all-to-all-start.3 = ((bf16[4,256,512]{2,1,0:T(8,128)(2,1)}), bf16[4,256,512]{2,1,0:T(8,128)(2,1)S(1)}, u32[]{:S(2)}, u32[]{:S(2)}) async-start(bf16[4,256,512]{2,1,0:T(8,128)(2,1)} %broadcast_in_dim.34), calls=%async_computation.3 | async-start | bytes 2097152 | tf_op jit(solution)/shard_map/all_to_all | solution.py:313
  191.5 30.2 %all-to-all-start.4 = ((bf16[4,256,512]{2,1,0:T(8,128)(2,1)}), bf16[4,256,512]{2,1,0:T(8,128)(2,1)S(1)}, u32[]{:S(2)}, u32[]{:S(2)}) async-start(bf16[4,256,512]{2,1,0:T(8,128)(2,1)} %bitcast.126), calls=%async_computation.4 | async-start | bytes 2097152 | tf_op jit(solution)/shard_map/all_to_all | solution.py:313
  221.6 29.6 %all-to-all-start.5 = ((bf16[4,256,512]{2,1,0:T(8,128)(2,1)}), bf16[4,256,512]{2,1,0:T(8,128)(2,1)S(1)}, u32[]{:S(2)}, u32[]{:S(2)}) async-start(bf16[4,256,512]{2,1,0:T(8,128)(2,1)} %bitcast.125), calls=%async_computation.5 | async-start | bytes 2097152 | tf_op jit(solution)/shard_map/all_to_all | solution.py:313
  246.6 20.0 %collective-permute-start.34 = (bf16[512,512]{1,0:T(8,128)(2,1)}, bf16[512,512]{1,0:T(8,128)(2,1)}, u32[]{:S(2)}, u32[]{:S(2)}) collective-permute-start(bf16[512,512]{1,0:T(8,128)(2,1)} %get-tuple-element.138), channel_id=1, source_target_pairs={{0,8},{8,0},{16,24},{24,16},{1,9},{9,1},{17,25},{25,17},{2,10},{10... | collective-permute-start | bytes 1572872 | tf_op jit(solution)/shard_map/ppermute | solution.py:292
  247.7 21.4 %collective-permute-start.33 = (bf16[512,512]{1,0:T(8,128)(2,1)}, bf16[512,512]{1,0:T(8,128)(2,1)}, u32[]{:S(2)}, u32[]{:S(2)}) collective-permute-start(bf16[512,512]{1,0:T(8,128)(2,1)} %get-tuple-element.136), channel_id=1, source_target_pairs={{0,16},{8,24},{16,0},{24,8},{1,17},{9,25},{17,1},{25,9},{2,18},{10... | collective-permute-start | bytes 1572872 | tf_op jit(solution)/shard_map/ppermute | solution.py:292
  253.4 29.1 %all-to-all-start.6 = ((bf16[4,256,512]{2,1,0:T(8,128)(2,1)}), bf16[4,256,512]{2,1,0:T(8,128)(2,1)S(1)}, u32[]{:S(2)}, u32[]{:S(2)}) async-start(bf16[4,256,512]{2,1,0:T(8,128)(2,1)} %broadcast_in_dim.35), calls=%async_computation.6 | async-start | bytes 2097152 | tf_op jit(solution)/shard_map/all_to_all | solution.py:313
  271.5 24.7 %collective-permute-start.35 = (bf16[1024,512]{1,0:T(8,128)(2,1)}, bf16[1024,512]{1,0:T(8,128)(2,1)}, u32[]{:S(2)}, u32[]{:S(2)}) collective-permute-start(bf16[1024,512]{1,0:T(8,128)(2,1)} %pad_maximum_fusion.1), channel_id=1, source_target_pairs={{0,8},{8,0},{16,24},{24,16},{1,9},{9,1},{17,25},{25,17},{2,10},{10... | collective-permute-start | bytes 3145736 | tf_op jit(solution)/shard_map/ppermute | solution.py:292
  272.6 24.4 %collective-permute-start.36 = (bf16[1024,512]{1,0:T(8,128)(2,1)}, bf16[1024,512]{1,0:T(8,128)(2,1)}, u32[]{:S(2)}, u32[]{:S(2)}) collective-permute-start(bf16[1024,512]{1,0:T(8,128)(2,1)} %pad_maximum_fusion.2), channel_id=1, source_target_pairs={{0,16},{8,24},{16,0},{24,8},{1,17},{9,25},{17,1},{25,9},{2,18},{10... | collective-permute-start | bytes 3145736 | tf_op jit(solution)/shard_map/ppermute | solution.py:292
  292.0 65.4 %collective-permute-start.51 = (f32[128,1024]{1,0:T(8,128)}, f32[128,1024]{1,0:T(8,128)}, u32[]{:S(2)}, u32[]{:S(2)}) collective-permute-start(f32[128,1024]{1,0:T(8,128)} %fusion.39), channel_id=1, source_target_pairs={{0,4},{4,0},{1,5},{5,1},{2,6},{6,2},{3,7},{7,3},{8,12},{12,8},{9,1... | collective-permute-start | bytes 1572872 | tf_op jit(solution)/shard_map/ppermute | solution.py:292
  299.9 29.1 %all-to-all-start.7 = ((bf16[4,256,512]{2,1,0:T(8,128)(2,1)}), bf16[4,256,512]{2,1,0:T(8,128)(2,1)}, u32[]{:S(2)}, u32[]{:S(2)}) async-start(bf16[4,256,512]{2,1,0:T(8,128)(2,1)} %bitcast.16), calls=%async_computation.7 | async-start | bytes 2097152 | tf_op jit(solution)/shard_map/all_to_all | solution.py:313
  339.8 30.4 %collective-permute-start.43 = (bf16[512,1024]{1,0:T(8,128)(2,1)}, bf16[512,1024]{1,0:T(8,128)(2,1)}, u32[]{:S(2)}, u32[]{:S(2)}) collective-permute-start(bf16[512,1024]{1,0:T(8,128)(2,1)} %convolution_convert_fusion.1), channel_id=1, source_target_pairs={{0,4},{4,0},{1,5},{5,1},{2,6},{6,2},{3,7},{7,3},{8,12},{12,8},{9,1... | collective-permute-start | bytes 3145736 | tf_op jit(solution)/shard_map/ppermute | solution.py:292
  360.8 28.9 %all-to-all-start.8 = ((bf16[4,256,512]{2,1,0:T(8,128)(2,1)}), bf16[4,256,512]{2,1,0:T(8,128)(2,1)S(1)}, u32[]{:S(2)}, u32[]{:S(2)}) async-start(bf16[4,256,512]{2,1,0:T(8,128)(2,1)} %broadcast_in_dim.36), calls=%async_computation.8 | async-start | bytes 2097152 | tf_op jit(solution)/shard_map/all_to_all | solution.py:313
  370.2 24.5 %collective-permute-start.52 = (bf16[1024,512]{1,0:T(8,128)(2,1)}, bf16[1024,512]{1,0:T(8,128)(2,1)}, u32[]{:S(2)}, u32[]{:S(2)}) collective-permute-start(bf16[1024,512]{1,0:T(8,128)(2,1)} %pad_maximum_fusion.3), channel_id=1, source_target_pairs={{0,4},{4,0},{1,5},{5,1},{2,6},{6,2},{3,7},{7,3},{8,12},{12,8},{9,1... | collective-permute-start | bytes 3145736 | tf_op jit(solution)/shard_map/ppermute | solution.py:292
  390.8 28.7 %all-to-all-start.9 = ((bf16[4,256,512]{2,1,0:T(8,128)(2,1)}), bf16[4,256,512]{2,1,0:T(8,128)(2,1)S(1)}, u32[]{:S(2)}, u32[]{:S(2)}) async-start(bf16[4,256,512]{2,1,0:T(8,128)(2,1)} %broadcast_in_dim.37), calls=%async_computation.9 | async-start | bytes 2097152 | tf_op jit(solution)/shard_map/all_to_all | solution.py:313
  419.5 23.6 %all-to-all-start.10 = ((f32[4,24,128]{2,1,0:T(8,128)}), f32[4,24,128]{2,1,0:T(8,128)S(1)}, u32[]{:S(2)}, u32[]{:S(2)}) async-start(f32[4,24,128]{2,1,0:T(8,128)} %bitcast.36), calls=%async_computation.10 | async-start | bytes 98304 | tf_op jit(solution)/shard_map/all_to_all | solution.py:313
  452.0 30.4 %collective-permute-start.57 = (bf16[512,512]{1,0:T(8,128)(2,1)S(1)}, bf16[512,512]{1,0:T(8,128)(2,1)S(1)}, u32[]{:S(2)}, u32[]{:S(2)}) collective-permute-start(bf16[512,512]{1,0:T(8,128)(2,1)S(1)} %bitcast.118), channel_id=1, source_target_pairs={{0,8},{9,1},{18,26},{27,19},{4,12},{13,5},{22,30},{31,23}} | collective-permute-start | bytes 1572872 | tf_op jit(solution)/shard_map/ppermute | solution.py:292
  457.8 24.7 %collective-permute-start.58 = (bf16[512,512]{1,0:T(8,128)(2,1)S(1)}, bf16[512,512]{1,0:T(8,128)(2,1)S(1)}, u32[]{:S(2)}, u32[]{:S(2)}) collective-permute-start(bf16[512,512]{1,0:T(8,128)(2,1)S(1)} %bitcast.116), channel_id=1, source_target_pairs={{0,16},{9,25},{18,2},{27,11},{4,20},{13,29},{22,6},{31,15}} | collective-permute-start | bytes 1572872 | tf_op jit(solution)/shard_map/ppermute | solution.py:292
  460.1 33.4 %collective-permute-start.63 = (bf16[256,512]{1,0:T(8,128)(2,1)S(1)}, bf16[256,512]{1,0:T(8,128)(2,1)S(1)}, u32[]{:S(2)}, u32[]{:S(2)}) collective-permute-start(bf16[256,512]{1,0:T(8,128)(2,1)S(1)} %copy-done.80), channel_id=1, source_target_pairs={{0,0},{1,8},{2,16},{3,24},{8,1},{9,9},{10,17},{11,25},{16,2},{17,1... | collective-permute-start | bytes 786440 | tf_op jit(solution)/shard_map/ppermute | solution.py:292
  508.1 39.2 %collective-permute-start.61 = (bf16[1024,512]{1,0:T(8,128)(2,1)S(1)}, bf16[1024,512]{1,0:T(8,128)(2,1)S(1)}, u32[]{:S(2)}, u32[]{:S(2)}) collective-permute-start(bf16[1024,512]{1,0:T(8,128)(2,1)S(1)} %pad_maximum_fusion.4), channel_id=1, source_target_pairs={{0,4},{4,0},{1,5},{5,1},{2,6},{6,2},{3,7},{7,3},{8,12},{12,8},{9,1... | collective-permute-start | bytes 3145736 | tf_op jit(solution)/shard_map/ppermute | solution.py:292
  (178 other events, 1896.0 us)
Sparse Core Ops, SparseCore 0:
  93.8 97.5 all-gather.2

commit v3 on v2

--- a/solution.py
+++ b/solution.py
@@ -511,8 +511,9 @@
     )
 
     proj_turned = here.transpose_chips(proj_share.T, "plane")
+    qkv_parts = here.gather_plane(here.gather_depth(qkv_share).reshape(width, -1))
     plane_cotangent = here.gather_tokens(cotangent)
-    qkv_parts = here.gather_plane(here.gather_depth(qkv_share).reshape(width, -1))
+    fc_full = here.gather_depth(fc_share).reshape(width, -1)
     small_share = jnp.concatenate(
         [out_share, vectors.astype(BF16).reshape(-1, out_share.shape[1])]
     )
@@ -520,7 +521,6 @@
     vector_whole = small_whole[:, out_share.shape[0] :].reshape(-1)
     out_rows = small_whole[:, : out_share.shape[0]].reshape(-1, out_share.shape[1])
     out_full = jnp.concatenate(here.shuffle(here.gather_plane(out_rows), q), axis=1)
-    fc_full = here.gather_depth(fc_share).reshape(width, -1)
     proj_full = here.gather_depth(proj_turned).reshape(width, -1)
 
     numbers = jnp.stack([c, z] + [q ^ d for d in range(plane)]).astype(jnp.int32)
@@ -543,6 +543,7 @@
     inputs = pair_tokens.astype(F32)
     scaled_one, spread_one = norm_parts(inputs)
     normed_one = (scaled_one * gain_one + shift_one).astype(BF16)
+    normed_one = here.after(normed_one, fc_full)
     qkv_bias = jnp.concatenate([bias_query, jnp.zeros_like(bias_query), bias_value])
     qkv_bias = qkv_bias.reshape(-1, 2, block)
     qkv_bias = here.mine((qkv_bias[:, 0], qkv_bias[:, 1])).reshape(-1)
@@ -563,12 +564,11 @@
         ALL,
     )
     attended = attention_forward(projected, mask)
-    attended = here.after(attended, plane_cotangent, fc_full)
+    attended = here.after(attended, plane_cotangent, proj_full)
     branch = dot(attended[:length], out_full) + here.swap_core(dot(attended[length:], out_full))
     middle = inputs[:length] + (branch + bias_out)
     scaled_two, spread_two = norm_parts(middle)
     normed_two = here.gather_tokens((scaled_two * gain_two + shift_two).astype(BF16))
-    normed_two = here.after(normed_two, proj_full)
     pre_act = dot(normed_two, fc_full) + bias_fc
     activated = gelu(pre_act).astype(BF16)
 
@@ -576,12 +576,21 @@
     factor = 1.0 / math.sqrt(token_total)
     half = plane * length
     proj_terms = dot_tn(plane_cotangent, activated)
-    proj_parts = here.on_depth(proj_terms.reshape(depth, -1, unit).astype(BF16))
     late_cotangent = here.after(plane_cotangent, proj_terms)
     grad_pre = (dot(late_cotangent, proj_full) * gelu_slope(pre_act)).astype(BF16)
     two_mine, two_theirs = dot_nt(grad_pre[:half], fc_full), dot_nt(grad_pre[half:], fc_full)
     grad_normed_two = here.reduce_tokens(two_mine, two_theirs)
     fc_terms = dot_tn(here.after(normed_two, two_mine, two_theirs), grad_pre)
+    rows_own = qkv_weight.shape[0]
+    forward_parts = here.on_depth(
+        jnp.concatenate(
+            [
+                proj_terms.reshape(depth, rows_own, unit).astype(BF16),
+                fc_terms.reshape(depth, rows_own, unit).astype(BF16),
+            ],
+            axis=1,
+        )
+    )
 
     grad_top = cotangent.astype(F32)
     grad_middle = grad_top + norm_backward(grad_normed_two, scaled_two, spread_two, gain_two)
@@ -591,17 +600,14 @@
     def total(parts):
         return jnp.sum(parts.astype(F32), axis=0) * factor
 
-    proj_sum = total(here.after(proj_parts, own_branch))
-    fc_grad = total(
-        here.on_depth(here.after(fc_terms.reshape(depth, -1, unit).astype(BF16), own_branch))
-    )
-
+    forward_sum = total(here.after(forward_parts, own_branch))
+    proj_sum, fc_grad = forward_sum[:rows_own], forward_sum[rows_own:]
     fc_own = here.gather_depth(fc_grad.astype(BF16)).reshape(width, -1)
 
     grad_attended = dot_nt(grad_branch, out_full).astype(BF16)
     grad_heads = attention_backward(projected, mask, grad_attended)
 
-    rows_own, qkv_cols = qkv_weight.shape
+    qkv_cols = qkv_weight.shape[1]
     out_cols = out_weight.shape[1]
     aligned = out_cols % 128 == 0
     head_blocks = here.shuffle(jnp.split(grad_heads, plane, axis=1), q)
@@ -717,12 +723,14 @@
     )
     output = (middle + (output + bias_proj)).astype(BF16)
 
+    unit_cols = fc_weight.shape[1]
+    fc_direction = here.transpose_chips(fc_total[:, :unit_cols].astype(BF16), "plane").astype(F32)
+
     first_total = sum_over_group(
-        *column_terms(here.after(first_own, fc_far[0], output), [(0, qkv_right_root), (1, out_right_root)])
+        *column_terms(first_own, [(0, qkv_right_root), (1, out_right_root)])
     )
 
     proj_own = here.gather_depth(proj_sum.astype(BF16)).reshape(width, -1)
-    unit_cols = fc_weight.shape[1]
     first_far = far_columns(first_own)
     proj_total = sum_over_group(*row_terms(proj_own, 3, proj_left_root))
     proj_far = far_columns(proj_own)
@@ -758,7 +766,14 @@
         ]
     )
     vector_sum = here.swap_core(vector_terms) + vector_terms
-    vector_sum = jnp.sum(here.on_depth(vector_sum.reshape(depth, -1, 128)), axis=0)
+    vector_sum = vector_sum.reshape(depth, -1, 128)
+    steps = range(1, depth)
+    vector_parts = here.send(
+        [lax.dynamic_index_in_dim(vector_sum, (z + k) % depth, 0, False) for k in steps],
+        "in",
+        [[(n, (n + k) % depth) for n in range(depth)] for k in steps],
+    )
+    vector_sum = sum(vector_parts, lax.dynamic_index_in_dim(vector_sum, z, 0, False))
     distance = 1
     while distance < plane:
         vector_sum = vector_sum + here.swap_plane([vector_sum], [distance], None)[0]
@@ -767,7 +782,6 @@
 
     cut = qkv_cols + out_cols
     first_direction = here.transpose_chips(first_total[:, :cut].astype(BF16), "turn").astype(F32)
-    fc_direction = here.transpose_chips(fc_total[:, :unit_cols].astype(BF16), "turn").astype(F32)
     qkv_direction, out_direction = first_direction[:, :qkv_cols], first_direction[:, qkv_cols:]
     qkv_left_sum = first_total[:, cut : cut + out_cols]
     out_left_sum = first_total[:, cut + out_cols :]

time: 574 us -> 541 us (0.943)
  waiting for transfers between devices: 224 us -> 182 us
  starting transfers between devices: 131 us -> 147 us
  other arithmetic: 63.6 us -> 57.2 us
    ppermute x76 -> x79, waiting for transfers between devices: 148 us -> 124 us  [send(): lax.ppermute(value, axes, pair)]
    ppermute x76 -> x79, starting transfers between devices: 85.8 us -> 104 us  [send(): lax.ppermute(value, axes, pair)]
    all_to_all x11 -> x9, waiting for transfers between devices: 75.1 us -> 58.1 us  [on_depth(): value = lax.all_to_all(value, 'in', 0, 0, tiled=True)]
    all_to_all x11 -> x9, starting transfers between devices: 45.1 us -> 43.2 us  [on_depth(): value = lax.all_to_all(value, 'in', 0, 0, tiled=True)]
  transfers between devices with their start and end apart: 88 -> 89, of which waited for: 50 -> 40; matrix products, arithmetic and copies ran while one was open for 22% -> 21% of each run, Pallas kernels for 9% -> 10%
where the time goes in v3:
time: 541 us; the launch traced here: 530 us
  waiting for transfers between devices  182 us (34%)
  starting transfers between devices  147 us (27%)
  other arithmetic  57.2 us (11%)
  Pallas kernels  51.1 us (9%)
  matrix products  41.8 us (8%)
  local copies, waits for them, and re-layouts  35.7 us (7%)
  between operations  16.2 us (3%)
    ppermute x79, waiting for transfers between devices, send(): lax.ppermute(value, axes, pair)  124 us
    ppermute x79, starting transfers between devices, send(): lax.ppermute(value, axes, pair)  104 us
    all_to_all x9, waiting for transfers between devices, on_depth(): value = lax.all_to_all(value, 'in', 0, 0, tiled=True)  58.1 us
    all_to_all x9, starting transfers between devices, on_depth(): value = lax.all_to_all(value, 'in', 0, 0, tiled=True)  43.2 us
    dot_general x13, matrix products, dot_nt(): lax.dot_general(left, right, (((1,), (1,)), ((), ())), preferred_element_...  20 us
    pallas_call x2, Pallas kernels, column_kernel(): pl.pallas_call(body, grid=(1,), out_shape=(jax.ShapeDtypeStruct(shape, F3...  14.9 us
    dot_general x8, matrix products, dot(): return jnp.dot(left, right, preferred_element_type=F32)  11.3 us
  transfers between devices with their start and end apart: 89, of which 40 were waited for; matrix products, arithmetic and copies ran while one was open for 21% of the time, Pallas kernels for 10%

profile of v3, /device:TPU:0, one launch (start us, length us, event | category | flops | bytes accessed | tf_op | source)
XLA Modules:
  0.0 530.5 jit_solution(11374555772881714592)
XLA Ops:
  11.9 6.4 %all-to-all-start = ((bf16[4,256,384]{2,1,0:T(8,128)(2,1)}), bf16[4,256,384]{2,1,0:T(8,128)(2,1)S(1)}, u32[]{:S(2)}, u32[]{:S(2)}) async-start(bf16[4,256,384]{2,1,0:T(8,128)(2,1)} %broadcast_in_dim.30), calls=%async_computation | async-start | bytes 1572864 | tf_op jit(solution)/shard_map/all_to_all | solution.py:313
  20.7 24.8 %all-to-all-done = bf16[4,256,384]{2,1,0:T(8,128)(2,1)S(1)} async-done(((bf16[4,256,384]{2,1,0:T(8,128)(2,1)}), bf16[4,256,384]{2,1,0:T(8,128)(2,1)S(1)}, u32[]{:S(2)}, u32[]{:S(2)}) %all-to-all-start) | async-done | bytes 786464 | tf_op jit(solution)/shard_map/all_to_all | solution.py:313
  55.7 13.4 %collective-permute-done.5 = bf16[1024,384]{1,0:T(8,128)(2,1)S(1)} collective-permute-done((bf16[1024,384]{1,0:T(8,128)(2,1)S(1)}, bf16[1024,384]{1,0:T(8,128)(2,1)S(1)}, u32[]{:S(2)}, u32[]{:S(2)}) %collective-permute-start.5) | collective-permute-done | bytes 786464 | tf_op jit(solution)/shard_map/ppermute | solution.py:292
  82.6 5.8 %all-to-all-done.2 = bf16[4,140,256]{2,1,0:T(8,128)(2,1)S(1)} async-done(((bf16[4,140,256]{2,1,0:T(8,128)(2,1)}), bf16[4,140,256]{2,1,0:T(8,128)(2,1)S(1)}, u32[]{:S(2)}, u32[]{:S(2)}) %all-to-all-start.2) | async-done | bytes 286752 | tf_op jit(solution)/shard_map/all_to_all | solution.py:313
  103.6 7.4 %collective-permute-done.10.refs_1_ = bf16[128,1024]{1,0:T(8,128)(2,1)S(1)} collective-permute-done((bf16[128,1024]{1,0:T(8,128)(2,1)S(1)}, bf16[128,1024]{1,0:T(8,128)(2,1)S(1)}, u32[]{:S(2)}, u32[]{:S(2)}) %collective-permute-start.10) | collective-permute-done | bytes 262176 | tf_op jit(solution)/shard_map/ppermute | solution.py:292
  125.1 7.1 %attention_forward.1.attended_ref = bf16[256,512]{1,0:T(8,128)(2,1)} custom-call(bf16[256,1536]{1,0:T(8,128)(2,1)} %fusion.27.qkv_ref, f32[2,128,128]{2,1,0:T(8,128)} %and_select_fusion.bias_ref), custom_call_target="tpu_custom_call" | custom-call | tf_op jit(solution)/shard_map/attention_forward/pallas_call | solution.py:70
  143.6 5.7 %collective-permute-done.21.refs_1_ = bf16[128,1024]{1,0:T(8,128)(2,1)S(1)} collective-permute-done((bf16[128,1024]{1,0:T(8,128)(2,1)S(1)}, bf16[128,1024]{1,0:T(8,128)(2,1)S(1)}, u32[]{:S(2)}, u32[]{:S(2)}) %collective-permute-start.21) | collective-permute-done | bytes 262176 | tf_op jit(solution)/shard_map/ppermute | solution.py:292
  149.3 5.6 %collective-permute-done.22.refs_2_ = bf16[128,1024]{1,0:T(8,128)(2,1)S(1)} collective-permute-done((bf16[128,1024]{1,0:T(8,128)(2,1)S(1)}, bf16[128,1024]{1,0:T(8,128)(2,1)S(1)}, u32[]{:S(2)}, u32[]{:S(2)}) %collective-permute-start.22) | collective-permute-done | bytes 262176 | tf_op jit(solution)/shard_map/ppermute | solution.py:292
  183.3 5.6 %all-to-all-start.4 = ((bf16[4,512,512]{2,1,0:T(8,128)(2,1)}), bf16[4,512,512]{2,1,0:T(8,128)(2,1)}, u32[]{:S(2)}, u32[]{:S(2)}) async-start(bf16[4,512,512]{2,1,0:T(8,128)(2,1)} %pad_maximum_fusion), calls=%async_computation.4 | async-start | bytes 4194304 | tf_op jit(solution)/shard_map/all_to_all | solution.py:313
  199.8 9.5 %attention_backward.1.heads_ref = bf16[256,1536]{1,0:T(8,128)(2,1)} custom-call(bf16[256,1536]{1,0:T(8,128)(2,1)} %fusion.27.qkv_ref, f32[2,128,128]{2,1,0:T(8,128)} %and_select_fusion.bias_ref, bf16[256,512]{1,0:T(8,128)(2,1)} %convolution_convert_fusion.2.grad_ref), custom_call_target="tpu_custom_call" | custom-call | tf_op jit(solution)/shard_map/attention_backward/pallas_call | solution.py:116
  226.5 10.4 %all-to-all-done.4 = bf16[4,512,512]{2,1,0:T(8,128)(2,1)} async-done(((bf16[4,512,512]{2,1,0:T(8,128)(2,1)}), bf16[4,512,512]{2,1,0:T(8,128)(2,1)}, u32[]{:S(2)}, u32[]{:S(2)}) %all-to-all-start.4) | async-done | bytes 2097184 | tf_op jit(solution)/shard_map/all_to_all | solution.py:313
  257.8 13.1 %all-to-all-done.5 = bf16[4,256,512]{2,1,0:T(8,128)(2,1)S(1)} async-done(((bf16[4,256,512]{2,1,0:T(8,128)(2,1)}), bf16[4,256,512]{2,1,0:T(8,128)(2,1)S(1)}, u32[]{:S(2)}, u32[]{:S(2)}) %all-to-all-start.5) | async-done | bytes 1048608 | tf_op jit(solution)/shard_map/all_to_all | solution.py:313
  270.9 6.6 %column_terms.2 = (f32[1024,640]{1,0:T(8,128)S(1)}, bf16[1024,640]{1,0:T(8,128)(2,1)}) custom-call(s32[6]{0:T(128)S(1)} %copy-done.7, bf16[1024,512]{1,0:T(8,128)(2,1)S(1)} %bitcast.108, bf16[32,4,256,128]{3,2,1,0:T(8,128)(2,1)} %bitcast.118, f32[512,1024]{1,0:T(8,128)S(1)} %copy-done.3), custom_call_target="tpu_custom_call" | custom-call | tf_op jit(solution)/shard_map/column_terms/pallas_call | solution.py:210
  282.0 5.2 all-to-all-start.6
  359.7 8.3 %column_terms.3 = (f32[1024,768]{1,0:T(8,128)S(1)}, bf16[1024,768]{1,0:T(8,128)(2,1)}) custom-call(s32[6]{0:T(128)S(1)} %copy-done.7, bf16[1024,512]{1,0:T(8,128)(2,1)S(1)} %bitcast.113, bf16[32,4,256,128]{3,2,1,0:T(8,128)(2,1)} %bitcast.119, bf16[32,4,256,128]{3,2,1,0:T(8,128)(2,1)} %bitcast.120, f32[384,768]{1,0:T(8,128)S(1)} %copy-done.5, ...), custom_call_target="tpu_custom_call" | custom-call | tf_op jit(solution)/shard_map/column_terms/pallas_call | solution.py:210
  376.8 7.2 %all-to-all-start.8 = ((bf16[4,256,512]{2,1,0:T(8,128)(2,1)}), bf16[4,256,512]{2,1,0:T(8,128)(2,1)S(1)}, u32[]{:S(2)}, u32[]{:S(2)}) async-start(bf16[4,256,512]{2,1,0:T(8,128)(2,1)} %broadcast_in_dim.37), calls=%async_computation.8 | async-start | bytes 2097152 | tf_op jit(solution)/shard_map/all_to_all | solution.py:313
  394.3 18.5 %collective-permute-start.54 = (bf16[256,768]{1,0:T(8,128)(2,1)}, bf16[256,768]{1,0:T(8,128)(2,1)}, u32[]{:S(2)}, u32[]{:S(2)}) collective-permute-start(bf16[256,768]{1,0:T(8,128)(2,1)} %get-tuple-element.158), channel_id=1, source_target_pairs={{0,8},{8,0},{16,24},{24,16},{1,9},{9,1},{17,25},{25,17},{2,10},{10... | collective-permute-start | bytes 1179656 | tf_op jit(solution)/shard_map/ppermute | solution.py:292
  418.5 5.7 %row_terms.1 = (f32[5120,128]{1,0:T(8,128)S(1)}, bf16[5120,128]{1,0:T(8,128)(2,1)S(1)}) custom-call(s32[6]{0:T(128)S(1)} %copy-done.7, bf16[1024,512]{1,0:T(8,128)(2,1)S(1)} %bitcast.116, bf16[32,4,256,128]{3,2,1,0:T(8,128)(2,1)} %bitcast.121, f32[1024,512]{1,0:T(8,128)S(1)} %copy-done.4), custom_call_target="tpu_custom_call" | custom-call | tf_op jit(solution)/shard_map/row_terms/pallas_call | solution.py:262
  424.3 6.2 %collective-permute-done.55 = bf16[256,768]{1,0:T(8,128)(2,1)} collective-permute-done((bf16[256,768]{1,0:T(8,128)(2,1)}, bf16[256,768]{1,0:T(8,128)(2,1)}, u32[]{:S(2)}, u32[]{:S(2)}) %collective-permute-start.55) | collective-permute-done | bytes 393248 | tf_op jit(solution)/shard_map/ppermute | solution.py:292
  440.8 14.9 %collective-permute-done.57 = bf16[512,512]{1,0:T(8,128)(2,1)S(1)} collective-permute-done((bf16[512,512]{1,0:T(8,128)(2,1)S(1)}, bf16[512,512]{1,0:T(8,128)(2,1)S(1)}, u32[]{:S(2)}, u32[]{:S(2)}) %collective-permute-start.57) | collective-permute-done | bytes 524320 | tf_op jit(solution)/shard_map/ppermute | solution.py:292
  462.1 5.2 collective-permute-done.59
  475.9 6.7 %collective-permute-done.65 = bf16[1280,128]{1,0:T(8,128)(2,1)S(1)} collective-permute-done((bf16[1280,128]{1,0:T(8,128)(2,1)S(1)}, bf16[1280,128]{1,0:T(8,128)(2,1)S(1)}, u32[]{:S(2)}, u32[]{:S(2)}) %collective-permute-start.65) | collective-permute-done | bytes 327712 | tf_op jit(solution)/shard_map/ppermute | solution.py:292
  482.5 5.2 collective-permute-done.66
  491.5 6.9 %collective-permute-done.68 = bf16[512,512]{1,0:T(8,128)(2,1)S(1)} collective-permute-done((bf16[512,512]{1,0:T(8,128)(2,1)S(1)}, bf16[512,512]{1,0:T(8,128)(2,1)S(1)}, u32[]{:S(2)}, u32[]{:S(2)}) %collective-permute-start.68) | collective-permute-done | bytes 524320 | tf_op jit(solution)/shard_map/ppermute | solution.py:292
  (551 shorter events, 302.9 us)
Async XLA Ops:
  11.9 33.5 %all-to-all-start = ((bf16[4,256,384]{2,1,0:T(8,128)(2,1)}), bf16[4,256,384]{2,1,0:T(8,128)(2,1)S(1)}, u32[]{:S(2)}, u32[]{:S(2)}) async-start(bf16[4,256,384]{2,1,0:T(8,128)(2,1)} %broadcast_in_dim.30), calls=%async_computation | async-start | bytes 1572864 | tf_op jit(solution)/shard_map/all_to_all | solution.py:313
  18.5 37.1 %collective-permute-start.1 = (bf16[128,128]{1,0:T(8,128)(2,1)S(1)}, bf16[128,128]{1,0:T(8,128)(2,1)S(1)}, u32[]{:S(2)}, u32[]{:S(2)}) collective-permute-start(bf16[128,128]{1,0:T(8,128)(2,1)S(1)} %select_bitcast_fusion.2), channel_id=1, source_target_pairs={{0,4},{4,0},{1,5},{5,1},{2,6},{6,2},{3,7},{7,3},{8,12},{12,8},{9,1... | collective-permute-start | bytes 98312 | tf_op jit(solution)/shard_map/ppermute | solution.py:292
  19.0 36.5 %collective-permute-start = (bf16[128,1024]{1,0:T(8,128)(2,1)S(1)}, bf16[128,1024]{1,0:T(8,128)(2,1)S(1)}, u32[]{:S(2)}, u32[]{:S(2)}) collective-permute-start(bf16[128,1024]{1,0:T(8,128)(2,1)S(1)} %copy-done.26), channel_id=1, source_target_pairs={{0,4},{4,0},{1,5},{5,1},{2,6},{6,2},{3,7},{7,3},{8,12},{12,8},{9,1... | collective-permute-start | bytes 786440 | tf_op jit(solution)/shard_map/ppermute | solution.py:292
  19.8 31.1 %collective-permute-start.4 = (bf16[256,512]{0,1:T(8,128)(2,1)S(1)}, bf16[256,512]{0,1:T(8,128)(2,1)S(1)}, u32[]{:S(2)}, u32[]{:S(2)}) collective-permute-start(bf16[256,512]{0,1:T(8,128)(2,1)S(1)} %maximum_bitcast_fusion), channel_id=1, source_target_pairs={{0,0},{1,8},{2,16},{3,24},{8,1},{9,9},{10,17},{11,25},{16,2},{17,1... | collective-permute-start | bytes 786440 | tf_op jit(solution)/shard_map/ppermute | solution.py:292
  46.5 28.7 %all-to-all-start.1 = ((bf16[4,256,512]{2,1,0:T(8,128)(2,1)}), bf16[4,256,512]{2,1,0:T(8,128)(2,1)}, u32[]{:S(2)}, u32[]{:S(2)}) async-start(bf16[4,256,512]{2,1,0:T(8,128)(2,1)} %broadcast_in_dim.29), calls=%async_computation.1 | async-start | bytes 2097152 | tf_op jit(solution)/shard_map/all_to_all | solution.py:313
  79.3 191.5 %all-gather.3.cloned.1.call-start = ((), (), s32[]{:S(2)}) async-start(), calls=%async_computation.9 | async-start | bytes 8650752 | tf_op jit(solution)/shard_map/all_gather | solution.py:556
  96.3 39.0 %all-to-all-start.3 = ((bf16[4,256,512]{2,1,0:T(8,128)(2,1)}), bf16[4,256,512]{2,1,0:T(8,128)(2,1)S(1)}, u32[]{:S(2)}, u32[]{:S(2)}) async-start(bf16[4,256,512]{2,1,0:T(8,128)(2,1)} %broadcast_in_dim.34), calls=%async_computation.3 | async-start | bytes 2097152 | tf_op jit(solution)/shard_map/all_to_all | solution.py:313
  183.3 53.7 %all-to-all-start.4 = ((bf16[4,512,512]{2,1,0:T(8,128)(2,1)}), bf16[4,512,512]{2,1,0:T(8,128)(2,1)}, u32[]{:S(2)}, u32[]{:S(2)}) async-start(bf16[4,512,512]{2,1,0:T(8,128)(2,1)} %pad_maximum_fusion), calls=%async_computation.4 | async-start | bytes 4194304 | tf_op jit(solution)/shard_map/all_to_all | solution.py:313
  220.8 34.7 %collective-permute-start.51 = (f32[128,1024]{1,0:T(8,128)}, f32[128,1024]{1,0:T(8,128)}, u32[]{:S(2)}, u32[]{:S(2)}) collective-permute-start(f32[128,1024]{1,0:T(8,128)} %fusion.39), channel_id=1, source_target_pairs={{0,4},{4,0},{1,5},{5,1},{2,6},{6,2},{3,7},{7,3},{8,12},{12,8},{9,1... | collective-permute-start | bytes 1572872 | tf_op jit(solution)/shard_map/ppermute | solution.py:292
  222.0 26.5 %collective-permute-start.34 = (bf16[512,512]{1,0:T(8,128)(2,1)}, bf16[512,512]{1,0:T(8,128)(2,1)}, u32[]{:S(2)}, u32[]{:S(2)}) collective-permute-start(bf16[512,512]{1,0:T(8,128)(2,1)} %get-tuple-element.133), channel_id=1, source_target_pairs={{0,8},{8,0},{16,24},{24,16},{1,9},{9,1},{17,25},{25,17},{2,10},{10... | collective-permute-start | bytes 1572872 | tf_op jit(solution)/shard_map/ppermute | solution.py:292
  222.3 28.6 %collective-permute-start.33 = (bf16[512,512]{1,0:T(8,128)(2,1)}, bf16[512,512]{1,0:T(8,128)(2,1)}, u32[]{:S(2)}, u32[]{:S(2)}) collective-permute-start(bf16[512,512]{1,0:T(8,128)(2,1)} %get-tuple-element.131), channel_id=1, source_target_pairs={{0,16},{8,24},{16,0},{24,8},{1,17},{9,25},{17,1},{25,9},{2,18},{10... | collective-permute-start | bytes 1572872 | tf_op jit(solution)/shard_map/ppermute | solution.py:292
  242.0 28.8 %all-to-all-start.5 = ((bf16[4,256,512]{2,1,0:T(8,128)(2,1)}), bf16[4,256,512]{2,1,0:T(8,128)(2,1)S(1)}, u32[]{:S(2)}, u32[]{:S(2)}) async-start(bf16[4,256,512]{2,1,0:T(8,128)(2,1)} %broadcast_in_dim.35), calls=%async_computation.5 | async-start | bytes 2097152 | tf_op jit(solution)/shard_map/all_to_all | solution.py:313
  253.4 24.6 %collective-permute-start.35 = (bf16[1024,512]{1,0:T(8,128)(2,1)}, bf16[1024,512]{1,0:T(8,128)(2,1)}, u32[]{:S(2)}, u32[]{:S(2)}) collective-permute-start(bf16[1024,512]{1,0:T(8,128)(2,1)} %pad_maximum_fusion.2), channel_id=1, source_target_pairs={{0,8},{8,0},{16,24},{24,16},{1,9},{9,1},{17,25},{25,17},{2,10},{10... | collective-permute-start | bytes 3145736 | tf_op jit(solution)/shard_map/ppermute | solution.py:292
  254.8 24.2 %collective-permute-start.36 = (bf16[1024,512]{1,0:T(8,128)(2,1)}, bf16[1024,512]{1,0:T(8,128)(2,1)}, u32[]{:S(2)}, u32[]{:S(2)}) collective-permute-start(bf16[1024,512]{1,0:T(8,128)(2,1)} %pad_maximum_fusion.3), channel_id=1, source_target_pairs={{0,16},{8,24},{16,0},{24,8},{1,17},{9,25},{17,1},{25,9},{2,18},{10... | collective-permute-start | bytes 3145736 | tf_op jit(solution)/shard_map/ppermute | solution.py:292
  282.0 29.9 %all-to-all-start.6 = ((bf16[4,256,512]{2,1,0:T(8,128)(2,1)}), bf16[4,256,512]{2,1,0:T(8,128)(2,1)S(1)}, u32[]{:S(2)}, u32[]{:S(2)}) async-start(bf16[4,256,512]{2,1,0:T(8,128)(2,1)} %bitcast.16), calls=%async_computation.6 | async-start | bytes 2097152 | tf_op jit(solution)/shard_map/all_to_all | solution.py:313
  318.1 25.6 %collective-permute-start.43 = (bf16[512,1024]{1,0:T(8,128)(2,1)}, bf16[512,1024]{1,0:T(8,128)(2,1)}, u32[]{:S(2)}, u32[]{:S(2)}) collective-permute-start(bf16[512,1024]{1,0:T(8,128)(2,1)} %convolution_convert_fusion.1), channel_id=1, source_target_pairs={{0,4},{4,0},{1,5},{5,1},{2,6},{6,2},{3,7},{7,3},{8,12},{12,8},{9,1... | collective-permute-start | bytes 3145736 | tf_op jit(solution)/shard_map/ppermute | solution.py:292
  326.1 33.6 %all-to-all-start.7 = ((bf16[4,256,512]{2,1,0:T(8,128)(2,1)}), bf16[4,256,512]{2,1,0:T(8,128)(2,1)S(1)}, u32[]{:S(2)}, u32[]{:S(2)}) async-start(bf16[4,256,512]{2,1,0:T(8,128)(2,1)} %broadcast_in_dim.36), calls=%async_computation.7 | async-start | bytes 2097152 | tf_op jit(solution)/shard_map/all_to_all | solution.py:313
  368.1 21.2 %collective-permute-start.52 = (bf16[1024,768]{1,0:T(8,128)(2,1)}, bf16[1024,768]{1,0:T(8,128)(2,1)}, u32[]{:S(2)}, u32[]{:S(2)}) collective-permute-start(bf16[1024,768]{1,0:T(8,128)(2,1)} %get-tuple-element.156), channel_id=1, source_target_pairs={{0,4},{4,0},{1,5},{5,1},{2,6},{6,2},{3,7},{7,3},{8,12},{12,8},{9,1... | collective-permute-start | bytes 4718600 | tf_op jit(solution)/shard_map/ppermute | solution.py:292
  376.8 40.1 %all-to-all-start.8 = ((bf16[4,256,512]{2,1,0:T(8,128)(2,1)}), bf16[4,256,512]{2,1,0:T(8,128)(2,1)S(1)}, u32[]{:S(2)}, u32[]{:S(2)}) async-start(bf16[4,256,512]{2,1,0:T(8,128)(2,1)} %broadcast_in_dim.37), calls=%async_computation.8 | async-start | bytes 2097152 | tf_op jit(solution)/shard_map/all_to_all | solution.py:313
  394.3 30.0 %collective-permute-start.54 = (bf16[256,768]{1,0:T(8,128)(2,1)}, bf16[256,768]{1,0:T(8,128)(2,1)}, u32[]{:S(2)}, u32[]{:S(2)}) collective-permute-start(bf16[256,768]{1,0:T(8,128)(2,1)} %get-tuple-element.158), channel_id=1, source_target_pairs={{0,8},{8,0},{16,24},{24,16},{1,9},{9,1},{17,25},{25,17},{2,10},{10... | collective-permute-start | bytes 1179656 | tf_op jit(solution)/shard_map/ppermute | solution.py:292
  424.2 37.5 %collective-permute-start.64 = (bf16[5120,128]{1,0:T(8,128)(2,1)S(1)}, bf16[5120,128]{1,0:T(8,128)(2,1)S(1)}, u32[]{:S(2)}, u32[]{:S(2)}) collective-permute-start(bf16[5120,128]{1,0:T(8,128)(2,1)S(1)} %get-tuple-element.167), channel_id=1, source_target_pairs={{0,4},{4,0},{1,5},{5,1},{2,6},{6,2},{3,7},{7,3},{8,12},{12,8},{9,1... | collective-permute-start | bytes 3932168 | tf_op jit(solution)/shard_map/ppermute | solution.py:292
  433.3 22.4 %collective-permute-start.57 = (bf16[512,512]{1,0:T(8,128)(2,1)S(1)}, bf16[512,512]{1,0:T(8,128)(2,1)S(1)}, u32[]{:S(2)}, u32[]{:S(2)}) collective-permute-start(bf16[512,512]{1,0:T(8,128)(2,1)S(1)} %bitcast.128), channel_id=1, source_target_pairs={{0,8},{9,1},{18,26},{27,19},{4,12},{13,5},{22,30},{31,23}} | collective-permute-start | bytes 1572872 | tf_op jit(solution)/shard_map/ppermute | solution.py:292
  436.9 18.9 %collective-permute-start.58 = (bf16[512,512]{1,0:T(8,128)(2,1)S(1)}, bf16[512,512]{1,0:T(8,128)(2,1)S(1)}, u32[]{:S(2)}, u32[]{:S(2)}) collective-permute-start(bf16[512,512]{1,0:T(8,128)(2,1)S(1)} %bitcast.127), channel_id=1, source_target_pairs={{0,16},{9,25},{18,2},{27,11},{4,20},{13,29},{22,6},{31,15}} | collective-permute-start | bytes 1572872 | tf_op jit(solution)/shard_map/ppermute | solution.py:292
  475.8 38.3 %collective-permute-start.61 = (bf16[1024,512]{1,0:T(8,128)(2,1)S(1)}, bf16[1024,512]{1,0:T(8,128)(2,1)S(1)}, u32[]{:S(2)}, u32[]{:S(2)}) collective-permute-start(bf16[1024,512]{1,0:T(8,128)(2,1)S(1)} %pad_maximum_fusion.4), channel_id=1, source_target_pairs={{0,4},{4,0},{1,5},{5,1},{2,6},{6,2},{3,7},{7,3},{8,12},{12,8},{9,1... | collective-permute-start | bytes 3145736 | tf_op jit(solution)/shard_map/ppermute | solution.py:292
  (164 other events, 1480.8 us)
Sparse Core Ops, SparseCore 0:
  95.2 87.4 all-gather.2

commit v4 on v3

--- a/solution.py
+++ b/solution.py
@@ -384,7 +384,9 @@
         return jnp.concatenate([low, high])
 
     def gather_tokens(self, value):
-        mine = self.gather_plane(value)
+        return self.join_cores(self.gather_plane(value))
+
+    def join_cores(self, mine):
         return join(mine + [self.swap_core(part) for part in mine])
 
     def reduce_tokens(self, mine, theirs):
@@ -510,9 +512,10 @@
         here.by_core(here.mine(out_split), here.swap_core(here.theirs(out_split))), axis=1
     )
 
-    proj_turned = here.transpose_chips(proj_share.T, "plane")
-    qkv_parts = here.gather_plane(here.gather_depth(qkv_share).reshape(width, -1))
-    plane_cotangent = here.gather_tokens(cotangent)
+    cotangent_pieces = here.gather_plane(cotangent)
+    proj_turned = here.transpose_chips(proj_share.T, None)
+    qkv_rows = here.gather_depth(qkv_share).reshape(width, -1)
+    qkv_parts = here.gather_plane(here.after(qkv_rows, proj_turned, *cotangent_pieces))
     fc_full = here.gather_depth(fc_share).reshape(width, -1)
     small_share = jnp.concatenate(
         [out_share, vectors.astype(BF16).reshape(-1, out_share.shape[1])]
@@ -564,11 +567,13 @@
         ALL,
     )
     attended = attention_forward(projected, mask)
-    attended = here.after(attended, plane_cotangent, proj_full)
+    attended = here.after(attended, proj_full)
     branch = dot(attended[:length], out_full) + here.swap_core(dot(attended[length:], out_full))
     middle = inputs[:length] + (branch + bias_out)
     scaled_two, spread_two = norm_parts(middle)
+    plane_cotangent = here.join_cores(cotangent_pieces)
     normed_two = here.gather_tokens((scaled_two * gain_two + shift_two).astype(BF16))
+    normed_two = here.after(normed_two, plane_cotangent)
     pre_act = dot(normed_two, fc_full) + bias_fc
     activated = gelu(pre_act).astype(BF16)
 
@@ -765,6 +770,7 @@
             jnp.sum(grad_top, axis=0),
         ]
     )
+    vector_terms = here.after(vector_terms, first_own)
     vector_sum = here.swap_core(vector_terms) + vector_terms
     vector_sum = vector_sum.reshape(depth, -1, 128)
     steps = range(1, depth)

time: 541 us -> 538 us (level)
  starting transfers between devices: 147 us -> 131 us
  waiting for transfers between devices: 182 us -> 198 us
    ppermute x79, starting transfers between devices: 104 us -> 90.4 us  [send(): lax.ppermute(value, axes, pair)]
    ppermute x79, waiting for transfers between devices: 124 us -> 134 us  [send(): lax.ppermute(value, axes, pair)]
    all_to_all x9, waiting for transfers between devices: 58.1 us -> 64.4 us  [on_depth(): value = lax.all_to_all(value, 'in', 0, 0, tiled=True)]
    unnamed x206 -> x224, local copies, waits for them, and re-layouts: 10.3 us -> 11.5 us
  transfers between devices with their start and end apart: 89 -> 89, of which waited for: 40 -> 45; matrix products, arithmetic and copies ran while one was open for 21% -> 20% of each run, Pallas kernels for 10% -> 10%
where the time goes in v4:
time: 538 us; the launch traced here: 528 us
  waiting for transfers between devices  198 us (37%)
  starting transfers between devices  131 us (24%)
  other arithmetic  55.7 us (10%)
  Pallas kernels  51 us (9%)
  matrix products  41.5 us (8%)
  local copies, waits for them, and re-layouts  34.8 us (6%)
  between operations  16.4 us (3%)
    ppermute x79, waiting for transfers between devices, send(): lax.ppermute(value, axes, pair)  134 us
    ppermute x79, starting transfers between devices, send(): lax.ppermute(value, axes, pair)  90.4 us
    all_to_all x9, waiting for transfers between devices, on_depth(): value = lax.all_to_all(value, 'in', 0, 0, tiled=True)  64.4 us
    all_to_all x9, starting transfers between devices, on_depth(): value = lax.all_to_all(value, 'in', 0, 0, tiled=True)  40.4 us
    dot_general x13, matrix products, dot_nt(): lax.dot_general(left, right, (((1,), (1,)), ((), ())), preferred_element_...  19.7 us
    pallas_call x2, Pallas kernels, column_kernel(): pl.pallas_call(body, grid=(1,), out_shape=(jax.ShapeDtypeStruct(shape, F3...  14.8 us
    unnamed x224, local copies, waits for them, and re-layouts  11.5 us
    dot_general x8, matrix products, dot(): return jnp.dot(left, right, preferred_element_type=F32)  11.3 us
  transfers between devices with their start and end apart: 89, of which 45 were waited for; matrix products, arithmetic and copies ran while one was open for 20% of the time, Pallas kernels for 10%

profile of v4, /device:TPU:0, one launch (start us, length us, event | category | flops | bytes accessed | tf_op | source)
XLA Modules:
  0.0 528.5 jit_solution(14548377655926876823)
XLA Ops:
  11.9 6.4 %all-to-all-start = ((bf16[4,256,384]{2,1,0:T(8,128)(2,1)}), bf16[4,256,384]{2,1,0:T(8,128)(2,1)S(1)}, u32[]{:S(2)}, u32[]{:S(2)}) async-start(bf16[4,256,384]{2,1,0:T(8,128)(2,1)} %broadcast_in_dim.30), calls=%async_computation | async-start | bytes 1572864 | tf_op jit(solution)/shard_map/all_to_all | solution.py:313
  24.2 21.3 %all-to-all-done = bf16[4,256,384]{2,1,0:T(8,128)(2,1)S(1)} async-done(((bf16[4,256,384]{2,1,0:T(8,128)(2,1)}), bf16[4,256,384]{2,1,0:T(8,128)(2,1)S(1)}, u32[]{:S(2)}, u32[]{:S(2)}) %all-to-all-start) | async-done | bytes 786464 | tf_op jit(solution)/shard_map/all_to_all | solution.py:313
  55.5 16.3 %collective-permute-done.8 = bf16[1024,384]{1,0:T(8,128)(2,1)S(1)} collective-permute-done((bf16[1024,384]{1,0:T(8,128)(2,1)S(1)}, bf16[1024,384]{1,0:T(8,128)(2,1)S(1)}, u32[]{:S(2)}, u32[]{:S(2)}) %collective-permute-start.8) | collective-permute-done | bytes 786464 | tf_op jit(solution)/shard_map/ppermute | solution.py:292
  76.8 5.0 all-to-all-start.2
  107.6 7.1 %attention_forward.1.attended_ref = bf16[256,512]{1,0:T(8,128)(2,1)} custom-call(bf16[256,1536]{1,0:T(8,128)(2,1)} %fusion.27.qkv_ref, f32[2,128,128]{2,1,0:T(8,128)} %and_select_fusion.bias_ref), custom_call_target="tpu_custom_call" | custom-call | tf_op jit(solution)/shard_map/attention_forward/pallas_call | solution.py:70
  121.8 9.2 %all-to-all-done.3 = bf16[4,256,512]{2,1,0:T(8,128)(2,1)S(1)} async-done(((bf16[4,256,512]{2,1,0:T(8,128)(2,1)}), bf16[4,256,512]{2,1,0:T(8,128)(2,1)S(1)}, u32[]{:S(2)}, u32[]{:S(2)}) %all-to-all-start.3) | async-done | bytes 1048608 | tf_op jit(solution)/shard_map/all_to_all | solution.py:313
  139.9 6.5 %collective-permute-done.17.refs_1_ = bf16[128,1024]{1,0:T(8,128)(2,1)S(1)} collective-permute-done((bf16[128,1024]{1,0:T(8,128)(2,1)S(1)}, bf16[128,1024]{1,0:T(8,128)(2,1)S(1)}, u32[]{:S(2)}, u32[]{:S(2)}) %collective-permute-start.17) | collective-permute-done | bytes 262176 | tf_op jit(solution)/shard_map/ppermute | solution.py:292
  147.0 5.7 %collective-permute-done.19.refs_3_ = bf16[128,1024]{1,0:T(8,128)(2,1)S(1)} collective-permute-done((bf16[128,1024]{1,0:T(8,128)(2,1)S(1)}, bf16[128,1024]{1,0:T(8,128)(2,1)S(1)}, u32[]{:S(2)}, u32[]{:S(2)}) %collective-permute-start.19) | collective-permute-done | bytes 262176 | tf_op jit(solution)/shard_map/ppermute | solution.py:292
  198.9 9.5 %attention_backward.1.heads_ref = bf16[256,1536]{1,0:T(8,128)(2,1)} custom-call(bf16[256,1536]{1,0:T(8,128)(2,1)} %fusion.27.qkv_ref, f32[2,128,128]{2,1,0:T(8,128)} %and_select_fusion.bias_ref, bf16[256,512]{1,0:T(8,128)(2,1)} %convolution_convert_fusion.2.grad_ref), custom_call_target="tpu_custom_call" | custom-call | tf_op jit(solution)/shard_map/attention_backward/pallas_call | solution.py:116
  227.1 8.3 %all-to-all-done.4 = bf16[4,512,512]{2,1,0:T(8,128)(2,1)} async-done(((bf16[4,512,512]{2,1,0:T(8,128)(2,1)}), bf16[4,512,512]{2,1,0:T(8,128)(2,1)}, u32[]{:S(2)}, u32[]{:S(2)}) %all-to-all-start.4) | async-done | bytes 2097184 | tf_op jit(solution)/shard_map/all_to_all | solution.py:313
  255.7 13.4 %all-to-all-done.5 = bf16[4,256,512]{2,1,0:T(8,128)(2,1)S(1)} async-done(((bf16[4,256,512]{2,1,0:T(8,128)(2,1)}), bf16[4,256,512]{2,1,0:T(8,128)(2,1)S(1)}, u32[]{:S(2)}, u32[]{:S(2)}) %all-to-all-start.5) | async-done | bytes 1048608 | tf_op jit(solution)/shard_map/all_to_all | solution.py:313
  269.2 6.6 %column_terms.2 = (f32[1024,640]{1,0:T(8,128)S(1)}, bf16[1024,640]{1,0:T(8,128)(2,1)}) custom-call(s32[6]{0:T(128)S(1)} %copy-done.7, bf16[1024,512]{1,0:T(8,128)(2,1)S(1)} %bitcast.108, bf16[32,4,256,128]{3,2,1,0:T(8,128)(2,1)} %bitcast.118, f32[512,1024]{1,0:T(8,128)S(1)} %copy-done.3), custom_call_target="tpu_custom_call" | custom-call | tf_op jit(solution)/shard_map/column_terms/pallas_call | solution.py:210
  280.2 5.2 all-to-all-start.6
  292.5 6.3 %collective-permute-done.38 = bf16[256,640]{1,0:T(8,128)(2,1)S(1)} collective-permute-done((bf16[256,640]{1,0:T(8,128)(2,1)S(1)}, bf16[256,640]{1,0:T(8,128)(2,1)S(1)}, u32[]{:S(2)}, u32[]{:S(2)}) %collective-permute-start.38) | collective-permute-done | bytes 327712 | tf_op jit(solution)/shard_map/ppermute | solution.py:292
  327.3 6.8 %collective-permute-done.44 = bf16[512,512]{1,0:T(8,128)(2,1)S(1)} collective-permute-done((bf16[512,512]{1,0:T(8,128)(2,1)S(1)}, bf16[512,512]{1,0:T(8,128)(2,1)S(1)}, u32[]{:S(2)}, u32[]{:S(2)}) %collective-permute-start.44) | collective-permute-done | bytes 524320 | tf_op jit(solution)/shard_map/ppermute | solution.py:292
  344.3 6.3 %collective-permute-done.46 = bf16[512,512]{1,0:T(8,128)(2,1)S(1)} collective-permute-done((bf16[512,512]{1,0:T(8,128)(2,1)S(1)}, bf16[512,512]{1,0:T(8,128)(2,1)S(1)}, u32[]{:S(2)}, u32[]{:S(2)}) %collective-permute-start.46) | collective-permute-done | bytes 524320 | tf_op jit(solution)/shard_map/ppermute | solution.py:292
  369.9 8.2 %column_terms.3 = (f32[1024,768]{1,0:T(8,128)S(1)}, bf16[1024,768]{1,0:T(8,128)(2,1)}) custom-call(s32[6]{0:T(128)S(1)} %copy-done.7, bf16[1024,512]{1,0:T(8,128)(2,1)S(1)} %bitcast.113, bf16[32,4,256,128]{3,2,1,0:T(8,128)(2,1)} %bitcast.119, bf16[32,4,256,128]{3,2,1,0:T(8,128)(2,1)} %bitcast.120, f32[384,768]{1,0:T(8,128)S(1)} %copy-done.5, ...), custom_call_target="tpu_custom_call" | custom-call | tf_op jit(solution)/shard_map/column_terms/pallas_call | solution.py:210
  418.1 5.7 %row_terms.1 = (f32[5120,128]{1,0:T(8,128)S(1)}, bf16[5120,128]{1,0:T(8,128)(2,1)S(1)}) custom-call(s32[6]{0:T(128)S(1)} %copy-done.7, bf16[1024,512]{1,0:T(8,128)(2,1)S(1)} %bitcast.116, bf16[32,4,256,128]{3,2,1,0:T(8,128)(2,1)} %bitcast.121, f32[1024,512]{1,0:T(8,128)S(1)} %copy-done.4), custom_call_target="tpu_custom_call" | custom-call | tf_op jit(solution)/shard_map/row_terms/pallas_call | solution.py:262
  429.2 6.5 %collective-permute-start.57 = (bf16[512,512]{1,0:T(8,128)(2,1)S(1)}, bf16[512,512]{1,0:T(8,128)(2,1)S(1)}, u32[]{:S(2)}, u32[]{:S(2)}) collective-permute-start(bf16[512,512]{1,0:T(8,128)(2,1)S(1)} %bitcast.128), channel_id=1, source_target_pairs={{0,8},{9,1},{18,26},{27,19},{4,12},{13,5},{22,30},{31,23}} | collective-permute-start | bytes 1572872 | tf_op jit(solution)/shard_map/ppermute | solution.py:292
  440.0 13.6 %collective-permute-done.57 = bf16[512,512]{1,0:T(8,128)(2,1)S(1)} collective-permute-done((bf16[512,512]{1,0:T(8,128)(2,1)S(1)}, bf16[512,512]{1,0:T(8,128)(2,1)S(1)}, u32[]{:S(2)}, u32[]{:S(2)}) %collective-permute-start.57) | collective-permute-done | bytes 524320 | tf_op jit(solution)/shard_map/ppermute | solution.py:292
  460.0 5.2 collective-permute-done.59
  473.8 6.7 %collective-permute-done.65 = bf16[1280,128]{1,0:T(8,128)(2,1)S(1)} collective-permute-done((bf16[1280,128]{1,0:T(8,128)(2,1)S(1)}, bf16[1280,128]{1,0:T(8,128)(2,1)S(1)}, u32[]{:S(2)}, u32[]{:S(2)}) %collective-permute-start.65) | collective-permute-done | bytes 327712 | tf_op jit(solution)/shard_map/ppermute | solution.py:292
  480.4 5.3 %collective-permute-done.66 = bf16[1280,128]{1,0:T(8,128)(2,1)S(1)} collective-permute-done((bf16[1280,128]{1,0:T(8,128)(2,1)S(1)}, bf16[1280,128]{1,0:T(8,128)(2,1)S(1)}, u32[]{:S(2)}, u32[]{:S(2)}) %collective-permute-start.66) | collective-permute-done | bytes 327712 | tf_op jit(solution)/shard_map/ppermute | solution.py:292
  489.5 6.9 %collective-permute-done.68 = bf16[512,512]{1,0:T(8,128)(2,1)S(1)} collective-permute-done((bf16[512,512]{1,0:T(8,128)(2,1)S(1)}, bf16[512,512]{1,0:T(8,128)(2,1)S(1)}, u32[]{:S(2)}, u32[]{:S(2)}) %collective-permute-start.68) | collective-permute-done | bytes 524320 | tf_op jit(solution)/shard_map/ppermute | solution.py:292
  (569 shorter events, 314.0 us)
Async XLA Ops:
  11.9 33.5 %all-to-all-start = ((bf16[4,256,384]{2,1,0:T(8,128)(2,1)}), bf16[4,256,384]{2,1,0:T(8,128)(2,1)S(1)}, u32[]{:S(2)}, u32[]{:S(2)}) async-start(bf16[4,256,384]{2,1,0:T(8,128)(2,1)} %broadcast_in_dim.30), calls=%async_computation | async-start | bytes 1572864 | tf_op jit(solution)/shard_map/all_to_all | solution.py:313
  18.3 32.7 %collective-permute-start.5 = (bf16[128,1024]{1,0:T(8,128)(2,1)S(1)}, bf16[128,1024]{1,0:T(8,128)(2,1)S(1)}, u32[]{:S(2)}, u32[]{:S(2)}) collective-permute-start(bf16[128,1024]{1,0:T(8,128)(2,1)S(1)} %copy-done.52), channel_id=1, source_target_pairs={{0,8},{8,0},{16,24},{24,16},{1,9},{9,1},{17,25},{25,17},{2,10},{10... | collective-permute-start | bytes 786440 | tf_op jit(solution)/shard_map/ppermute | solution.py:292
  19.8 31.3 %collective-permute-start.6 = (bf16[128,1024]{1,0:T(8,128)(2,1)S(1)}, bf16[128,1024]{1,0:T(8,128)(2,1)S(1)}, u32[]{:S(2)}, u32[]{:S(2)}) collective-permute-start(bf16[128,1024]{1,0:T(8,128)(2,1)S(1)} %copy-done.52), channel_id=1, source_target_pairs={{0,16},{8,24},{16,0},{24,8},{1,17},{9,25},{17,1},{25,9},{2,18},{10... | collective-permute-start | bytes 786440 | tf_op jit(solution)/shard_map/ppermute | solution.py:292
  21.3 29.8 %collective-permute-start.7 = (bf16[128,1024]{1,0:T(8,128)(2,1)S(1)}, bf16[128,1024]{1,0:T(8,128)(2,1)}, u32[]{:S(2)}, u32[]{:S(2)}) collective-permute-start(bf16[128,1024]{1,0:T(8,128)(2,1)S(1)} %copy-done.52), channel_id=1, source_target_pairs={{0,24},{8,16},{16,8},{24,0},{1,25},{9,17},{17,9},{25,1},{2,26},{10... | collective-permute-start | bytes 786440 | tf_op jit(solution)/shard_map/ppermute | solution.py:292
  22.0 33.3 %collective-permute-start.1 = (bf16[128,128]{1,0:T(8,128)(2,1)S(1)}, bf16[128,128]{1,0:T(8,128)(2,1)S(1)}, u32[]{:S(2)}, u32[]{:S(2)}) collective-permute-start(bf16[128,128]{1,0:T(8,128)(2,1)S(1)} %select_bitcast_fusion.2), channel_id=1, source_target_pairs={{0,4},{4,0},{1,5},{5,1},{2,6},{6,2},{3,7},{7,3},{8,12},{12,8},{9,1... | collective-permute-start | bytes 98312 | tf_op jit(solution)/shard_map/ppermute | solution.py:292
  23.3 27.8 %collective-permute-start.4 = (bf16[256,512]{0,1:T(8,128)(2,1)S(1)}, bf16[256,512]{0,1:T(8,128)(2,1)S(1)}, u32[]{:S(2)}, u32[]{:S(2)}) collective-permute-start(bf16[256,512]{0,1:T(8,128)(2,1)S(1)} %maximum_bitcast_fusion), channel_id=1, source_target_pairs={{0,0},{1,8},{2,16},{3,24},{8,1},{9,9},{10,17},{11,25},{16,2},{17,1... | collective-permute-start | bytes 786440 | tf_op jit(solution)/shard_map/ppermute | solution.py:292
  46.6 29.5 %all-to-all-start.1 = ((bf16[4,256,512]{2,1,0:T(8,128)(2,1)}), bf16[4,256,512]{2,1,0:T(8,128)(2,1)}, u32[]{:S(2)}, u32[]{:S(2)}) async-start(bf16[4,256,512]{2,1,0:T(8,128)(2,1)} %broadcast_in_dim.29), calls=%async_computation.1 | async-start | bytes 2097152 | tf_op jit(solution)/shard_map/all_to_all | solution.py:313
  81.9 187.3 %all-gather.3.cloned.1.call-start = ((), (), s32[]{:S(2)}) async-start(), calls=%async_computation.9 | async-start | bytes 8650752 | tf_op jit(solution)/shard_map/all_gather | solution.py:559
  97.8 33.3 %all-to-all-start.3 = ((bf16[4,256,512]{2,1,0:T(8,128)(2,1)}), bf16[4,256,512]{2,1,0:T(8,128)(2,1)S(1)}, u32[]{:S(2)}, u32[]{:S(2)}) async-start(bf16[4,256,512]{2,1,0:T(8,128)(2,1)} %broadcast_in_dim.34), calls=%async_computation.3 | async-start | bytes 2097152 | tf_op jit(solution)/shard_map/all_to_all | solution.py:313
  182.4 52.9 %all-to-all-start.4 = ((bf16[4,512,512]{2,1,0:T(8,128)(2,1)}), bf16[4,512,512]{2,1,0:T(8,128)(2,1)}, u32[]{:S(2)}, u32[]{:S(2)}) async-start(bf16[4,512,512]{2,1,0:T(8,128)(2,1)} %pad_maximum_fusion), calls=%async_computation.4 | async-start | bytes 4194304 | tf_op jit(solution)/shard_map/all_to_all | solution.py:313
  220.3 33.1 %collective-permute-start.51 = (f32[128,1024]{1,0:T(8,128)}, f32[128,1024]{1,0:T(8,128)}, u32[]{:S(2)}, u32[]{:S(2)}) collective-permute-start(f32[128,1024]{1,0:T(8,128)} %fusion.40), channel_id=1, source_target_pairs={{0,4},{4,0},{1,5},{5,1},{2,6},{6,2},{3,7},{7,3},{8,12},{12,8},{9,1... | collective-permute-start | bytes 1572872 | tf_op jit(solution)/shard_map/ppermute | solution.py:292
  221.5 25.4 %collective-permute-start.34 = (bf16[512,512]{1,0:T(8,128)(2,1)}, bf16[512,512]{1,0:T(8,128)(2,1)}, u32[]{:S(2)}, u32[]{:S(2)}) collective-permute-start(bf16[512,512]{1,0:T(8,128)(2,1)} %get-tuple-element.132), channel_id=1, source_target_pairs={{0,8},{8,0},{16,24},{24,16},{1,9},{9,1},{17,25},{25,17},{2,10},{10... | collective-permute-start | bytes 1572872 | tf_op jit(solution)/shard_map/ppermute | solution.py:292
  222.4 27.0 %collective-permute-start.33 = (bf16[512,512]{1,0:T(8,128)(2,1)}, bf16[512,512]{1,0:T(8,128)(2,1)}, u32[]{:S(2)}, u32[]{:S(2)}) collective-permute-start(bf16[512,512]{1,0:T(8,128)(2,1)} %get-tuple-element.130), channel_id=1, source_target_pairs={{0,16},{8,24},{16,0},{24,8},{1,17},{9,25},{17,1},{25,9},{2,18},{10... | collective-permute-start | bytes 1572872 | tf_op jit(solution)/shard_map/ppermute | solution.py:292
  240.4 28.7 %all-to-all-start.5 = ((bf16[4,256,512]{2,1,0:T(8,128)(2,1)}), bf16[4,256,512]{2,1,0:T(8,128)(2,1)S(1)}, u32[]{:S(2)}, u32[]{:S(2)}) async-start(bf16[4,256,512]{2,1,0:T(8,128)(2,1)} %broadcast_in_dim.35), calls=%async_computation.5 | async-start | bytes 2097152 | tf_op jit(solution)/shard_map/all_to_all | solution.py:313
  251.9 24.4 %collective-permute-start.35 = (bf16[1024,512]{1,0:T(8,128)(2,1)}, bf16[1024,512]{1,0:T(8,128)(2,1)}, u32[]{:S(2)}, u32[]{:S(2)}) collective-permute-start(bf16[1024,512]{1,0:T(8,128)(2,1)} %pad_maximum_fusion.2), channel_id=1, source_target_pairs={{0,8},{8,0},{16,24},{24,16},{1,9},{9,1},{17,25},{25,17},{2,10},{10... | collective-permute-start | bytes 3145736 | tf_op jit(solution)/shard_map/ppermute | solution.py:292
  253.1 24.2 %collective-permute-start.36 = (bf16[1024,512]{1,0:T(8,128)(2,1)}, bf16[1024,512]{1,0:T(8,128)(2,1)}, u32[]{:S(2)}, u32[]{:S(2)}) collective-permute-start(bf16[1024,512]{1,0:T(8,128)(2,1)} %pad_maximum_fusion.3), channel_id=1, source_target_pairs={{0,16},{8,24},{16,0},{24,8},{1,17},{9,25},{17,1},{25,9},{2,18},{10... | collective-permute-start | bytes 3145736 | tf_op jit(solution)/shard_map/ppermute | solution.py:292
  280.2 29.2 %all-to-all-start.6 = ((bf16[4,256,512]{2,1,0:T(8,128)(2,1)}), bf16[4,256,512]{2,1,0:T(8,128)(2,1)S(1)}, u32[]{:S(2)}, u32[]{:S(2)}) async-start(bf16[4,256,512]{2,1,0:T(8,128)(2,1)} %bitcast.16), calls=%async_computation.6 | async-start | bytes 2097152 | tf_op jit(solution)/shard_map/all_to_all | solution.py:313
  313.5 42.4 %all-to-all-start.7 = ((bf16[4,256,512]{2,1,0:T(8,128)(2,1)}), bf16[4,256,512]{2,1,0:T(8,128)(2,1)S(1)}, u32[]{:S(2)}, u32[]{:S(2)}) async-start(bf16[4,256,512]{2,1,0:T(8,128)(2,1)} %broadcast_in_dim.36), calls=%async_computation.7 | async-start | bytes 2097152 | tf_op jit(solution)/shard_map/all_to_all | solution.py:313
  359.8 40.3 %collective-permute-start.63 = (bf16[1024,512]{1,0:T(8,128)(2,1)}, bf16[1024,512]{1,0:T(8,128)(2,1)}, u32[]{:S(2)}, u32[]{:S(2)}) collective-permute-start(bf16[1024,512]{1,0:T(8,128)(2,1)} %pad_maximum_fusion.5), channel_id=1, source_target_pairs={{0,4},{4,0},{1,5},{5,1},{2,6},{6,2},{3,7},{7,3},{8,12},{12,8},{9,1... | collective-permute-start | bytes 3145736 | tf_op jit(solution)/shard_map/ppermute | solution.py:292
  366.4 26.0 %collective-permute-start.53 = (bf16[256,512]{1,0:T(8,128)(2,1)}, bf16[256,512]{1,0:T(8,128)(2,1)}, u32[]{:S(2)}, u32[]{:S(2)}) collective-permute-start(bf16[256,512]{1,0:T(8,128)(2,1)} %slice.512), channel_id=1, source_target_pairs={{0,0},{1,8},{2,16},{3,24},{8,1},{9,9},{10,17},{11,25},{16,2},{17,1... | collective-permute-start | bytes 786440 | tf_op jit(solution)/shard_map/ppermute | solution.py:292
  386.6 30.0 %all-to-all-start.8 = ((bf16[4,256,512]{2,1,0:T(8,128)(2,1)}), bf16[4,256,512]{2,1,0:T(8,128)(2,1)S(1)}, u32[]{:S(2)}, u32[]{:S(2)}) async-start(bf16[4,256,512]{2,1,0:T(8,128)(2,1)} %broadcast_in_dim.37), calls=%async_computation.8 | async-start | bytes 2097152 | tf_op jit(solution)/shard_map/all_to_all | solution.py:313
  423.9 35.6 %collective-permute-start.64 = (bf16[5120,128]{1,0:T(8,128)(2,1)S(1)}, bf16[5120,128]{1,0:T(8,128)(2,1)S(1)}, u32[]{:S(2)}, u32[]{:S(2)}) collective-permute-start(bf16[5120,128]{1,0:T(8,128)(2,1)S(1)} %get-tuple-element.166), channel_id=1, source_target_pairs={{0,4},{4,0},{1,5},{5,1},{2,6},{6,2},{3,7},{7,3},{8,12},{12,8},{9,1... | collective-permute-start | bytes 3932168 | tf_op jit(solution)/shard_map/ppermute | solution.py:292
  429.2 24.3 %collective-permute-start.57 = (bf16[512,512]{1,0:T(8,128)(2,1)S(1)}, bf16[512,512]{1,0:T(8,128)(2,1)S(1)}, u32[]{:S(2)}, u32[]{:S(2)}) collective-permute-start(bf16[512,512]{1,0:T(8,128)(2,1)S(1)} %bitcast.128), channel_id=1, source_target_pairs={{0,8},{9,1},{18,26},{27,19},{4,12},{13,5},{22,30},{31,23}} | collective-permute-start | bytes 1572872 | tf_op jit(solution)/shard_map/ppermute | solution.py:292
  473.7 38.4 %collective-permute-start.61 = (bf16[1024,512]{1,0:T(8,128)(2,1)S(1)}, bf16[1024,512]{1,0:T(8,128)(2,1)S(1)}, u32[]{:S(2)}, u32[]{:S(2)}) collective-permute-start(bf16[1024,512]{1,0:T(8,128)(2,1)S(1)} %pad_maximum_fusion.4), channel_id=1, source_target_pairs={{0,4},{4,0},{1,5},{5,1},{2,6},{6,2},{3,7},{7,3},{8,12},{12,8},{9,1... | collective-permute-start | bytes 3145736 | tf_op jit(solution)/shard_map/ppermute | solution.py:292
  (173 other events, 1814.6 us)
Sparse Core Ops, SparseCore 0:
  96.7 89.1 all-gather.2
